TPU v7x, 512 devices: a whole 4x4x16 slice. The times are simulated.
512 devices in a mesh: head: 16 (over z_hi, x, core), seq: 32 (over y, z_lo).
Axes of the slice: x: 4, y: 4, z: 16 (z_hi: 2, z_lo: 8; z = z_hi * 8 + z_lo), core: 2. Of those that a mesh axis runs over, the one named last changes fastest.
Arguments:
- queries: bfloat16 [1536, 8192], P('seq', 'head'), may hold values from -2.5 to 2.5
- keys: bfloat16 [1024, 20480], P('head', 'seq'), may hold values from -2.5 to 2.5
- values: bfloat16 [1024, 20480], P('head', 'seq'), may hold values from -6 to 6
- outputs: bfloat16 [1536, 8192], P('seq', 'head'), may hold values from -6 to 6
- out_grad: bfloat16 [1536, 8192], P('seq', 'head'), may hold values from -192 to 192
- logsumexp: float32 [1536, 64], P('seq', 'head'), may hold values from 8.5 to 9.5
Outputs:
- query_grad: bfloat16 [1536, 8192], P('seq', 'head')
- key_grad: bfloat16 [1024, 20480], P('head', 'seq')
- value_grad: bfloat16 [1024, 20480], P('head', 'seq')
All inputs are finite; a program needn't handle non-finite values.
Results may differ from a plain program's by a relative error of at most 0.005.
Values may be sent and summed in bfloat16 or wider, within the bound.
No kernel may reach another device: no remote copies, remote signals or barrier semaphores. Data moves between devices by JAX's collectives and lax.ppermute only.
A program may use at most 64 MiB of HBM per device.

v0:
```python
import jax
import jax.numpy as jnp
from jax import lax
from jax.sharding import PartitionSpec as P

DH = 128
HQ_DEV = 4


def partner(shard, axis, distance):
    return lax.ppermute(shard, axis, [(i, i ^ 1 << distance) for i in range(lax.axis_size(axis))])


def shifted(value, axis, steps):
    count = lax.axis_size(axis)
    pairs = [(source, (source + steps) % count) for source in range(count)]
    return lax.ppermute(value, axis, pairs)


def block_grads(q_blk, g_blk, lse_blk, dterm_blk, key_all, value_all):
    softmax_scale = DH ** (-0.5)
    row_count = q_blk.shape[0] * HQ_DEV
    q_rows = q_blk.reshape(row_count, DH)
    g_rows = g_blk.reshape(row_count, DH)
    scores = (
        jnp.einsum("rd,dv->rv", q_rows, key_all, preferred_element_type=jnp.float32) * softmax_scale
    )
    probs = jnp.exp(scores - lse_blk.reshape(row_count, 1))
    dprobs = jnp.einsum("rd,dv->rv", g_rows, value_all, preferred_element_type=jnp.float32)
    dscores = (probs * (dprobs - dterm_blk.reshape(row_count, 1))).astype(jnp.bfloat16)
    probs_low = probs.astype(jnp.bfloat16)
    dv_term = jnp.einsum("rd,rv->dv", g_rows, probs_low, preferred_element_type=jnp.float32)
    dk_term = (
        jnp.einsum("rd,rv->dv", q_rows, dscores, preferred_element_type=jnp.float32) * softmax_scale
    )
    dq_term = (
        jnp.einsum("rv,dv->rd", dscores, key_all, preferred_element_type=jnp.float32)
        * softmax_scale
    )
    return (dq_term.reshape(q_blk.shape), dk_term, dv_term)


def per_device(queries, keys, values, outputs, out_grad, logsumexp):
    parity = lax.axis_index("head") % 2
    half_width = keys.shape[0]
    other_k, other_v = partner((keys, values), "head", 0)
    key_all = jnp.where(
        parity == 0, jnp.concatenate([keys, other_k], 0), jnp.concatenate([other_k, keys], 0)
    )
    value_all = jnp.where(
        parity == 0, jnp.concatenate([values, other_v], 0), jnp.concatenate([other_v, values], 0)
    )
    txt_rows = queries.shape[0]
    dterm = jnp.sum(
        (out_grad.astype(jnp.float32) * outputs.astype(jnp.float32)).reshape(txt_rows, HQ_DEV, DH),
        axis=2,
    )
    cycle_size = lax.axis_size("seq")
    dq_own, dk_start, dv_start = block_grads(
        queries, out_grad, logsumexp, dterm, key_all, value_all
    )

    def visit_turn(turn_index, state_tuple):
        q_blk, g_blk, lse_blk, d_blk, dq_acc, dk_acc, dv_acc = state_tuple
        q_blk, g_blk = shifted((q_blk, g_blk), "seq", 1)
        lse_blk, d_blk, dq_acc = shifted((lse_blk, d_blk, dq_acc), "seq", 1)
        dq_term, dk_term, dv_term = block_grads(q_blk, g_blk, lse_blk, d_blk, key_all, value_all)
        return (q_blk, g_blk, lse_blk, d_blk, dq_acc + dq_term, dk_acc + dk_term, dv_acc + dv_term)

    start_state = (queries, out_grad, logsumexp, dterm, dq_own, dk_start, dv_start)
    final_state = lax.fori_loop(0, cycle_size - 1, visit_turn, start_state)
    dk_acc = final_state[5]
    dv_acc = final_state[6]
    dq_total = shifted(final_state[4].astype(jnp.bfloat16), "seq", 1).astype(jnp.float32)
    send_k = lax.dynamic_slice_in_dim(dk_acc, (1 - parity) * half_width, half_width, 0)
    send_v = lax.dynamic_slice_in_dim(dv_acc, (1 - parity) * half_width, half_width, 0)
    keep_k = lax.dynamic_slice_in_dim(dk_acc, parity * half_width, half_width, 0)
    keep_v = lax.dynamic_slice_in_dim(dv_acc, parity * half_width, half_width, 0)
    got_k, got_v = partner((send_k, send_v), "head", 0)
    key_grad = (keep_k + got_k).astype(jnp.bfloat16)
    value_grad = (keep_v + got_v).astype(jnp.bfloat16)
    return (dq_total.astype(jnp.bfloat16), key_grad, value_grad)


def solution(mesh):
    in_specs = (
        P("seq", "head"),
        P("head", "seq"),
        P("head", "seq"),
        P("seq", "head"),
        P("seq", "head"),
        P("seq", "head"),
    )
    out_specs = (P("seq", "head"), P("head", "seq"), P("head", "seq"))
    return jax.shard_map(
        per_device, mesh=mesh, in_specs=in_specs, out_specs=out_specs, check_vma=False
    )
```

profile of v0, /device:TPU:6, one launch (start us, length us, event | category | flops | bytes accessed | tf_op | source)
XLA Modules:
  0.0 813.0 jit_solution(8930937344024835121)
XLA Ops:
  10.1 783.9 %while.22 = (s32[]{:T(128)}, bf16[48,512]{1,0:T(8,128)(2,1)S(1)}, bf16[48,512]{1,0:T(8,128)(2,1)S(1)}, f32[48,4]{1,0:T(8,128)S(1)}, f32[48,4]{1,0:T(8,128)S(1)},...) while((s32[]{:T(128)}, bf16[48,512]{1,0:T(8,128)(2,1)S(1)}, ...), condition=%wide.region_2.3_spmd, body=%wide.region_1.2_spmd.sunk | while | flops 158318592 | bytes 5994293 | solution.py:71
  10.1 3.8 collective-permute-start
  13.9 3.8 collective-permute-start.2
  17.8 3.8 collective-permute-start.3
  21.6 5.0 collective-permute-start.1
  26.6 3.8 collective-permute-start.4
  32.6 3.7 collective-permute-done.1
  37.5 4.4 collective-permute-done.4
  51.5 6.7 collective-permute-done.2
  71.3 5.5 collective-permute-start.1
  87.2 4.9 collective-permute-done.4
  101.7 6.7 collective-permute-done.2
  121.4 5.5 collective-permute-start.1
  137.3 4.9 collective-permute-done.4
  151.9 6.7 collective-permute-done.2
  171.3 5.5 collective-permute-start.1
  187.2 5.1 collective-permute-done.4
  202.0 6.7 collective-permute-done.2
  221.3 5.5 collective-permute-start.1
  237.5 5.1 collective-permute-done.4
  252.3 6.7 collective-permute-done.2
  271.9 5.6 collective-permute-start.1
  287.7 5.0 collective-permute-done.4
  302.4 6.7 collective-permute-done.2
  322.0 5.5 collective-permute-start.1
  337.9 4.9 collective-permute-done.4
  352.9 6.5 collective-permute-done.2
  372.3 5.5 collective-permute-start.1
  388.1 4.9 collective-permute-done.4
  402.9 6.5 collective-permute-done.2
  420.1 3.6 collective-permute-start.3
  423.8 5.6 collective-permute-start.1
  435.0 3.5 collective-permute-done.1
  439.7 5.0 collective-permute-done.4
  454.4 6.7 collective-permute-done.2
  473.7 4.7 collective-permute-start.1
  480.4 3.9 collective-permute-done.2
  490.0 3.8 collective-permute-done.4
  503.5 7.0 collective-permute-done.2
  523.0 4.7 collective-permute-start.1
  529.7 3.9 collective-permute-done.2
  539.1 4.0 collective-permute-done.4
  554.0 5.6 collective-permute-done.2
  573.1 5.3 collective-permute-start.1
  580.4 3.3 collective-permute-done.2
  589.4 4.3 collective-permute-done.4
  604.3 5.8 collective-permute-done.2
  621.4 3.6 collective-permute-start.3
  625.1 5.6 collective-permute-start.1
  636.3 3.5 collective-permute-done.1
  641.0 4.9 collective-permute-done.4
  656.1 6.2 collective-permute-done.2
  675.2 4.6 collective-permute-start.1
  681.8 4.1 collective-permute-done.2
  691.1 4.4 collective-permute-done.4
  705.2 6.7 collective-permute-done.2
  724.6 3.5 collective-permute-start.1
  730.0 5.1 collective-permute-done.2
  749.1 3.9 collective-permute-start.1
  754.9 4.8 collective-permute-done.2
  774.0 4.7 collective-permute-start.1
  780.6 4.0 collective-permute-done.2
  789.9 4.0 collective-permute-done.4
  800.7 10.4 %collective-permute-done.7 = bf16[48,512]{1,0:T(8,128)(2,1)S(1)} collective-permute-done((bf16[48,512]{1,0:T(8,128)(2,1)S(1)}, bf16[48,512]{1,0:T(8,128)(2,1)S(1)}, u32[]{:S(2)}, u32[]{:S(2)}) %collective-permute-start.7) | collective-permute-done | bytes 49184 | tf_op jit(solution)/shard_map/ppermute | solution.py:17
  (754 shorter events, 487.1 us)
Async XLA Ops:
  10.1 22.2 %collective-permute-start = (bf16[48,512]{1,0:T(8,128)(2,1)S(1)}, bf16[48,512]{1,0:T(8,128)(2,1)S(1)}, u32[]{:S(2)}, u32[]{:S(2)}) collective-permute-start(bf16[48,512]{1,0:T(8,128)(2,1)S(1)} %get-tuple-element.163), channel_id=1, source_target_pairs={{0,1},{1,2},{2,3},{3,4},{4,5},{5,6},{6,7},{7,8},{8,9},{9,10},{10,1... | collective-permute-start | bytes 147464 | tf_op jit(solution)/shard_map/while/body/eval_jaxpr/ppermute | solution.py:17
  13.9 16.6 %collective-permute-start.2 = (f32[48,4]{1,0:T(8,128)S(1)}, f32[48,4]{1,0:T(8,128)S(1)}, u32[]{:S(2)}, u32[]{:S(2)}) collective-permute-start(f32[48,4]{1,0:T(8,128)S(1)} %get-tuple-element.165), channel_id=1, source_target_pairs={{0,1},{1,2},{2,3},{3,4},{4,5},{5,6},{6,7},{7,8},{8,9},{9,10},{10,1... | collective-permute-start | bytes 2312 | tf_op jit(solution)/shard_map/while/body/eval_jaxpr/ppermute | solution.py:17
  26.6 15.2 %collective-permute-start.4 = (f32[48,512]{1,0:T(8,128)S(1)}, f32[48,512]{1,0:T(8,128)S(1)}, u32[]{:S(2)}, u32[]{:S(2)}) collective-permute-start(f32[48,512]{1,0:T(8,128)S(1)} %get-tuple-element.167), channel_id=1, source_target_pairs={{0,1},{1,2},{2,3},{3,4},{4,5},{5,6},{6,7},{7,8},{8,9},{9,10},{10,1... | collective-permute-start | bytes 294920 | tf_op jit(solution)/shard_map/while/body/eval_jaxpr/ppermute | solution.py:17
  41.9 18.4 %collective-permute-start = (bf16[48,512]{1,0:T(8,128)(2,1)S(1)}, bf16[48,512]{1,0:T(8,128)(2,1)S(1)}, u32[]{:S(2)}, u32[]{:S(2)}) collective-permute-start(bf16[48,512]{1,0:T(8,128)(2,1)S(1)} %get-tuple-element.163), channel_id=1, source_target_pairs={{0,1},{1,2},{2,3},{3,4},{4,5},{5,6},{6,7},{7,8},{8,9},{9,10},{10,1... | collective-permute-start | bytes 147464 | tf_op jit(solution)/shard_map/while/body/eval_jaxpr/ppermute | solution.py:17
  49.6 15.2 %collective-permute-start.4 = (f32[48,512]{1,0:T(8,128)S(1)}, f32[48,512]{1,0:T(8,128)S(1)}, u32[]{:S(2)}, u32[]{:S(2)}) collective-permute-start(f32[48,512]{1,0:T(8,128)S(1)} %get-tuple-element.167), channel_id=1, source_target_pairs={{0,1},{1,2},{2,3},{3,4},{4,5},{5,6},{6,7},{7,8},{8,9},{9,10},{10,1... | collective-permute-start | bytes 294920 | tf_op jit(solution)/shard_map/while/body/eval_jaxpr/ppermute | solution.py:17
  64.9 18.4 %collective-permute-start = (bf16[48,512]{1,0:T(8,128)(2,1)S(1)}, bf16[48,512]{1,0:T(8,128)(2,1)S(1)}, u32[]{:S(2)}, u32[]{:S(2)}) collective-permute-start(bf16[48,512]{1,0:T(8,128)(2,1)S(1)} %get-tuple-element.163), channel_id=1, source_target_pairs={{0,1},{1,2},{2,3},{3,4},{4,5},{5,6},{6,7},{7,8},{8,9},{9,10},{10,1... | collective-permute-start | bytes 147464 | tf_op jit(solution)/shard_map/while/body/eval_jaxpr/ppermute | solution.py:17
  76.8 15.2 %collective-permute-start.4 = (f32[48,512]{1,0:T(8,128)S(1)}, f32[48,512]{1,0:T(8,128)S(1)}, u32[]{:S(2)}, u32[]{:S(2)}) collective-permute-start(f32[48,512]{1,0:T(8,128)S(1)} %get-tuple-element.167), channel_id=1, source_target_pairs={{0,1},{1,2},{2,3},{3,4},{4,5},{5,6},{6,7},{7,8},{8,9},{9,10},{10,1... | collective-permute-start | bytes 294920 | tf_op jit(solution)/shard_map/while/body/eval_jaxpr/ppermute | solution.py:17
  92.1 18.4 %collective-permute-start = (bf16[48,512]{1,0:T(8,128)(2,1)S(1)}, bf16[48,512]{1,0:T(8,128)(2,1)S(1)}, u32[]{:S(2)}, u32[]{:S(2)}) collective-permute-start(bf16[48,512]{1,0:T(8,128)(2,1)S(1)} %get-tuple-element.163), channel_id=1, source_target_pairs={{0,1},{1,2},{2,3},{3,4},{4,5},{5,6},{6,7},{7,8},{8,9},{9,10},{10,1... | collective-permute-start | bytes 147464 | tf_op jit(solution)/shard_map/while/body/eval_jaxpr/ppermute | solution.py:17
  99.8 15.2 %collective-permute-start.4 = (f32[48,512]{1,0:T(8,128)S(1)}, f32[48,512]{1,0:T(8,128)S(1)}, u32[]{:S(2)}, u32[]{:S(2)}) collective-permute-start(f32[48,512]{1,0:T(8,128)S(1)} %get-tuple-element.167), channel_id=1, source_target_pairs={{0,1},{1,2},{2,3},{3,4},{4,5},{5,6},{6,7},{7,8},{8,9},{9,10},{10,1... | collective-permute-start | bytes 294920 | tf_op jit(solution)/shard_map/while/body/eval_jaxpr/ppermute | solution.py:17
  115.0 18.4 %collective-permute-start = (bf16[48,512]{1,0:T(8,128)(2,1)S(1)}, bf16[48,512]{1,0:T(8,128)(2,1)S(1)}, u32[]{:S(2)}, u32[]{:S(2)}) collective-permute-start(bf16[48,512]{1,0:T(8,128)(2,1)S(1)} %get-tuple-element.163), channel_id=1, source_target_pairs={{0,1},{1,2},{2,3},{3,4},{4,5},{5,6},{6,7},{7,8},{8,9},{9,10},{10,1... | collective-permute-start | bytes 147464 | tf_op jit(solution)/shard_map/while/body/eval_jaxpr/ppermute | solution.py:17
  127.0 15.2 %collective-permute-start.4 = (f32[48,512]{1,0:T(8,128)S(1)}, f32[48,512]{1,0:T(8,128)S(1)}, u32[]{:S(2)}, u32[]{:S(2)}) collective-permute-start(f32[48,512]{1,0:T(8,128)S(1)} %get-tuple-element.167), channel_id=1, source_target_pairs={{0,1},{1,2},{2,3},{3,4},{4,5},{5,6},{6,7},{7,8},{8,9},{9,10},{10,1... | collective-permute-start | bytes 294920 | tf_op jit(solution)/shard_map/while/body/eval_jaxpr/ppermute | solution.py:17
  142.2 18.4 %collective-permute-start = (bf16[48,512]{1,0:T(8,128)(2,1)S(1)}, bf16[48,512]{1,0:T(8,128)(2,1)S(1)}, u32[]{:S(2)}, u32[]{:S(2)}) collective-permute-start(bf16[48,512]{1,0:T(8,128)(2,1)S(1)} %get-tuple-element.163), channel_id=1, source_target_pairs={{0,1},{1,2},{2,3},{3,4},{4,5},{5,6},{6,7},{7,8},{8,9},{9,10},{10,1... | collective-permute-start | bytes 147464 | tf_op jit(solution)/shard_map/while/body/eval_jaxpr/ppermute | solution.py:17
  149.9 15.2 %collective-permute-start.4 = (f32[48,512]{1,0:T(8,128)S(1)}, f32[48,512]{1,0:T(8,128)S(1)}, u32[]{:S(2)}, u32[]{:S(2)}) collective-permute-start(f32[48,512]{1,0:T(8,128)S(1)} %get-tuple-element.167), channel_id=1, source_target_pairs={{0,1},{1,2},{2,3},{3,4},{4,5},{5,6},{6,7},{7,8},{8,9},{9,10},{10,1... | collective-permute-start | bytes 294920 | tf_op jit(solution)/shard_map/while/body/eval_jaxpr/ppermute | solution.py:17
  165.2 18.4 %collective-permute-start = (bf16[48,512]{1,0:T(8,128)(2,1)S(1)}, bf16[48,512]{1,0:T(8,128)(2,1)S(1)}, u32[]{:S(2)}, u32[]{:S(2)}) collective-permute-start(bf16[48,512]{1,0:T(8,128)(2,1)S(1)} %get-tuple-element.163), channel_id=1, source_target_pairs={{0,1},{1,2},{2,3},{3,4},{4,5},{5,6},{6,7},{7,8},{8,9},{9,10},{10,1... | collective-permute-start | bytes 147464 | tf_op jit(solution)/shard_map/while/body/eval_jaxpr/ppermute | solution.py:17
  176.8 15.5 %collective-permute-start.4 = (f32[48,512]{1,0:T(8,128)S(1)}, f32[48,512]{1,0:T(8,128)S(1)}, u32[]{:S(2)}, u32[]{:S(2)}) collective-permute-start(f32[48,512]{1,0:T(8,128)S(1)} %get-tuple-element.167), channel_id=1, source_target_pairs={{0,1},{1,2},{2,3},{3,4},{4,5},{5,6},{6,7},{7,8},{8,9},{9,10},{10,1... | collective-permute-start | bytes 294920 | tf_op jit(solution)/shard_map/while/body/eval_jaxpr/ppermute | solution.py:17
  192.3 18.4 %collective-permute-start = (bf16[48,512]{1,0:T(8,128)(2,1)S(1)}, bf16[48,512]{1,0:T(8,128)(2,1)S(1)}, u32[]{:S(2)}, u32[]{:S(2)}) collective-permute-start(bf16[48,512]{1,0:T(8,128)(2,1)S(1)} %get-tuple-element.163), channel_id=1, source_target_pairs={{0,1},{1,2},{2,3},{3,4},{4,5},{5,6},{6,7},{7,8},{8,9},{9,10},{10,1... | collective-permute-start | bytes 147464 | tf_op jit(solution)/shard_map/while/body/eval_jaxpr/ppermute | solution.py:17
  200.1 15.2 %collective-permute-start.4 = (f32[48,512]{1,0:T(8,128)S(1)}, f32[48,512]{1,0:T(8,128)S(1)}, u32[]{:S(2)}, u32[]{:S(2)}) collective-permute-start(f32[48,512]{1,0:T(8,128)S(1)} %get-tuple-element.167), channel_id=1, source_target_pairs={{0,1},{1,2},{2,3},{3,4},{4,5},{5,6},{6,7},{7,8},{8,9},{9,10},{10,1... | collective-permute-start | bytes 294920 | tf_op jit(solution)/shard_map/while/body/eval_jaxpr/ppermute | solution.py:17
  215.3 18.4 %collective-permute-start = (bf16[48,512]{1,0:T(8,128)(2,1)S(1)}, bf16[48,512]{1,0:T(8,128)(2,1)S(1)}, u32[]{:S(2)}, u32[]{:S(2)}) collective-permute-start(bf16[48,512]{1,0:T(8,128)(2,1)S(1)} %get-tuple-element.163), channel_id=1, source_target_pairs={{0,1},{1,2},{2,3},{3,4},{4,5},{5,6},{6,7},{7,8},{8,9},{9,10},{10,1... | collective-permute-start | bytes 147464 | tf_op jit(solution)/shard_map/while/body/eval_jaxpr/ppermute | solution.py:17
  226.9 15.8 %collective-permute-start.4 = (f32[48,512]{1,0:T(8,128)S(1)}, f32[48,512]{1,0:T(8,128)S(1)}, u32[]{:S(2)}, u32[]{:S(2)}) collective-permute-start(f32[48,512]{1,0:T(8,128)S(1)} %get-tuple-element.167), channel_id=1, source_target_pairs={{0,1},{1,2},{2,3},{3,4},{4,5},{5,6},{6,7},{7,8},{8,9},{9,10},{10,1... | collective-permute-start | bytes 294920 | tf_op jit(solution)/shard_map/while/body/eval_jaxpr/ppermute | solution.py:17
  242.7 18.4 %collective-permute-start = (bf16[48,512]{1,0:T(8,128)(2,1)S(1)}, bf16[48,512]{1,0:T(8,128)(2,1)S(1)}, u32[]{:S(2)}, u32[]{:S(2)}) collective-permute-start(bf16[48,512]{1,0:T(8,128)(2,1)S(1)} %get-tuple-element.163), channel_id=1, source_target_pairs={{0,1},{1,2},{2,3},{3,4},{4,5},{5,6},{6,7},{7,8},{8,9},{9,10},{10,1... | collective-permute-start | bytes 147464 | tf_op jit(solution)/shard_map/while/body/eval_jaxpr/ppermute | solution.py:17
  250.4 15.2 %collective-permute-start.4 = (f32[48,512]{1,0:T(8,128)S(1)}, f32[48,512]{1,0:T(8,128)S(1)}, u32[]{:S(2)}, u32[]{:S(2)}) collective-permute-start(f32[48,512]{1,0:T(8,128)S(1)} %get-tuple-element.167), channel_id=1, source_target_pairs={{0,1},{1,2},{2,3},{3,4},{4,5},{5,6},{6,7},{7,8},{8,9},{9,10},{10,1... | collective-permute-start | bytes 294920 | tf_op jit(solution)/shard_map/while/body/eval_jaxpr/ppermute | solution.py:17
  265.6 18.4 %collective-permute-start = (bf16[48,512]{1,0:T(8,128)(2,1)S(1)}, bf16[48,512]{1,0:T(8,128)(2,1)S(1)}, u32[]{:S(2)}, u32[]{:S(2)}) collective-permute-start(bf16[48,512]{1,0:T(8,128)(2,1)S(1)} %get-tuple-element.163), channel_id=1, source_target_pairs={{0,1},{1,2},{2,3},{3,4},{4,5},{5,6},{6,7},{7,8},{8,9},{9,10},{10,1... | collective-permute-start | bytes 147464 | tf_op jit(solution)/shard_map/while/body/eval_jaxpr/ppermute | solution.py:17
  277.5 15.2 %collective-permute-start.4 = (f32[48,512]{1,0:T(8,128)S(1)}, f32[48,512]{1,0:T(8,128)S(1)}, u32[]{:S(2)}, u32[]{:S(2)}) collective-permute-start(f32[48,512]{1,0:T(8,128)S(1)} %get-tuple-element.167), channel_id=1, source_target_pairs={{0,1},{1,2},{2,3},{3,4},{4,5},{5,6},{6,7},{7,8},{8,9},{9,10},{10,1... | collective-permute-start | bytes 294920 | tf_op jit(solution)/shard_map/while/body/eval_jaxpr/ppermute | solution.py:17
  292.7 18.4 %collective-permute-start = (bf16[48,512]{1,0:T(8,128)(2,1)S(1)}, bf16[48,512]{1,0:T(8,128)(2,1)S(1)}, u32[]{:S(2)}, u32[]{:S(2)}) collective-permute-start(bf16[48,512]{1,0:T(8,128)(2,1)S(1)} %get-tuple-element.163), channel_id=1, source_target_pairs={{0,1},{1,2},{2,3},{3,4},{4,5},{5,6},{6,7},{7,8},{8,9},{9,10},{10,1... | collective-permute-start | bytes 147464 | tf_op jit(solution)/shard_map/while/body/eval_jaxpr/ppermute | solution.py:17
  300.4 15.2 %collective-permute-start.4 = (f32[48,512]{1,0:T(8,128)S(1)}, f32[48,512]{1,0:T(8,128)S(1)}, u32[]{:S(2)}, u32[]{:S(2)}) collective-permute-start(f32[48,512]{1,0:T(8,128)S(1)} %get-tuple-element.167), channel_id=1, source_target_pairs={{0,1},{1,2},{2,3},{3,4},{4,5},{5,6},{6,7},{7,8},{8,9},{9,10},{10,1... | collective-permute-start | bytes 294920 | tf_op jit(solution)/shard_map/while/body/eval_jaxpr/ppermute | solution.py:17
  315.7 18.4 %collective-permute-start = (bf16[48,512]{1,0:T(8,128)(2,1)S(1)}, bf16[48,512]{1,0:T(8,128)(2,1)S(1)}, u32[]{:S(2)}, u32[]{:S(2)}) collective-permute-start(bf16[48,512]{1,0:T(8,128)(2,1)S(1)} %get-tuple-element.163), channel_id=1, source_target_pairs={{0,1},{1,2},{2,3},{3,4},{4,5},{5,6},{6,7},{7,8},{8,9},{9,10},{10,1... | collective-permute-start | bytes 147464 | tf_op jit(solution)/shard_map/while/body/eval_jaxpr/ppermute | solution.py:17
  327.5 15.2 %collective-permute-start.4 = (f32[48,512]{1,0:T(8,128)S(1)}, f32[48,512]{1,0:T(8,128)S(1)}, u32[]{:S(2)}, u32[]{:S(2)}) collective-permute-start(f32[48,512]{1,0:T(8,128)S(1)} %get-tuple-element.167), channel_id=1, source_target_pairs={{0,1},{1,2},{2,3},{3,4},{4,5},{5,6},{6,7},{7,8},{8,9},{9,10},{10,1... | collective-permute-start | bytes 294920 | tf_op jit(solution)/shard_map/while/body/eval_jaxpr/ppermute | solution.py:17
  342.8 18.4 %collective-permute-start = (bf16[48,512]{1,0:T(8,128)(2,1)S(1)}, bf16[48,512]{1,0:T(8,128)(2,1)S(1)}, u32[]{:S(2)}, u32[]{:S(2)}) collective-permute-start(bf16[48,512]{1,0:T(8,128)(2,1)S(1)} %get-tuple-element.163), channel_id=1, source_target_pairs={{0,1},{1,2},{2,3},{3,4},{4,5},{5,6},{6,7},{7,8},{8,9},{9,10},{10,1... | collective-permute-start | bytes 147464 | tf_op jit(solution)/shard_map/while/body/eval_jaxpr/ppermute | solution.py:17
  351.0 15.2 %collective-permute-start.4 = (f32[48,512]{1,0:T(8,128)S(1)}, f32[48,512]{1,0:T(8,128)S(1)}, u32[]{:S(2)}, u32[]{:S(2)}) collective-permute-start(f32[48,512]{1,0:T(8,128)S(1)} %get-tuple-element.167), channel_id=1, source_target_pairs={{0,1},{1,2},{2,3},{3,4},{4,5},{5,6},{6,7},{7,8},{8,9},{9,10},{10,1... | collective-permute-start | bytes 294920 | tf_op jit(solution)/shard_map/while/body/eval_jaxpr/ppermute | solution.py:17
  366.3 18.4 %collective-permute-start = (bf16[48,512]{1,0:T(8,128)(2,1)S(1)}, bf16[48,512]{1,0:T(8,128)(2,1)S(1)}, u32[]{:S(2)}, u32[]{:S(2)}) collective-permute-start(bf16[48,512]{1,0:T(8,128)(2,1)S(1)} %get-tuple-element.163), channel_id=1, source_target_pairs={{0,1},{1,2},{2,3},{3,4},{4,5},{5,6},{6,7},{7,8},{8,9},{9,10},{10,1... | collective-permute-start | bytes 147464 | tf_op jit(solution)/shard_map/while/body/eval_jaxpr/ppermute | solution.py:17
  377.8 15.2 %collective-permute-start.4 = (f32[48,512]{1,0:T(8,128)S(1)}, f32[48,512]{1,0:T(8,128)S(1)}, u32[]{:S(2)}, u32[]{:S(2)}) collective-permute-start(f32[48,512]{1,0:T(8,128)S(1)} %get-tuple-element.167), channel_id=1, source_target_pairs={{0,1},{1,2},{2,3},{3,4},{4,5},{5,6},{6,7},{7,8},{8,9},{9,10},{10,1... | collective-permute-start | bytes 294920 | tf_op jit(solution)/shard_map/while/body/eval_jaxpr/ppermute | solution.py:17
  393.1 18.4 %collective-permute-start = (bf16[48,512]{1,0:T(8,128)(2,1)S(1)}, bf16[48,512]{1,0:T(8,128)(2,1)S(1)}, u32[]{:S(2)}, u32[]{:S(2)}) collective-permute-start(bf16[48,512]{1,0:T(8,128)(2,1)S(1)} %get-tuple-element.163), channel_id=1, source_target_pairs={{0,1},{1,2},{2,3},{3,4},{4,5},{5,6},{6,7},{7,8},{8,9},{9,10},{10,1... | collective-permute-start | bytes 147464 | tf_op jit(solution)/shard_map/while/body/eval_jaxpr/ppermute | solution.py:17
  401.0 15.2 %collective-permute-start.4 = (f32[48,512]{1,0:T(8,128)S(1)}, f32[48,512]{1,0:T(8,128)S(1)}, u32[]{:S(2)}, u32[]{:S(2)}) collective-permute-start(f32[48,512]{1,0:T(8,128)S(1)} %get-tuple-element.167), channel_id=1, source_target_pairs={{0,1},{1,2},{2,3},{3,4},{4,5},{5,6},{6,7},{7,8},{8,9},{9,10},{10,1... | collective-permute-start | bytes 294920 | tf_op jit(solution)/shard_map/while/body/eval_jaxpr/ppermute | solution.py:17
  416.3 18.4 %collective-permute-start = (bf16[48,512]{1,0:T(8,128)(2,1)S(1)}, bf16[48,512]{1,0:T(8,128)(2,1)S(1)}, u32[]{:S(2)}, u32[]{:S(2)}) collective-permute-start(bf16[48,512]{1,0:T(8,128)(2,1)S(1)} %get-tuple-element.163), channel_id=1, source_target_pairs={{0,1},{1,2},{2,3},{3,4},{4,5},{5,6},{6,7},{7,8},{8,9},{9,10},{10,1... | collective-permute-start | bytes 147464 | tf_op jit(solution)/shard_map/while/body/eval_jaxpr/ppermute | solution.py:17
  429.4 15.3 %collective-permute-start.4 = (f32[48,512]{1,0:T(8,128)S(1)}, f32[48,512]{1,0:T(8,128)S(1)}, u32[]{:S(2)}, u32[]{:S(2)}) collective-permute-start(f32[48,512]{1,0:T(8,128)S(1)} %get-tuple-element.167), channel_id=1, source_target_pairs={{0,1},{1,2},{2,3},{3,4},{4,5},{5,6},{6,7},{7,8},{8,9},{9,10},{10,1... | collective-permute-start | bytes 294920 | tf_op jit(solution)/shard_map/while/body/eval_jaxpr/ppermute | solution.py:17
  444.7 18.4 %collective-permute-start = (bf16[48,512]{1,0:T(8,128)(2,1)S(1)}, bf16[48,512]{1,0:T(8,128)(2,1)S(1)}, u32[]{:S(2)}, u32[]{:S(2)}) collective-permute-start(bf16[48,512]{1,0:T(8,128)(2,1)S(1)} %get-tuple-element.163), channel_id=1, source_target_pairs={{0,1},{1,2},{2,3},{3,4},{4,5},{5,6},{6,7},{7,8},{8,9},{9,10},{10,1... | collective-permute-start | bytes 147464 | tf_op jit(solution)/shard_map/while/body/eval_jaxpr/ppermute | solution.py:17
  452.4 15.5 %collective-permute-start.4 = (f32[48,512]{1,0:T(8,128)S(1)}, f32[48,512]{1,0:T(8,128)S(1)}, u32[]{:S(2)}, u32[]{:S(2)}) collective-permute-start(f32[48,512]{1,0:T(8,128)S(1)} %get-tuple-element.167), channel_id=1, source_target_pairs={{0,1},{1,2},{2,3},{3,4},{4,5},{5,6},{6,7},{7,8},{8,9},{9,10},{10,1... | collective-permute-start | bytes 294920 | tf_op jit(solution)/shard_map/while/body/eval_jaxpr/ppermute | solution.py:17
  467.9 18.4 %collective-permute-start = (bf16[48,512]{1,0:T(8,128)(2,1)S(1)}, bf16[48,512]{1,0:T(8,128)(2,1)S(1)}, u32[]{:S(2)}, u32[]{:S(2)}) collective-permute-start(bf16[48,512]{1,0:T(8,128)(2,1)S(1)} %get-tuple-element.163), channel_id=1, source_target_pairs={{0,1},{1,2},{2,3},{3,4},{4,5},{5,6},{6,7},{7,8},{8,9},{9,10},{10,1... | collective-permute-start | bytes 147464 | tf_op jit(solution)/shard_map/while/body/eval_jaxpr/ppermute | solution.py:17
  478.5 15.4 %collective-permute-start.4 = (f32[48,512]{1,0:T(8,128)S(1)}, f32[48,512]{1,0:T(8,128)S(1)}, u32[]{:S(2)}, u32[]{:S(2)}) collective-permute-start(f32[48,512]{1,0:T(8,128)S(1)} %get-tuple-element.167), channel_id=1, source_target_pairs={{0,1},{1,2},{2,3},{3,4},{4,5},{5,6},{6,7},{7,8},{8,9},{9,10},{10,1... | collective-permute-start | bytes 294920 | tf_op jit(solution)/shard_map/while/body/eval_jaxpr/ppermute | solution.py:17
  493.9 18.5 %collective-permute-start = (bf16[48,512]{1,0:T(8,128)(2,1)S(1)}, bf16[48,512]{1,0:T(8,128)(2,1)S(1)}, u32[]{:S(2)}, u32[]{:S(2)}) collective-permute-start(bf16[48,512]{1,0:T(8,128)(2,1)S(1)} %get-tuple-element.163), channel_id=1, source_target_pairs={{0,1},{1,2},{2,3},{3,4},{4,5},{5,6},{6,7},{7,8},{8,9},{9,10},{10,1... | collective-permute-start | bytes 147464 | tf_op jit(solution)/shard_map/while/body/eval_jaxpr/ppermute | solution.py:17
  501.6 15.6 %collective-permute-start.4 = (f32[48,512]{1,0:T(8,128)S(1)}, f32[48,512]{1,0:T(8,128)S(1)}, u32[]{:S(2)}, u32[]{:S(2)}) collective-permute-start(f32[48,512]{1,0:T(8,128)S(1)} %get-tuple-element.167), channel_id=1, source_target_pairs={{0,1},{1,2},{2,3},{3,4},{4,5},{5,6},{6,7},{7,8},{8,9},{9,10},{10,1... | collective-permute-start | bytes 294920 | tf_op jit(solution)/shard_map/while/body/eval_jaxpr/ppermute | solution.py:17
  517.2 18.4 %collective-permute-start = (bf16[48,512]{1,0:T(8,128)(2,1)S(1)}, bf16[48,512]{1,0:T(8,128)(2,1)S(1)}, u32[]{:S(2)}, u32[]{:S(2)}) collective-permute-start(bf16[48,512]{1,0:T(8,128)(2,1)S(1)} %get-tuple-element.163), channel_id=1, source_target_pairs={{0,1},{1,2},{2,3},{3,4},{4,5},{5,6},{6,7},{7,8},{8,9},{9,10},{10,1... | collective-permute-start | bytes 147464 | tf_op jit(solution)/shard_map/while/body/eval_jaxpr/ppermute | solution.py:17
  527.7 15.4 %collective-permute-start.4 = (f32[48,512]{1,0:T(8,128)S(1)}, f32[48,512]{1,0:T(8,128)S(1)}, u32[]{:S(2)}, u32[]{:S(2)}) collective-permute-start(f32[48,512]{1,0:T(8,128)S(1)} %get-tuple-element.167), channel_id=1, source_target_pairs={{0,1},{1,2},{2,3},{3,4},{4,5},{5,6},{6,7},{7,8},{8,9},{9,10},{10,1... | collective-permute-start | bytes 294920 | tf_op jit(solution)/shard_map/while/body/eval_jaxpr/ppermute | solution.py:17
  543.1 18.5 %collective-permute-start = (bf16[48,512]{1,0:T(8,128)(2,1)S(1)}, bf16[48,512]{1,0:T(8,128)(2,1)S(1)}, u32[]{:S(2)}, u32[]{:S(2)}) collective-permute-start(bf16[48,512]{1,0:T(8,128)(2,1)S(1)} %get-tuple-element.163), channel_id=1, source_target_pairs={{0,1},{1,2},{2,3},{3,4},{4,5},{5,6},{6,7},{7,8},{8,9},{9,10},{10,1... | collective-permute-start | bytes 147464 | tf_op jit(solution)/shard_map/while/body/eval_jaxpr/ppermute | solution.py:17
  552.1 15.2 %collective-permute-start.4 = (f32[48,512]{1,0:T(8,128)S(1)}, f32[48,512]{1,0:T(8,128)S(1)}, u32[]{:S(2)}, u32[]{:S(2)}) collective-permute-start(f32[48,512]{1,0:T(8,128)S(1)} %get-tuple-element.167), channel_id=1, source_target_pairs={{0,1},{1,2},{2,3},{3,4},{4,5},{5,6},{6,7},{7,8},{8,9},{9,10},{10,1... | collective-permute-start | bytes 294920 | tf_op jit(solution)/shard_map/while/body/eval_jaxpr/ppermute | solution.py:17
  567.3 18.4 %collective-permute-start = (bf16[48,512]{1,0:T(8,128)(2,1)S(1)}, bf16[48,512]{1,0:T(8,128)(2,1)S(1)}, u32[]{:S(2)}, u32[]{:S(2)}) collective-permute-start(bf16[48,512]{1,0:T(8,128)(2,1)S(1)} %get-tuple-element.163), channel_id=1, source_target_pairs={{0,1},{1,2},{2,3},{3,4},{4,5},{5,6},{6,7},{7,8},{8,9},{9,10},{10,1... | collective-permute-start | bytes 147464 | tf_op jit(solution)/shard_map/while/body/eval_jaxpr/ppermute | solution.py:17
  578.4 15.2 %collective-permute-start.4 = (f32[48,512]{1,0:T(8,128)S(1)}, f32[48,512]{1,0:T(8,128)S(1)}, u32[]{:S(2)}, u32[]{:S(2)}) collective-permute-start(f32[48,512]{1,0:T(8,128)S(1)} %get-tuple-element.167), channel_id=1, source_target_pairs={{0,1},{1,2},{2,3},{3,4},{4,5},{5,6},{6,7},{7,8},{8,9},{9,10},{10,1... | collective-permute-start | bytes 294920 | tf_op jit(solution)/shard_map/while/body/eval_jaxpr/ppermute | solution.py:17
  593.7 18.4 %collective-permute-start = (bf16[48,512]{1,0:T(8,128)(2,1)S(1)}, bf16[48,512]{1,0:T(8,128)(2,1)S(1)}, u32[]{:S(2)}, u32[]{:S(2)}) collective-permute-start(bf16[48,512]{1,0:T(8,128)(2,1)S(1)} %get-tuple-element.163), channel_id=1, source_target_pairs={{0,1},{1,2},{2,3},{3,4},{4,5},{5,6},{6,7},{7,8},{8,9},{9,10},{10,1... | collective-permute-start | bytes 147464 | tf_op jit(solution)/shard_map/while/body/eval_jaxpr/ppermute | solution.py:17
  602.3 15.2 %collective-permute-start.4 = (f32[48,512]{1,0:T(8,128)S(1)}, f32[48,512]{1,0:T(8,128)S(1)}, u32[]{:S(2)}, u32[]{:S(2)}) collective-permute-start(f32[48,512]{1,0:T(8,128)S(1)} %get-tuple-element.167), channel_id=1, source_target_pairs={{0,1},{1,2},{2,3},{3,4},{4,5},{5,6},{6,7},{7,8},{8,9},{9,10},{10,1... | collective-permute-start | bytes 294920 | tf_op jit(solution)/shard_map/while/body/eval_jaxpr/ppermute | solution.py:17
  617.6 18.4 %collective-permute-start = (bf16[48,512]{1,0:T(8,128)(2,1)S(1)}, bf16[48,512]{1,0:T(8,128)(2,1)S(1)}, u32[]{:S(2)}, u32[]{:S(2)}) collective-permute-start(bf16[48,512]{1,0:T(8,128)(2,1)S(1)} %get-tuple-element.163), channel_id=1, source_target_pairs={{0,1},{1,2},{2,3},{3,4},{4,5},{5,6},{6,7},{7,8},{8,9},{9,10},{10,1... | collective-permute-start | bytes 147464 | tf_op jit(solution)/shard_map/while/body/eval_jaxpr/ppermute | solution.py:17
  630.7 15.2 %collective-permute-start.4 = (f32[48,512]{1,0:T(8,128)S(1)}, f32[48,512]{1,0:T(8,128)S(1)}, u32[]{:S(2)}, u32[]{:S(2)}) collective-permute-start(f32[48,512]{1,0:T(8,128)S(1)} %get-tuple-element.167), channel_id=1, source_target_pairs={{0,1},{1,2},{2,3},{3,4},{4,5},{5,6},{6,7},{7,8},{8,9},{9,10},{10,1... | collective-permute-start | bytes 294920 | tf_op jit(solution)/shard_map/while/body/eval_jaxpr/ppermute | solution.py:17
  645.9 18.4 %collective-permute-start = (bf16[48,512]{1,0:T(8,128)(2,1)S(1)}, bf16[48,512]{1,0:T(8,128)(2,1)S(1)}, u32[]{:S(2)}, u32[]{:S(2)}) collective-permute-start(bf16[48,512]{1,0:T(8,128)(2,1)S(1)} %get-tuple-element.163), channel_id=1, source_target_pairs={{0,1},{1,2},{2,3},{3,4},{4,5},{5,6},{6,7},{7,8},{8,9},{9,10},{10,1... | collective-permute-start | bytes 147464 | tf_op jit(solution)/shard_map/while/body/eval_jaxpr/ppermute | solution.py:17
  654.2 15.2 %collective-permute-start.4 = (f32[48,512]{1,0:T(8,128)S(1)}, f32[48,512]{1,0:T(8,128)S(1)}, u32[]{:S(2)}, u32[]{:S(2)}) collective-permute-start(f32[48,512]{1,0:T(8,128)S(1)} %get-tuple-element.167), channel_id=1, source_target_pairs={{0,1},{1,2},{2,3},{3,4},{4,5},{5,6},{6,7},{7,8},{8,9},{9,10},{10,1... | collective-permute-start | bytes 294920 | tf_op jit(solution)/shard_map/while/body/eval_jaxpr/ppermute | solution.py:17
  669.5 18.4 %collective-permute-start = (bf16[48,512]{1,0:T(8,128)(2,1)S(1)}, bf16[48,512]{1,0:T(8,128)(2,1)S(1)}, u32[]{:S(2)}, u32[]{:S(2)}) collective-permute-start(bf16[48,512]{1,0:T(8,128)(2,1)S(1)} %get-tuple-element.163), channel_id=1, source_target_pairs={{0,1},{1,2},{2,3},{3,4},{4,5},{5,6},{6,7},{7,8},{8,9},{9,10},{10,1... | collective-permute-start | bytes 147464 | tf_op jit(solution)/shard_map/while/body/eval_jaxpr/ppermute | solution.py:17
  679.8 15.7 %collective-permute-start.4 = (f32[48,512]{1,0:T(8,128)S(1)}, f32[48,512]{1,0:T(8,128)S(1)}, u32[]{:S(2)}, u32[]{:S(2)}) collective-permute-start(f32[48,512]{1,0:T(8,128)S(1)} %get-tuple-element.167), channel_id=1, source_target_pairs={{0,1},{1,2},{2,3},{3,4},{4,5},{5,6},{6,7},{7,8},{8,9},{9,10},{10,1... | collective-permute-start | bytes 294920 | tf_op jit(solution)/shard_map/while/body/eval_jaxpr/ppermute | solution.py:17
  695.5 18.4 %collective-permute-start = (bf16[48,512]{1,0:T(8,128)(2,1)S(1)}, bf16[48,512]{1,0:T(8,128)(2,1)S(1)}, u32[]{:S(2)}, u32[]{:S(2)}) collective-permute-start(bf16[48,512]{1,0:T(8,128)(2,1)S(1)} %get-tuple-element.163), channel_id=1, source_target_pairs={{0,1},{1,2},{2,3},{3,4},{4,5},{5,6},{6,7},{7,8},{8,9},{9,10},{10,1... | collective-permute-start | bytes 147464 | tf_op jit(solution)/shard_map/while/body/eval_jaxpr/ppermute | solution.py:17
  703.3 15.5 %collective-permute-start.4 = (f32[48,512]{1,0:T(8,128)S(1)}, f32[48,512]{1,0:T(8,128)S(1)}, u32[]{:S(2)}, u32[]{:S(2)}) collective-permute-start(f32[48,512]{1,0:T(8,128)S(1)} %get-tuple-element.167), channel_id=1, source_target_pairs={{0,1},{1,2},{2,3},{3,4},{4,5},{5,6},{6,7},{7,8},{8,9},{9,10},{10,1... | collective-permute-start | bytes 294920 | tf_op jit(solution)/shard_map/while/body/eval_jaxpr/ppermute | solution.py:17
  718.8 18.4 %collective-permute-start = (bf16[48,512]{1,0:T(8,128)(2,1)S(1)}, bf16[48,512]{1,0:T(8,128)(2,1)S(1)}, u32[]{:S(2)}, u32[]{:S(2)}) collective-permute-start(bf16[48,512]{1,0:T(8,128)(2,1)S(1)} %get-tuple-element.163), channel_id=1, source_target_pairs={{0,1},{1,2},{2,3},{3,4},{4,5},{5,6},{6,7},{7,8},{8,9},{9,10},{10,1... | collective-permute-start | bytes 147464 | tf_op jit(solution)/shard_map/while/body/eval_jaxpr/ppermute | solution.py:17
  728.1 15.2 %collective-permute-start.4 = (f32[48,512]{1,0:T(8,128)S(1)}, f32[48,512]{1,0:T(8,128)S(1)}, u32[]{:S(2)}, u32[]{:S(2)}) collective-permute-start(f32[48,512]{1,0:T(8,128)S(1)} %get-tuple-element.167), channel_id=1, source_target_pairs={{0,1},{1,2},{2,3},{3,4},{4,5},{5,6},{6,7},{7,8},{8,9},{9,10},{10,1... | collective-permute-start | bytes 294920 | tf_op jit(solution)/shard_map/while/body/eval_jaxpr/ppermute | solution.py:17
  743.3 18.4 %collective-permute-start = (bf16[48,512]{1,0:T(8,128)(2,1)S(1)}, bf16[48,512]{1,0:T(8,128)(2,1)S(1)}, u32[]{:S(2)}, u32[]{:S(2)}) collective-permute-start(bf16[48,512]{1,0:T(8,128)(2,1)S(1)} %get-tuple-element.163), channel_id=1, source_target_pairs={{0,1},{1,2},{2,3},{3,4},{4,5},{5,6},{6,7},{7,8},{8,9},{9,10},{10,1... | collective-permute-start | bytes 147464 | tf_op jit(solution)/shard_map/while/body/eval_jaxpr/ppermute | solution.py:17
  753.0 15.2 %collective-permute-start.4 = (f32[48,512]{1,0:T(8,128)S(1)}, f32[48,512]{1,0:T(8,128)S(1)}, u32[]{:S(2)}, u32[]{:S(2)}) collective-permute-start(f32[48,512]{1,0:T(8,128)S(1)} %get-tuple-element.167), channel_id=1, source_target_pairs={{0,1},{1,2},{2,3},{3,4},{4,5},{5,6},{6,7},{7,8},{8,9},{9,10},{10,1... | collective-permute-start | bytes 294920 | tf_op jit(solution)/shard_map/while/body/eval_jaxpr/ppermute | solution.py:17
  768.3 18.4 %collective-permute-start = (bf16[48,512]{1,0:T(8,128)(2,1)S(1)}, bf16[48,512]{1,0:T(8,128)(2,1)S(1)}, u32[]{:S(2)}, u32[]{:S(2)}) collective-permute-start(bf16[48,512]{1,0:T(8,128)(2,1)S(1)} %get-tuple-element.163), channel_id=1, source_target_pairs={{0,1},{1,2},{2,3},{3,4},{4,5},{5,6},{6,7},{7,8},{8,9},{9,10},{10,1... | collective-permute-start | bytes 147464 | tf_op jit(solution)/shard_map/while/body/eval_jaxpr/ppermute | solution.py:17
  778.7 15.2 %collective-permute-start.4 = (f32[48,512]{1,0:T(8,128)S(1)}, f32[48,512]{1,0:T(8,128)S(1)}, u32[]{:S(2)}, u32[]{:S(2)}) collective-permute-start(f32[48,512]{1,0:T(8,128)S(1)} %get-tuple-element.167), channel_id=1, source_target_pairs={{0,1},{1,2},{2,3},{3,4},{4,5},{5,6},{6,7},{7,8},{8,9},{9,10},{10,1... | collective-permute-start | bytes 294920 | tf_op jit(solution)/shard_map/while/body/eval_jaxpr/ppermute | solution.py:17
  794.2 16.9 %collective-permute-start.9 = (f32[64,640]{1,0:T(8,128)S(1)}, f32[64,640]{1,0:T(8,128)S(1)}, u32[]{:S(2)}, u32[]{:S(2)}) collective-permute-start(f32[64,640]{1,0:T(8,128)S(1)} %constant_dynamic-slice_fusion), channel_id=1, source_target_pairs={{0,32},{32,0},{64,96},{96,64},{128,160},{160,128},{192,224},{224,1... | collective-permute-start | bytes 491528 | tf_op jit(solution)/shard_map/ppermute | solution.py:11
  (99 other events, 1384.5 us)
where the time goes:
time: 820 us; the launch traced here: 813 us
  starting transfers between devices  379 us (46%)
  waiting for transfers between devices  371 us (45%)
  matrix products  40.8 us (5%)
  local copies, waits for them, and re-layouts  13.6 us (2%)
    ppermute x156, starting transfers between devices, shifted(): return lax.ppermute(value, axis, pairs)  371 us
    ppermute x156, waiting for transfers between devices, shifted(): return lax.ppermute(value, axis, pairs)  371 us
  transfers between devices with their start and end apart: 160, of which 124 were waited for; matrix products, arithmetic and copies ran while one was open for 6% of the time, Pallas kernels for 0%

commit v1 on v0

v1 whole, which is shorter than its diff:
```python
import jax
import jax.numpy as jnp
from jax import lax
from jax.experimental import pallas as pl
from jax.experimental.pallas import tpu as pltpu
from jax.sharding import Mesh, PartitionSpec as P

DH = 128
HQ = 4
WIDTH = HQ * DH
SCALE = DH**-0.5
LOG2E = 1.4426950408889634
BF = jnp.bfloat16
F32 = jnp.float32


def pieces(value):
    out = []
    for _ in range(3):
        part = lax.reduce_precision(value, 8, 7)
        out.append(part.astype(BF))
        value = value - part
    return out


def grads_kernel(x_ref, k_ref, v_ref, dq_ref, dk_ref, dv_ref):
    chunks, _, cols = k_ref.shape
    rows = x_ref.shape[0]
    first = pl.program_id(0) == 0

    @pl.when(first)
    def _():
        dk_ref[...] = jnp.zeros_like(dk_ref)
        dv_ref[...] = jnp.zeros_like(dv_ref)

    lane = lax.broadcasted_iota(jnp.int32, (rows, DH), 1)
    row = lax.broadcasted_iota(jnp.int32, (DH, cols), 0)
    k_ones = jnp.where((row < 6 * HQ) & (lax.rem(row, 6) < 3), 1.0, 0.0).astype(BF)
    v_ones = jnp.where((row < 6 * HQ) & (lax.rem(row, 6) >= 3), 1.0, 0.0).astype(BF)
    stats = x_ref[:, 2 * WIDTH : 2 * WIDTH + DH]
    for h in range(HQ):
        q_h = x_ref[:, h * DH : (h + 1) * DH]
        g_h = x_ref[:, WIDTH + h * DH : WIDTH + (h + 1) * DH]
        s_h = jnp.where((lane >= 6 * h) & (lane < 6 * h + 6), stats, jnp.zeros_like(stats))
        q_s = jnp.concatenate([q_h, s_h], 1)
        g_s = jnp.concatenate([g_h, s_h], 1)
        dq = jnp.zeros((rows, DH), F32)
        for j in range(chunks):
            k_j = k_ref[j]
            v_j = v_ref[j]
            s = jnp.dot(q_s, jnp.concatenate([k_j, k_ones], 0), preferred_element_type=F32)
            p = jnp.exp2(s * (SCALE * LOG2E))
            dp = jnp.dot(g_s, jnp.concatenate([v_j, v_ones], 0), preferred_element_type=F32)
            ds = (p * dp).astype(BF)
            pb = p.astype(BF)
            over_rows = (((0,), (0,)), ((), ()))
            dv_ref[j] += lax.dot_general(g_h, pb, over_rows, preferred_element_type=F32)
            dk_ref[j] += lax.dot_general(q_h, ds, over_rows, preferred_element_type=F32)
            dq += lax.dot_general(ds, k_j, (((1,), (1,)), ((), ())), preferred_element_type=F32)
        dq_ref[:, h * DH : (h + 1) * DH] = (dq * SCALE).astype(BF)


def grads(x, k_all, v_all, block):
    rows, width = x.shape
    kv_shape = k_all.shape
    kv_spec = pl.BlockSpec(kv_shape, lambda i: (0, 0, 0))
    work = rows * HQ * kv_shape[0] * kv_shape[2]
    return pl.pallas_call(
        grads_kernel,
        grid=(rows // block,),
        in_specs=[pl.BlockSpec((block, width), lambda i: (i, 0)), kv_spec, kv_spec],
        out_specs=[pl.BlockSpec((block, WIDTH), lambda i: (i, 0)), kv_spec, kv_spec],
        out_shape=[
            jax.ShapeDtypeStruct((rows, WIDTH), BF),
            jax.ShapeDtypeStruct(kv_shape, F32),
            jax.ShapeDtypeStruct(kv_shape, F32),
        ],
        compiler_params=pltpu.CompilerParams(vmem_limit_bytes=48 << 20),
        cost_estimate=pl.CostEstimate(flops=10 * work * DH, bytes_accessed=8 << 20, transcendentals=work),
        name="grads",
    )(x, k_all, v_all)


def per_device(queries, keys, values, outputs, out_grad, logsumexp):
    rows = queries.shape[0]
    half, cols = keys.shape
    zn = lax.axis_size("zl")
    yn = lax.axis_size("y")
    core = lax.axis_index("core")
    swap = [(0, 1), (1, 0)]

    dterm = jnp.sum(
        (out_grad.astype(F32) * outputs.astype(F32)).reshape(rows, HQ, DH), axis=2
    )
    stats = jnp.stack(pieces(logsumexp * (-1.0 / SCALE)) + pieces(-dterm), axis=2)
    stats = jnp.pad(stats.reshape(rows, 6 * HQ), ((0, 0), (0, DH - 6 * HQ)))
    x = jnp.concatenate([queries, out_grad, stats], 1)

    x_all = lax.all_to_all(jnp.broadcast_to(x, (zn,) + x.shape), "zl", 0, 0)
    x_all = x_all.reshape(zn * rows, x.shape[1])

    kv = jnp.stack([keys, values])
    kv_own = lax.all_gather(kv, "y")
    kv_other = lax.ppermute(kv_own, "core", swap)
    low = jnp.where(core == 0, kv_own, kv_other)
    high = jnp.where(core == 0, kv_other, kv_own)
    k_all = jnp.concatenate([low[:, 0], high[:, 0]], 1)
    v_all = jnp.concatenate([low[:, 1], high[:, 1]], 1)

    dq, dk, dv = grads(x_all, k_all, v_all, zn * rows // 2)

    dq = lax.all_to_all(dq.reshape(zn, rows, WIDTH), "zl", 0, 0)
    query_grad = jnp.sum(dq.astype(F32), axis=0).astype(BF)

    dkv = jnp.stack([dk * SCALE, dv], 1).reshape(yn, 2, 2, half, cols)
    keep = jnp.where(core == 0, dkv[:, :, 0], dkv[:, :, 1])
    send = jnp.where(core == 0, dkv[:, :, 1], dkv[:, :, 0]).astype(BF)
    both = keep + lax.ppermute(send, "core", swap).astype(F32)
    parts = lax.all_to_all(both.astype(BF), "y", 0, 0)
    total = jnp.sum(parts.astype(F32), axis=0).astype(BF)
    return query_grad, total[0], total[1]


def solution(mesh):
    devices = mesh.devices.reshape(2, 4, 2, 4, 8)
    inner = Mesh(devices, ("zh", "x", "core", "y", "zl"))
    head = ("zh", "x", "core")
    seq = ("y", "zl")
    text = P(seq, head)
    visual = P(head, seq)
    return jax.shard_map(
        per_device,
        mesh=inner,
        in_specs=(text, visual, visual, text, text, text),
        out_specs=(text, visual, visual),
        check_vma=False,
    )
```

time: 820 us -> 124 us (0.15)
  starting transfers between devices: 379 us -> 20.7 us
  waiting for transfers between devices: 371 us -> 51.4 us
  matrix products: 40.8 us -> 0 us
  blocking collectives: 0 us -> 29 us
  Pallas kernels: 0 us -> 13.6 us
  local copies, waits for them, and re-layouts: 13.6 us -> 2.07 us
    ppermute x160 -> x2, starting transfers between devices: 379 us -> 3.84 us  [the longest x1 1.92 us: per_device(): kv_other = lax.ppermute(kv_own, 'core', swap)]
    ppermute x160 -> x2, waiting for transfers between devices: 371 us -> 4.12 us  [the longest x1 2.06 us: per_device(): both = keep + lax.ppermute(send, 'core', swap).astype(F32)]
    all_to_all x0 -> x2, waiting for transfers between devices: none -> 47.3 us  [the longest x1 26.1 us: per_device(): x_all = lax.all_to_all(jnp.broadcast_to(x, (zn,) + x.shape), 'zl', 0, 0)]
    dot_general x160 -> x0, matrix products: 40.8 us -> none  [the longest x32 9.96 us: block_grads(): jnp.einsum('rd,rv->dv', g_rows, probs_low, preferred_element_type=jnp.flo...]
    all_to_all x0 -> x2, starting transfers between devices: none -> 16.8 us  [the longest x1 12.5 us: per_device(): x_all = lax.all_to_all(jnp.broadcast_to(x, (zn,) + x.shape), 'zl', 0, 0)]
    all_to_all x0 -> x1, blocking collectives: none -> 15.4 us  [per_device(): parts = lax.all_to_all(both.astype(BF), 'y', 0, 0)]
    pallas_call x0 -> x1, Pallas kernels: none -> 13.6 us  [grads(): pl.pallas_call(grads_kernel, grid=(rows // block,), in_specs=[pl.BlockSpe...]
    all_gather x0 -> x1, blocking collectives: none -> 13.6 us  [per_device(): kv_own = lax.all_gather(kv, 'y')]
  transfers between devices with their start and end apart: 160 -> 4, of which waited for: 124 -> 4; matrix products, arithmetic and copies ran while one was open for 6% -> 1% of each run, Pallas kernels for 0% -> 0%
where the time goes in v1:
time: 124 us; the launch traced here: 123 us
  waiting for transfers between devices  51.4 us (41%)
  blocking collectives  29 us (23%)
  starting transfers between devices  20.7 us (17%)
  Pallas kernels  13.6 us (11%)
  other arithmetic  5.67 us (5%)
  local copies, waits for them, and re-layouts  2.07 us (2%)
    all_to_all x1, waiting for transfers between devices, per_device(): x_all = lax.all_to_all(jnp.broadcast_to(x, (zn,) + x.shape), 'zl', 0, 0)  26.1 us
    all_to_all x1, waiting for transfers between devices, per_device(): dq = lax.all_to_all(dq.reshape(zn, rows, WIDTH), 'zl', 0, 0)  21.2 us
    all_to_all x1, blocking collectives, per_device(): parts = lax.all_to_all(both.astype(BF), 'y', 0, 0)  15.4 us
    pallas_call x1, Pallas kernels, grads(): pl.pallas_call(grads_kernel, grid=(rows // block,), in_specs=[pl.BlockSpe...  13.6 us
    all_gather x1, blocking collectives, per_device(): kv_own = lax.all_gather(kv, 'y')  13.6 us
    all_to_all x1, starting transfers between devices, per_device(): x_all = lax.all_to_all(jnp.broadcast_to(x, (zn,) + x.shape), 'zl', 0, 0)  12.5 us
    all_to_all x1, starting transfers between devices, per_device(): dq = lax.all_to_all(dq.reshape(zn, rows, WIDTH), 'zl', 0, 0)  4.3 us
  transfers between devices with their start and end apart: 4, of which 4 were waited for; matrix products, arithmetic and copies ran while one was open for 1% of the time, Pallas kernels for 0%

profile of v1, /device:TPU:6, one launch (start us, length us, event | category | flops | bytes accessed | tf_op | source)
XLA Modules:
  0.0 123.3 jit_solution(4401961000810228072)
XLA Ops:
  0.6 0.7 constant_dynamic-update-slice_fusion.5
  1.3 0.7 constant_dynamic-update-slice_fusion.4
  2.0 0.7 constant_dynamic-update-slice_fusion.3
  2.7 0.8 convert_multiply_fusion
  3.6 0.1 reduce_sum.33
  3.7 0.1 copy.64
  3.9 0.1 copy.63
  4.0 0.8 fusion.4
  4.8 0.0 copy-start
  4.8 0.0 copy-start.1
  4.8 1.0 broadcast_in_dim.3
  5.8 12.5 %all-to-all-start = ((bf16[8,48,1152]{2,1,0:T(8,128)(2,1)}), bf16[8,48,1152]{2,1,0:T(8,128)(2,1)S(1)}, u32[]{:S(2)}, u32[]{:S(2)}) async-start(bf16[8,48,1152]{2,1,0:T(8,128)(2,1)} %broadcast_in_dim.3), calls=%async_computation | async-start | bytes 1769472 | tf_op jit(solution)/shard_map/all_to_all | solution.py:99
  18.3 0.0 copy-done
  18.3 0.0 copy-done.1
  18.4 13.6 %all-gather = bf16[8,64,640]{2,1,0:T(8,128)(2,1)S(1)} all-gather(bf16[2,64,640]{2,1,0:T(8,128)(2,1)S(1)} %pad_maximum_fusion.3), channel_id=2, replica_groups=mesh['zh'=2,'x'=4,'core'=2,'y'=4,'zl'=8] {'y'}, dimensions={0}, use_global_device_ids=true | all-gather | bytes 819200 | tf_op jit(solution)/shard_map/all_gather | solution.py:103
  32.0 0.1 copy.56
  32.0 1.9 %collective-permute-start = (bf16[4,2,64,640]{3,2,0,1:T(8,128)(2,1)S(1)}, bf16[4,2,64,640]{3,2,0,1:T(8,128)(2,1)S(1)}, u32[]{:S(2)}, u32[]{:S(2)}) collective-permute-start(bf16[4,2,64,640]{3,2,0,1:T(8,128)(2,1)S(1)} %copy.56), channel_id=1, source_target_pairs={{0,32},{32,0},{1,33},{33,1},{2,34},{34,2},{3,35},{35,3},{4,36},{36... | collective-permute-start | bytes 1966088 | tf_op jit(solution)/shard_map/ppermute | solution.py:104
  34.0 2.1 %collective-permute-done = bf16[4,2,64,640]{3,2,0,1:T(8,128)(2,1)S(1)} collective-permute-done((bf16[4,2,64,640]{3,2,0,1:T(8,128)(2,1)S(1)}, bf16[4,2,64,640]{3,2,0,1:T(8,128)(2,1)S(1)}, u32[]{:S(2)}, u32[]{:S(2)}) %collective-permute-start) | collective-permute-done | bytes 655392 | tf_op jit(solution)/shard_map/ppermute | solution.py:104
  36.0 0.1 broadcast_select_fusion.1
  36.1 0.1 slice_bitcast_fusion
  36.3 0.1 pad_maximum_fusion.2.v_ref
  36.3 0.1 pad_maximum_fusion.1.k_ref
  36.4 26.1 %all-to-all-done = bf16[8,48,1152]{2,1,0:T(8,128)(2,1)S(1)} async-done(((bf16[8,48,1152]{2,1,0:T(8,128)(2,1)}), bf16[8,48,1152]{2,1,0:T(8,128)(2,1)S(1)}, u32[]{:S(2)}, u32[]{:S(2)}) %all-to-all-start) | async-done | bytes 884768 | tf_op jit(solution)/shard_map/all_to_all | solution.py:99
  62.5 13.6 %grads.1 = (bf16[384,512]{1,0:T(8,128)(2,1)}, f32[4,128,640]{2,1,0:T(8,128)S(1)}, f32[4,128,640]{2,1,0:T(8,128)S(1)}) custom-call(bf16[384,1152]{1,0:T(8,128)(2,1)S(1)} %bitcast.51, bf16[4,128,640]{2,1,0:T(8,128)(2,1)S(1)} %pad_maximum_fusion.1.k_ref, bf16[4,128,640]{2,1,0:T(8,128)(2,1)S(1)} %pad_maximum_fusion.2.v_ref), custom_call_target="tpu_custom_call" | custom-call | flops 5033164800 | bytes 8388608 | tf_op jit(solution)/shard_map/grads/pallas_call | solution.py:68
  76.2 0.1 broadcast_multiply_fusion
  76.3 0.2 pad_maximum_fusion
  76.5 0.1 fusion.2
  76.6 1.9 %collective-permute-start.1 = (bf16[4,2,64,640]{3,2,1,0:T(8,128)(2,1)S(1)}, bf16[4,2,64,640]{3,2,1,0:T(8,128)(2,1)S(1)}, u32[]{:S(2)}, u32[]{:S(2)}) collective-permute-start(bf16[4,2,64,640]{3,2,1,0:T(8,128)(2,1)S(1)} %fusion.2), channel_id=1, source_target_pairs={{0,32},{32,0},{1,33},{33,1},{2,34},{34,2},{3,35},{35,3},{4,36},{36... | collective-permute-start | bytes 1966088 | tf_op jit(solution)/shard_map/ppermute | solution.py:118
  78.5 2.1 %collective-permute-done.1 = bf16[4,2,64,640]{3,2,1,0:T(8,128)(2,1)S(1)} collective-permute-done((bf16[4,2,64,640]{3,2,1,0:T(8,128)(2,1)S(1)}, bf16[4,2,64,640]{3,2,1,0:T(8,128)(2,1)S(1)}, u32[]{:S(2)}, u32[]{:S(2)}) %collective-permute-start.1) | collective-permute-done | bytes 655392 | tf_op jit(solution)/shard_map/ppermute | solution.py:118
  80.6 0.3 fusion.1
  80.9 15.4 %all_to_all.15 = bf16[4,2,64,640]{3,2,1,0:T(8,128)(2,1)S(1)} all-to-all(bf16[4,2,64,640]{3,2,1,0:T(8,128)(2,1)S(1)} %fusion.1), channel_id=1, replica_groups=mesh['zh'=2,'x'=4,'core'=2,'y'=4,'zl'=8] {'y'}, dimensions={0} | all-to-all | bytes 1310720 | tf_op jit(solution)/shard_map/all_to_all | solution.py:119
  96.3 4.3 %all-to-all-start.1 = ((bf16[8,48,512]{2,1,0:T(8,128)(2,1)}), bf16[8,48,512]{2,1,0:T(8,128)(2,1)S(1)}, u32[]{:S(2)}, u32[]{:S(2)}) async-start(bf16[8,48,512]{2,1,0:T(8,128)(2,1)} %bitcast.12), calls=%async_computation.1 | async-start | bytes 786432 | tf_op jit(solution)/shard_map/all_to_all | solution.py:112
  100.6 0.1 reduce_sum.35
  100.7 0.7 slice_bitcast_fusion.4
  101.4 21.2 %all-to-all-done.1 = bf16[8,48,512]{2,1,0:T(8,128)(2,1)S(1)} async-done(((bf16[8,48,512]{2,1,0:T(8,128)(2,1)}), bf16[8,48,512]{2,1,0:T(8,128)(2,1)S(1)}, u32[]{:S(2)}, u32[]{:S(2)}) %all-to-all-start.1) | async-done | bytes 393248 | tf_op jit(solution)/shard_map/all_to_all | solution.py:112
  122.6 0.7 reduce_sum.34
  (8 shorter events, 0.1 us)
Async XLA Ops:
  4.8 13.5 %copy-start = (bf16[64,640]{1,0:T(8,128)(2,1)S(1)}, bf16[64,640]{1,0:T(8,128)(2,1)}, u32[]{:S(2)}) copy-start(bf16[64,640]{1,0:T(8,128)(2,1)} %param.8) | copy-start | bytes 245764
  4.8 13.5 %copy-start.1 = (bf16[64,640]{1,0:T(8,128)(2,1)S(1)}, bf16[64,640]{1,0:T(8,128)(2,1)}, u32[]{:S(2)}) copy-start(bf16[64,640]{1,0:T(8,128)(2,1)} %param.7) | copy-start | bytes 245764
  5.8 56.7 %all-to-all-start = ((bf16[8,48,1152]{2,1,0:T(8,128)(2,1)}), bf16[8,48,1152]{2,1,0:T(8,128)(2,1)S(1)}, u32[]{:S(2)}, u32[]{:S(2)}) async-start(bf16[8,48,1152]{2,1,0:T(8,128)(2,1)} %broadcast_in_dim.3), calls=%async_computation | async-start | bytes 1769472 | tf_op jit(solution)/shard_map/all_to_all | solution.py:99
  32.0 4.0 %collective-permute-start = (bf16[4,2,64,640]{3,2,0,1:T(8,128)(2,1)S(1)}, bf16[4,2,64,640]{3,2,0,1:T(8,128)(2,1)S(1)}, u32[]{:S(2)}, u32[]{:S(2)}) collective-permute-start(bf16[4,2,64,640]{3,2,0,1:T(8,128)(2,1)S(1)} %copy.56), channel_id=1, source_target_pairs={{0,32},{32,0},{1,33},{33,1},{2,34},{34,2},{3,35},{35,3},{4,36},{36... | collective-permute-start | bytes 1966088 | tf_op jit(solution)/shard_map/ppermute | solution.py:104
  76.6 4.0 %collective-permute-start.1 = (bf16[4,2,64,640]{3,2,1,0:T(8,128)(2,1)S(1)}, bf16[4,2,64,640]{3,2,1,0:T(8,128)(2,1)S(1)}, u32[]{:S(2)}, u32[]{:S(2)}) collective-permute-start(bf16[4,2,64,640]{3,2,1,0:T(8,128)(2,1)S(1)} %fusion.2), channel_id=1, source_target_pairs={{0,32},{32,0},{1,33},{33,1},{2,34},{34,2},{3,35},{35,3},{4,36},{36... | collective-permute-start | bytes 1966088 | tf_op jit(solution)/shard_map/ppermute | solution.py:118
  96.3 26.3 %all-to-all-start.1 = ((bf16[8,48,512]{2,1,0:T(8,128)(2,1)}), bf16[8,48,512]{2,1,0:T(8,128)(2,1)S(1)}, u32[]{:S(2)}, u32[]{:S(2)}) async-start(bf16[8,48,512]{2,1,0:T(8,128)(2,1)} %bitcast.12), calls=%async_computation.1 | async-start | bytes 786432 | tf_op jit(solution)/shard_map/all_to_all | solution.py:112

commit v2 on v1

v2 whole, which is shorter than its diff:
```python
import jax
import jax.numpy as jnp
from jax import lax
from jax.experimental import pallas as pl
from jax.experimental.pallas import tpu as pltpu
from jax.sharding import Mesh, PartitionSpec as P

DH = 128
HQ = 4
WIDTH = HQ * DH
SCALE = DH**-0.5
LOG2E = 1.4426950408889634
BF = jnp.bfloat16
F32 = jnp.float32
SWAP = [(0, 1), (1, 0)]
VMEM_GRADS = 60 << 20
MEDIUM = pltpu.CompilerParams(vmem_limit_bytes=12 << 20)
SMALL = pltpu.CompilerParams(vmem_limit_bytes=4 << 20)


def half_swap(value, core):
    rolled = jnp.concatenate([value[:, DH // 2 :], value[:, : DH // 2]], 1)
    return jnp.where(core == 0, value, rolled)


def prep_kernel(core_ref, q_ref, g_ref, o_ref, lse_ref, k_ref, v_ref, x_ref, kv_ref):
    core = core_ref[0]
    rows = q_ref.shape[0]
    lane = lax.broadcasted_iota(jnp.int32, (rows, DH), 1)
    lse = jnp.transpose(lse_ref[...]) * (-1.0 / SCALE)
    stats = jnp.zeros((rows, DH), F32)
    for h in range(HQ):
        at = pl.ds(h * DH, DH)
        q = q_ref[:, at].astype(F32)
        g = g_ref[:, at].astype(F32)
        dterm = jnp.sum(g * o_ref[:, at].astype(F32), axis=1, keepdims=True)
        mine = (lane & (HQ - 1)) == h
        stats = jnp.where(mine & (lane < 3 * HQ), lse[:, h : h + 1], stats)
        stats = jnp.where(mine & (lane >= 3 * HQ) & (lane < 6 * HQ), -dterm, stats)
        x_ref[:, at] = half_swap(q, core).astype(BF)
        x_ref[:, pl.ds(WIDTH + h * DH, DH)] = half_swap(g, core).astype(BF)
    high = stats.astype(BF).astype(F32)
    rest = stats - high
    middle = rest.astype(BF).astype(F32)
    group = lax.shift_right_logical(lane, 2)
    first = (group == 0) | (group == 3)
    second = (group == 1) | (group == 4)
    stats = jnp.where(first, high, jnp.where(second, middle, rest - middle))
    x_ref[:, pl.ds(2 * WIDTH, DH)] = stats.astype(BF)
    kv_ref[0] = k_ref[...]
    kv_ref[1] = v_ref[...]


def prep(core, queries, out_grad, outputs, lse_t, keys, values):
    rows = queries.shape[0]
    return pl.pallas_call(
        prep_kernel,
        in_specs=[pl.BlockSpec(memory_space=pltpu.SMEM)] + [pl.BlockSpec(memory_space=pltpu.VMEM)] * 6,
        out_shape=[
            jax.ShapeDtypeStruct((rows, 2 * WIDTH + DH), BF),
            jax.ShapeDtypeStruct((2,) + keys.shape, BF),
        ],
        name="prep",
    )(core, queries, out_grad, outputs, lse_t, keys, values)


def grads_kernel(last, *refs):
    if last:
        x_ref, own_ref, other_ref, keep_in, send_in, dq_ref, keep_ref, send_ref, q_s, g_s, acc = refs
    else:
        x_ref, own_ref, other_ref, dq_ref, keep_ref, send_ref, q_s, g_s, acc = refs
    blocks, rows, _ = x_ref.shape
    half, cols = own_ref.shape[2:]
    step = pl.program_id(0)

    @pl.when(step == 0)
    def _():
        lane = lax.broadcasted_iota(jnp.int32, (rows, DH), 1)
        for b in range(blocks):
            stats = x_ref[b, :, 2 * WIDTH : 2 * WIDTH + DH].astype(F32)
            for h in range(HQ):
                to = pl.ds((h * blocks + b) * rows, rows)
                mine = jnp.where((lane & (HQ - 1)) == h, stats, 0.0).astype(BF)
                q_s[to, :DH] = x_ref[b, :, h * DH : (h + 1) * DH]
                g_s[to, :DH] = x_ref[b, :, WIDTH + h * DH : WIDTH + (h + 1) * DH]
                q_s[to, DH:] = mine
                g_s[to, DH:] = mine

    row = lax.broadcasted_iota(jnp.int32, (DH, cols), 0)
    k_ones = jnp.where(row < 3 * HQ, 1.0, 0.0).astype(BF)
    v_ones = jnp.where((row >= 3 * HQ) & (row < 6 * HQ), 1.0, 0.0).astype(BF)
    k = jnp.concatenate([own_ref[0, 0], other_ref[0, 0]], 0)
    v = jnp.concatenate([own_ref[0, 1], other_ref[0, 1]], 0)
    s = jnp.dot(q_s[...], jnp.concatenate([k, k_ones], 0), preferred_element_type=F32)
    p = jnp.exp2(s * (SCALE * LOG2E))
    dp = jnp.dot(g_s[...], jnp.concatenate([v, v_ones], 0), preferred_element_type=F32)
    ds = (p * dp).astype(BF)
    pb = p.astype(BF)
    over_rows = (((0,), (0,)), ((), ()))
    dv = lax.dot_general(g_s[:, :DH], pb, over_rows, preferred_element_type=F32)
    dk = lax.dot_general(q_s[:, :DH], ds, over_rows, preferred_element_type=F32) * SCALE
    dq = lax.dot_general(ds, k, (((1,), (1,)), ((), ())), preferred_element_type=F32) * SCALE
    for i, part in enumerate((dk, dv)):
        keep = part[:half]
        send = part[half:]
        if last:
            keep = keep + keep_in[0, i]
            send = send + send_in[0, i]
        keep_ref[0, i] = keep
        send_ref[0, i] = send.astype(send_ref.dtype)

    @pl.when(step == 0)
    def _():
        acc[...] = dq

    @pl.when(step > 0)
    def _():
        acc[...] += dq

    @pl.when(step == pl.num_programs(0) - 1)
    def _():
        for b in range(blocks):
            for h in range(HQ):
                at = pl.ds((h * blocks + b) * rows, rows)
                dq_ref[b, :, h * DH : (h + 1) * DH] = acc[at, :].astype(BF)


def grads(x, own, other, before=None):
    blocks, rows, width = x.shape
    chunks, _, half, cols = own.shape
    total = blocks * rows * HQ
    last = before is not None
    kv_spec = pl.BlockSpec((1, 2, half, cols), lambda i: (i, 0, 0, 0))
    work = total * chunks * cols
    return pl.pallas_call(
        lambda *refs: grads_kernel(last, *refs),
        grid=(chunks,),
        in_specs=[pl.BlockSpec(x.shape, lambda i: (0, 0, 0)), kv_spec, kv_spec] + ([kv_spec] * 2 if last else []),
        out_specs=[pl.BlockSpec((blocks, rows, WIDTH), lambda i: (0, 0, 0)), kv_spec, kv_spec],
        out_shape=[
            jax.ShapeDtypeStruct((blocks, rows, WIDTH), BF),
            jax.ShapeDtypeStruct(own.shape, F32),
            jax.ShapeDtypeStruct(own.shape, BF if last else F32),
        ],
        scratch_shapes=[
            pltpu.VMEM((total, 2 * DH), BF),
            pltpu.VMEM((total, 2 * DH), BF),
            pltpu.VMEM((total, DH), F32),
        ],
        compiler_params=pltpu.CompilerParams(vmem_limit_bytes=VMEM_GRADS),
        cost_estimate=pl.CostEstimate(flops=10 * work * DH, bytes_accessed=4 << 20, transcendentals=work),
        name="grads",
    )(x, own, other, *(before or ()))


def sum_kernel(parts_ref, out_ref):
    total = parts_ref[0].astype(F32)
    for b in range(1, parts_ref.shape[0]):
        total = total + parts_ref[b].astype(F32)
    out_ref[...] = total.astype(out_ref.dtype)


def total_of(parts, dtype):
    return pl.pallas_call(
        sum_kernel,
        out_shape=jax.ShapeDtypeStruct(parts.shape[1:], dtype),
        compiler_params=SMALL,
        name="total_of",
    )(parts)


def query_kernel(core_ref, parts_ref, far_ref, out_ref):
    core = core_ref[0]
    for h in range(HQ):
        at = pl.ds(h * DH, DH)
        total = far_ref[:, at].astype(F32)
        for b in range(parts_ref.shape[0]):
            total = total + parts_ref[b, :, at].astype(F32)
        out_ref[:, at] = half_swap(total, core).astype(BF)


def query_total(core, parts, far):
    return pl.pallas_call(
        query_kernel,
        in_specs=[pl.BlockSpec(memory_space=pltpu.SMEM)] + [pl.BlockSpec(memory_space=pltpu.VMEM)] * 2,
        out_shape=jax.ShapeDtypeStruct(far.shape, BF),
        compiler_params=SMALL,
        name="query_total",
    )(core, parts, far)


def both_kernel(y_ref, keep_ref, got_ref, *out_refs):
    count = len(out_refs)
    for r, out_ref in enumerate(out_refs):
        at = lax.rem(y_ref[0] + r, count)
        out_ref[...] = (keep_ref[at] + got_ref[at].astype(F32)).astype(out_ref.dtype)


def both_cores(y, keep, got):
    one = keep.shape[1:]
    return pl.pallas_call(
        both_kernel,
        in_specs=[pl.BlockSpec(memory_space=pltpu.SMEM)] + [pl.BlockSpec(memory_space=pltpu.VMEM)] * 2,
        out_shape=[jax.ShapeDtypeStruct(one, BF) for r in range(keep.shape[0])],
        compiler_params=MEDIUM,
        name="both_cores",
    )(y, keep, got)


def visual_kernel(*refs):
    parts = refs[:-2]
    for i, out_ref in enumerate(refs[-2:]):
        total = parts[0][i].astype(F32)
        for part in parts[1:]:
            total = total + part[i].astype(F32)
        out_ref[...] = total.astype(BF)


def visual_total(parts):
    one = jax.ShapeDtypeStruct(parts[0].shape[1:], BF)
    return pl.pallas_call(
        visual_kernel, out_shape=[one, one], compiler_params=SMALL, name="visual_total"
    )(*parts)


def along_y(value, steps):
    count = lax.axis_size("y")
    return lax.ppermute(value, "y", [(i, (i + steps) % count) for i in range(count)])


def to_quad(block):
    count = lax.axis_size("zi")
    return lax.all_to_all(jnp.broadcast_to(block, (count,) + block.shape), "zi", 0, 0)


def per_device(queries, keys, values, outputs, out_grad, logsumexp):
    core = lax.axis_index("core").astype(jnp.int32).reshape(1)
    x, kv = prep(core, queries, out_grad, outputs, logsumexp.T, keys, values)

    far = lax.ppermute(x, "zq", SWAP)
    x_near = to_quad(x)

    own = lax.all_gather(kv, "y")
    far, own = lax.optimization_barrier((far, own))
    other = lax.ppermute(own, "core", SWAP)
    x_far = to_quad(far)

    dq_near, keep, send = grads(x_near, own, other)
    near = lax.all_to_all(dq_near, "zi", 0, 0)
    dq_far, keep, send = grads(x_far, own, other, (keep, send))
    near, dq_far = lax.optimization_barrier((near, dq_far))
    far_sum = total_of(lax.all_to_all(dq_far, "zi", 0, 0), BF)
    query_grad = query_total(core, near, lax.ppermute(far_sum, "zq", SWAP))

    y = lax.axis_index("y").astype(jnp.int32).reshape(1)
    both = both_cores(y, keep, lax.ppermute(send, "core", SWAP))
    parts = [both[0]] + [along_y(both[r], r) for r in range(1, len(both))]
    key_grad, value_grad = visual_total(parts)
    return query_grad, key_grad, value_grad


def solution(mesh):
    devices = mesh.devices.reshape(2, 4, 2, 4, 2, 4)
    inner = Mesh(devices, ("zh", "x", "core", "y", "zq", "zi"))
    head = ("zh", "x", "core")
    seq = ("y", "zq", "zi")
    text = P(seq, head)
    visual = P(head, seq)
    return jax.shard_map(
        per_device,
        mesh=inner,
        in_specs=(text, visual, visual, text, text, text),
        out_specs=(text, visual, visual),
        check_vma=False,
    )
```

time: 124 us -> 97.5 us (0.79)
  waiting for transfers between devices: 51.4 us -> 7.59 us
  starting transfers between devices: 20.7 us -> 49 us
  blocking collectives: 29 us -> 13.6 us
  Pallas kernels: 13.6 us -> 20.4 us
  other arithmetic: 5.67 us -> 0 us
  local copies, waits for them, and re-layouts: 2.07 us -> 4.82 us
    all_to_all x2 -> x4, waiting for transfers between devices: 47.3 us -> 0.01 us  [the longest x2 0.01 us: to_quad(): lax.all_to_all(jnp.broadcast_to(block, (count,) + block.shape), 'zi', 0, 0)]
    ppermute x2 -> x7, starting transfers between devices: 3.84 us -> 27.8 us  [the longest x3 10.4 us: along_y(): lax.ppermute(value, 'y', [(i, (i + steps) % count) for i in range(count)])]
    all_to_all x1 -> x0, blocking collectives: 15.4 us -> none  [per_device(): parts = lax.all_to_all(both.astype(BF), 'y', 0, 0)]
    pallas_call x1 -> x7, Pallas kernels: 13.6 us -> 20.4 us  [the longest x2 16.8 us: grads(): pl.pallas_call(lambda *refs: grads_kernel(last, *refs), grid=(chunks,), i...]
    all_to_all x2 -> x4, starting transfers between devices: 16.8 us -> 21.2 us  [the longest x2 11 us: to_quad(): lax.all_to_all(jnp.broadcast_to(block, (count,) + block.shape), 'zi', 0, 0)]
    ppermute x2 -> x7, waiting for transfers between devices: 4.12 us -> 7.58 us  [the longest x1 4.41 us: per_device(): query_grad = query_total(core, near, lax.ppermute(far_sum, 'zq', SWAP))]
    unnamed x5 -> x0, other arithmetic: 2.1 us -> none
    unnamed x6 -> x14, local copies, waits for them, and re-layouts: 0.18 us -> 2.19 us
  transfers between devices with their start and end apart: 4 -> 11, of which waited for: 4 -> 3; matrix products, arithmetic and copies ran while one was open for 1% -> 0% of each run, Pallas kernels for 0% -> 18%
where the time goes in v2:
time: 97.5 us; the launch traced here: 96.1 us
  starting transfers between devices  49 us (50%)
  Pallas kernels  20.4 us (21%)
  blocking collectives  13.6 us (14%)
  waiting for transfers between devices  7.59 us (8%)
  local copies, waits for them, and re-layouts  4.82 us (5%)
    pallas_call x2, Pallas kernels, grads(): pl.pallas_call(lambda *refs: grads_kernel(last, *refs), grid=(chunks,), i...  16.8 us
    all_gather x1, blocking collectives, per_device(): own = lax.all_gather(kv, 'y')  13.6 us
    all_to_all x2, starting transfers between devices, to_quad(): lax.all_to_all(jnp.broadcast_to(block, (count,) + block.shape), 'zi', 0, 0)  11 us
    ppermute x3, starting transfers between devices, along_y(): lax.ppermute(value, 'y', [(i, (i + steps) % count) for i in range(count)])  10.4 us
    ppermute x1, starting transfers between devices, per_device(): far = lax.ppermute(x, 'zq', SWAP)  9.09 us
    all_to_all x1, starting transfers between devices, per_device(): near = lax.all_to_all(dq_near, 'zi', 0, 0)  5.11 us
    all_to_all x1, starting transfers between devices, per_device(): far_sum = total_of(lax.all_to_all(dq_far, 'zi', 0, 0), BF)  5.1 us
    ppermute x1, starting transfers between devices, per_device(): query_grad = query_total(core, near, lax.ppermute(far_sum, 'zq', SWAP))  4.55 us
  transfers between devices with their start and end apart: 11, of which 3 were waited for; matrix products, arithmetic and copies ran while one was open for 0% of the time, Pallas kernels for 18%

profile of v2, /device:TPU:6, one launch (start us, length us, event | category | flops | bytes accessed | tf_op | source)
XLA Modules:
  0.0 96.1 jit_solution(188146295004398460)
XLA Ops:
  0.6 2.0 %prep.1 = (bf16[48,1152]{1,0:T(8,128)(2,1)}, bf16[2,64,640]{2,1,0:T(8,128)(2,1)}) custom-call(s32[1]{0:T(128)} %bitcast.core_ref, bf16[48,512]{1,0:T(8,128)(2,1)} %q_ref.1, bf16[48,512]{1,0:T(8,128)(2,1)} %g_ref.1, bf16[48,512]{1,0:T(8,128)(2,1)} %o_ref.1, f32[4,48]{1,0:T(4,128)} %bitcast.7, bf16[64,640]{1,0:T(8,128)(2,1)} %k_ref.1, bf16[64,640]{1,0:T(8,128)(2,1)} %v_ref.1), custom_call_target="tpu_custom_call" | custom-call | tf_op jit(solution)/shard_map/prep/pallas_call | solution.py:56
  2.6 0.0 copy-start.5
  2.6 0.0 copy-start.4
  2.6 1.8 %broadcast_in_dim.6 = bf16[4,48,1152]{2,1,0:T(8,128)(2,1)} broadcast(bf16[48,1152]{1,0:T(8,128)(2,1)} %get-tuple-element.21), dimensions={1,2} | broadcast | bytes 552960 | tf_op jit(solution)/shard_map/broadcast_in_dim | solution.py:233
  4.4 5.9 %all-to-all-start = ((bf16[4,48,1152]{2,1,0:T(8,128)(2,1)}), bf16[4,48,1152]{2,1,0:T(8,128)(2,1)S(1)}, u32[]{:S(2)}, u32[]{:S(2)}) async-start(bf16[4,48,1152]{2,1,0:T(8,128)(2,1)} %broadcast_in_dim.6), calls=%async_computation | async-start | bytes 884736 | tf_op jit(solution)/shard_map/all_to_all | solution.py:233
  10.3 0.0 copy-done.5
  10.3 9.1 %collective-permute-start = (bf16[48,1152]{1,0:T(8,128)(2,1)S(1)}, bf16[48,1152]{1,0:T(8,128)(2,1)S(1)}, u32[]{:S(2)}, u32[]{:S(2)}) collective-permute-start(bf16[48,1152]{1,0:T(8,128)(2,1)S(1)} %copy-done.5), channel_id=1, source_target_pairs={{0,4},{4,0},{1,5},{5,1},{2,6},{6,2},{3,7},{7,3},{8,12},{12,8},{9,1... | collective-permute-start | bytes 331784 | tf_op jit(solution)/shard_map/ppermute | solution.py:240
  19.4 0.0 copy-done.4
  19.4 13.6 %all-gather = bf16[8,64,640]{2,1,0:T(8,128)(2,1)S(1)} all-gather(bf16[2,64,640]{2,1,0:T(8,128)(2,1)S(1)} %copy-done.4), channel_id=2, replica_groups=mesh['zh'=2,'x'=4,'core'=2,'y'=4,'zq'=2,'zi'=4] {'y'}, dimensions={0}, use_global_device_ids=true | all-gather | bytes 819200 | tf_op jit(solution)/shard_map/all_gather | solution.py:243
  33.0 0.0 copy-start.1
  33.0 0.0 collective-permute-done
  33.0 0.0 all-to-all-done.refs_0_
  33.0 0.0 copy-start.2
  33.0 0.9 broadcast_in_dim.7
  33.9 5.1 %all-to-all-start.2 = ((bf16[4,48,1152]{2,1,0:T(8,128)(2,1)}), bf16[4,48,1152]{2,1,0:T(8,128)(2,1)S(1)}, u32[]{:S(2)}, u32[]{:S(2)}) async-start(bf16[4,48,1152]{2,1,0:T(8,128)(2,1)} %broadcast_in_dim.7), calls=%async_computation.2 | async-start | bytes 884736 | tf_op jit(solution)/shard_map/all_to_all | solution.py:233
  39.0 1.9 %collective-permute-start.1 = (bf16[4,2,64,640]{3,2,1,0:T(8,128)(2,1)S(1)}, bf16[4,2,64,640]{3,2,1,0:T(8,128)(2,1)S(1)}, u32[]{:S(2)}, u32[]{:S(2)}) collective-permute-start(bf16[4,2,64,640]{3,2,1,0:T(8,128)(2,1)S(1)} %bitcast.4), channel_id=1, source_target_pairs={{0,32},{32,0},{1,33},{33,1},{2,34},{34,2},{3,35},{35,3},{4,36},{36... | collective-permute-start | bytes 1966088 | tf_op jit(solution)/shard_map/ppermute | solution.py:245
  40.9 2.1 %collective-permute-done.1.refs_2_ = bf16[4,2,64,640]{3,2,1,0:T(8,128)(2,1)S(1)} collective-permute-done((bf16[4,2,64,640]{3,2,1,0:T(8,128)(2,1)S(1)}, bf16[4,2,64,640]{3,2,1,0:T(8,128)(2,1)S(1)}, u32[]{:S(2)}, u32[]{:S(2)}) %collective-permute-start.1) | collective-permute-done | bytes 655392 | tf_op jit(solution)/shard_map/ppermute | solution.py:245
  42.9 0.0 copy-done.1
  42.9 0.0 copy-done.2
  42.9 0.0 copy-start.6
  42.9 0.9 copy-done.6
  43.8 8.3 %grads.2 = (bf16[4,48,512]{2,1,0:T(8,128)(2,1)}, f32[4,2,64,640]{3,2,1,0:T(8,128)}, f32[4,2,64,640]{3,2,1,0:T(8,128)}) custom-call(bf16[4,48,1152]{2,1,0:T(8,128)(2,1)} %copy-done.2, bf16[4,2,64,640]{3,2,1,0:T(8,128)(2,1)} %bitcast.5, bf16[4,2,64,640]{3,2,1,0:T(8,128)(2,1)} %copy-done.6), custom_call_target="tpu_custom_call" | custom-call | flops 2516582400 | bytes 4194304 | tf_op jit(solution)/shard_map/grads/pallas_call | solution.py:135
  52.1 0.0 all-to-all-done.2.refs_0_
  52.1 0.0 copy-start.3
  52.1 5.1 %all-to-all-start.1 = ((bf16[4,48,512]{2,1,0:T(8,128)(2,1)}), bf16[4,48,512]{2,1,0:T(8,128)(2,1)S(1)}, u32[]{:S(2)}, u32[]{:S(2)}) async-start(bf16[4,48,512]{2,1,0:T(8,128)(2,1)} %get-tuple-element.24), calls=%async_computation.1 | async-start | bytes 393216 | tf_op jit(solution)/shard_map/all_to_all | solution.py:249
  57.2 0.0 copy-done.3
  57.2 8.5 %grads.3 = (bf16[4,48,512]{2,1,0:T(8,128)(2,1)}, f32[4,2,64,640]{3,2,1,0:T(8,128)}, bf16[4,2,64,640]{3,2,1,0:T(8,128)(2,1)}) custom-call(bf16[4,48,1152]{2,1,0:T(8,128)(2,1)} %copy-done.3, bf16[4,2,64,640]{3,2,1,0:T(8,128)(2,1)} %bitcast.6, bf16[4,2,64,640]{3,2,1,0:T(8,128)(2,1)} %copy-done.6, f32[4,2,64,640]{3,2,1,0:T(8,128)} %get-tuple-element.26.refs_3_, ...), custom_call_target="tpu_custom_call" | custom-call | flops 2516582400 | bytes 4194304 | tf_op jit(solution)/shard_map/grads/pallas_call | solution.py:135
  65.7 1.9 %collective-permute-start.3 = (bf16[4,2,64,640]{3,2,1,0:T(8,128)(2,1)}, bf16[4,2,64,640]{3,2,1,0:T(8,128)(2,1)S(1)}, u32[]{:S(2)}, u32[]{:S(2)}) collective-permute-start(bf16[4,2,64,640]{3,2,1,0:T(8,128)(2,1)} %get-tuple-element.32), channel_id=1, source_target_pairs={{0,32},{32,0},{1,33},{33,1},{2,34},{34,2},{3,35},{35,3},{4,36},{36... | collective-permute-start | bytes 1966088 | tf_op jit(solution)/shard_map/ppermute | solution.py:256
  67.6 0.0 all-to-all-done.1.parts_ref
  67.6 5.1 %all-to-all-start.3 = ((bf16[4,48,512]{2,1,0:T(8,128)(2,1)}), bf16[4,48,512]{2,1,0:T(8,128)(2,1)S(1)}, u32[]{:S(2)}, u32[]{:S(2)}) async-start(bf16[4,48,512]{2,1,0:T(8,128)(2,1)} %get-tuple-element.30), calls=%async_computation.3 | async-start | bytes 393216 | tf_op jit(solution)/shard_map/all_to_all | solution.py:252
  72.7 0.0 collective-permute-done.3.got_ref
  72.7 0.0 copy-start
  72.7 1.3 %copy-done = f32[4,2,64,640]{3,2,1,0:T(8,128)S(1)} copy-done((f32[4,2,64,640]{3,2,1,0:T(8,128)S(1)}, f32[4,2,64,640]{3,2,1,0:T(8,128)}, u32[]{:S(2)}) %copy-start) | copy-done | bytes 1310744
  74.1 0.1 both_cores.1
  74.2 3.9 %collective-permute-start.4 = (bf16[2,64,640]{2,1,0:T(8,128)(2,1)S(1)}, bf16[2,64,640]{2,1,0:T(8,128)(2,1)S(1)}, u32[]{:S(2)}, u32[]{:S(2)}) collective-permute-start(bf16[2,64,640]{2,1,0:T(8,128)(2,1)S(1)} %get-tuple-element.34), channel_id=1, source_target_pairs={{0,8},{8,16},{16,24},{24,0},{1,9},{9,17},{17,25},{25,1},{2,10},{10... | collective-permute-start | bytes 491528 | tf_op jit(solution)/shard_map/ppermute | solution.py:228
  78.0 4.6 %collective-permute-start.5 = (bf16[2,64,640]{2,1,0:T(8,128)(2,1)S(1)}, bf16[2,64,640]{2,1,0:T(8,128)(2,1)S(1)}, u32[]{:S(2)}, u32[]{:S(2)}) collective-permute-start(bf16[2,64,640]{2,1,0:T(8,128)(2,1)S(1)} %get-tuple-element.35), channel_id=1, source_target_pairs={{0,16},{8,24},{16,0},{24,8},{1,17},{9,25},{17,1},{25,9},{2,18},{10... | collective-permute-start | bytes 491528 | tf_op jit(solution)/shard_map/ppermute | solution.py:228
  82.6 1.9 %collective-permute-start.6 = (bf16[2,64,640]{2,1,0:T(8,128)(2,1)S(1)}, bf16[2,64,640]{2,1,0:T(8,128)(2,1)S(1)}, u32[]{:S(2)}, u32[]{:S(2)}) collective-permute-start(bf16[2,64,640]{2,1,0:T(8,128)(2,1)S(1)} %get-tuple-element.36), channel_id=1, source_target_pairs={{0,24},{8,0},{16,8},{24,16},{1,25},{9,1},{17,9},{25,17},{2,26},{10... | collective-permute-start | bytes 491528 | tf_op jit(solution)/shard_map/ppermute | solution.py:228
  84.6 0.0 all-to-all-done.3.parts_ref
  84.6 4.6 %collective-permute-start.2 = (bf16[48,512]{1,0:T(8,128)(2,1)S(1)}, bf16[48,512]{1,0:T(8,128)(2,1)S(1)}, u32[]{:S(2)}, u32[]{:S(2)}) collective-permute-start(bf16[48,512]{1,0:T(8,128)(2,1)S(1)} %total_of.1), channel_id=1, source_target_pairs={{0,4},{4,0},{1,5},{5,1},{2,6},{6,2},{3,7},{7,3},{8,12},{12,8},{9,1... | collective-permute-start | bytes 147464 | tf_op jit(solution)/shard_map/ppermute | solution.py:253
  89.2 0.0 collective-permute-done.4.refs_1_
  89.2 0.0 collective-permute-done.5.refs_2_
  89.2 1.1 %collective-permute-done.6.refs_3_ = bf16[2,64,640]{2,1,0:T(8,128)(2,1)S(1)} collective-permute-done((bf16[2,64,640]{2,1,0:T(8,128)(2,1)S(1)}, bf16[2,64,640]{2,1,0:T(8,128)(2,1)S(1)}, u32[]{:S(2)}, u32[]{:S(2)}) %collective-permute-start.6) | collective-permute-done | bytes 163872 | tf_op jit(solution)/shard_map/ppermute | solution.py:228
  90.3 0.7 visual_total.1
  91.0 4.4 %collective-permute-done.2.far_ref = bf16[48,512]{1,0:T(8,128)(2,1)S(1)} collective-permute-done((bf16[48,512]{1,0:T(8,128)(2,1)S(1)}, bf16[48,512]{1,0:T(8,128)(2,1)S(1)}, u32[]{:S(2)}, u32[]{:S(2)}) %collective-permute-start.2) | collective-permute-done | bytes 49184 | tf_op jit(solution)/shard_map/ppermute | solution.py:253
  95.4 0.7 query_total.1
  (1 shorter events, 0.0 us)
Async XLA Ops:
  2.6 7.7 %copy-start.5 = (bf16[48,1152]{1,0:T(8,128)(2,1)S(1)}, bf16[48,1152]{1,0:T(8,128)(2,1)}, u32[]{:S(2)}) copy-start(bf16[48,1152]{1,0:T(8,128)(2,1)} %get-tuple-element.21) | copy-start | bytes 331780
  2.6 16.8 %copy-start.4 = (bf16[2,64,640]{2,1,0:T(8,128)(2,1)S(1)}, bf16[2,64,640]{2,1,0:T(8,128)(2,1)}, u32[]{:S(2)}) copy-start(bf16[2,64,640]{2,1,0:T(8,128)(2,1)} %get-tuple-element.22) | copy-start | bytes 491524
  4.4 28.6 %all-to-all-start = ((bf16[4,48,1152]{2,1,0:T(8,128)(2,1)}), bf16[4,48,1152]{2,1,0:T(8,128)(2,1)S(1)}, u32[]{:S(2)}, u32[]{:S(2)}) async-start(bf16[4,48,1152]{2,1,0:T(8,128)(2,1)} %broadcast_in_dim.6), calls=%async_computation | async-start | bytes 884736 | tf_op jit(solution)/shard_map/all_to_all | solution.py:233
  10.3 22.7 %collective-permute-start = (bf16[48,1152]{1,0:T(8,128)(2,1)S(1)}, bf16[48,1152]{1,0:T(8,128)(2,1)S(1)}, u32[]{:S(2)}, u32[]{:S(2)}) collective-permute-start(bf16[48,1152]{1,0:T(8,128)(2,1)S(1)} %copy-done.5), channel_id=1, source_target_pairs={{0,4},{4,0},{1,5},{5,1},{2,6},{6,2},{3,7},{7,3},{8,12},{12,8},{9,1... | collective-permute-start | bytes 331784 | tf_op jit(solution)/shard_map/ppermute | solution.py:240
  33.0 10.0 %copy-start.1 = (bf16[8,64,640]{2,1,0:T(8,128)(2,1)}, bf16[8,64,640]{2,1,0:T(8,128)(2,1)S(1)}, u32[]{:S(2)}) copy-start(bf16[8,64,640]{2,1,0:T(8,128)(2,1)S(1)} %all-gather) | copy-start | bytes 1966084
  33.0 9.9 %copy-start.2 = (bf16[4,48,1152]{2,1,0:T(8,128)(2,1)}, bf16[4,48,1152]{2,1,0:T(8,128)(2,1)S(1)}, u32[]{:S(2)}) copy-start(bf16[4,48,1152]{2,1,0:T(8,128)(2,1)S(1)} %all-to-all-done.refs_0_) | copy-start | bytes 1327108
  33.9 18.2 %all-to-all-start.2 = ((bf16[4,48,1152]{2,1,0:T(8,128)(2,1)}), bf16[4,48,1152]{2,1,0:T(8,128)(2,1)S(1)}, u32[]{:S(2)}, u32[]{:S(2)}) async-start(bf16[4,48,1152]{2,1,0:T(8,128)(2,1)} %broadcast_in_dim.7), calls=%async_computation.2 | async-start | bytes 884736 | tf_op jit(solution)/shard_map/all_to_all | solution.py:233
  39.0 4.0 %collective-permute-start.1 = (bf16[4,2,64,640]{3,2,1,0:T(8,128)(2,1)S(1)}, bf16[4,2,64,640]{3,2,1,0:T(8,128)(2,1)S(1)}, u32[]{:S(2)}, u32[]{:S(2)}) collective-permute-start(bf16[4,2,64,640]{3,2,1,0:T(8,128)(2,1)S(1)} %bitcast.4), channel_id=1, source_target_pairs={{0,32},{32,0},{1,33},{33,1},{2,34},{34,2},{3,35},{35,3},{4,36},{36... | collective-permute-start | bytes 1966088 | tf_op jit(solution)/shard_map/ppermute | solution.py:245
  42.9 0.9 copy-start.6
  52.1 5.1 %copy-start.3 = (bf16[4,48,1152]{2,1,0:T(8,128)(2,1)}, bf16[4,48,1152]{2,1,0:T(8,128)(2,1)S(1)}, u32[]{:S(2)}) copy-start(bf16[4,48,1152]{2,1,0:T(8,128)(2,1)S(1)} %all-to-all-done.2.refs_0_) | copy-start | bytes 1327108
  52.1 15.5 %all-to-all-start.1 = ((bf16[4,48,512]{2,1,0:T(8,128)(2,1)}), bf16[4,48,512]{2,1,0:T(8,128)(2,1)S(1)}, u32[]{:S(2)}, u32[]{:S(2)}) async-start(bf16[4,48,512]{2,1,0:T(8,128)(2,1)} %get-tuple-element.24), calls=%async_computation.1 | async-start | bytes 393216 | tf_op jit(solution)/shard_map/all_to_all | solution.py:249
  65.7 7.0 %collective-permute-start.3 = (bf16[4,2,64,640]{3,2,1,0:T(8,128)(2,1)}, bf16[4,2,64,640]{3,2,1,0:T(8,128)(2,1)S(1)}, u32[]{:S(2)}, u32[]{:S(2)}) collective-permute-start(bf16[4,2,64,640]{3,2,1,0:T(8,128)(2,1)} %get-tuple-element.32), channel_id=1, source_target_pairs={{0,32},{32,0},{1,33},{33,1},{2,34},{34,2},{3,35},{35,3},{4,36},{36... | collective-permute-start | bytes 1966088 | tf_op jit(solution)/shard_map/ppermute | solution.py:256
  67.6 16.9 %all-to-all-start.3 = ((bf16[4,48,512]{2,1,0:T(8,128)(2,1)}), bf16[4,48,512]{2,1,0:T(8,128)(2,1)S(1)}, u32[]{:S(2)}, u32[]{:S(2)}) async-start(bf16[4,48,512]{2,1,0:T(8,128)(2,1)} %get-tuple-element.30), calls=%async_computation.3 | async-start | bytes 393216 | tf_op jit(solution)/shard_map/all_to_all | solution.py:252
  72.7 1.3 %copy-start = (f32[4,2,64,640]{3,2,1,0:T(8,128)S(1)}, f32[4,2,64,640]{3,2,1,0:T(8,128)}, u32[]{:S(2)}) copy-start(f32[4,2,64,640]{3,2,1,0:T(8,128)} %get-tuple-element.31.keep_ref) | copy-start | bytes 3932164
  74.2 15.0 %collective-permute-start.4 = (bf16[2,64,640]{2,1,0:T(8,128)(2,1)S(1)}, bf16[2,64,640]{2,1,0:T(8,128)(2,1)S(1)}, u32[]{:S(2)}, u32[]{:S(2)}) collective-permute-start(bf16[2,64,640]{2,1,0:T(8,128)(2,1)S(1)} %get-tuple-element.34), channel_id=1, source_target_pairs={{0,8},{8,16},{16,24},{24,0},{1,9},{9,17},{17,25},{25,1},{2,10},{10... | collective-permute-start | bytes 491528 | tf_op jit(solution)/shard_map/ppermute | solution.py:228
  78.0 11.1 %collective-permute-start.5 = (bf16[2,64,640]{2,1,0:T(8,128)(2,1)S(1)}, bf16[2,64,640]{2,1,0:T(8,128)(2,1)S(1)}, u32[]{:S(2)}, u32[]{:S(2)}) collective-permute-start(bf16[2,64,640]{2,1,0:T(8,128)(2,1)S(1)} %get-tuple-element.35), channel_id=1, source_target_pairs={{0,16},{8,24},{16,0},{24,8},{1,17},{9,25},{17,1},{25,9},{2,18},{10... | collective-permute-start | bytes 491528 | tf_op jit(solution)/shard_map/ppermute | solution.py:228
  82.6 7.7 %collective-permute-start.6 = (bf16[2,64,640]{2,1,0:T(8,128)(2,1)S(1)}, bf16[2,64,640]{2,1,0:T(8,128)(2,1)S(1)}, u32[]{:S(2)}, u32[]{:S(2)}) collective-permute-start(bf16[2,64,640]{2,1,0:T(8,128)(2,1)S(1)} %get-tuple-element.36), channel_id=1, source_target_pairs={{0,24},{8,0},{16,8},{24,16},{1,25},{9,1},{17,9},{25,17},{2,26},{10... | collective-permute-start | bytes 491528 | tf_op jit(solution)/shard_map/ppermute | solution.py:228
  84.6 10.8 %collective-permute-start.2 = (bf16[48,512]{1,0:T(8,128)(2,1)S(1)}, bf16[48,512]{1,0:T(8,128)(2,1)S(1)}, u32[]{:S(2)}, u32[]{:S(2)}) collective-permute-start(bf16[48,512]{1,0:T(8,128)(2,1)S(1)} %total_of.1), channel_id=1, source_target_pairs={{0,4},{4,0},{1,5},{5,1},{2,6},{6,2},{3,7},{7,3},{8,12},{12,8},{9,1... | collective-permute-start | bytes 147464 | tf_op jit(solution)/shard_map/ppermute | solution.py:253

commit v3 on v2

v3 whole, which is shorter than its diff:
```python
import jax
import jax.numpy as jnp
from jax import lax
from jax.experimental import pallas as pl
from jax.experimental.pallas import tpu as pltpu
from jax.sharding import Mesh, PartitionSpec as P

DH = 128
HQ = 4
WIDTH = HQ * DH
SCALE = DH**-0.5
LOG2E = 1.4426950408889634
BF = jnp.bfloat16
F32 = jnp.float32
SWAP = [(0, 1), (1, 0)]
VMEM_GRADS = 40 << 20
SPARE = 10
MEDIUM = pltpu.CompilerParams(vmem_limit_bytes=12 << 20)
SMALL = pltpu.CompilerParams(vmem_limit_bytes=4 << 20)


def half_swap(value, core):
    rolled = jnp.concatenate([value[:, DH // 2 :], value[:, : DH // 2]], 1)
    return jnp.where(core == 0, value, rolled)


def prep_kernel(core_ref, q_ref, g_ref, o_ref, lse_ref, k_ref, v_ref, x_ref, kv_ref):
    core = core_ref[0]
    rows = q_ref.shape[0]
    lane = lax.broadcasted_iota(jnp.int32, (rows, DH), 1)
    lse = jnp.transpose(lse_ref[...]) * (-1.0 / SCALE)
    stats = jnp.zeros((rows, DH), F32)
    for h in range(HQ):
        at = pl.ds(h * DH, DH)
        q = q_ref[:, at].astype(F32)
        g = g_ref[:, at].astype(F32)
        dterm = jnp.sum(g * o_ref[:, at].astype(F32), axis=1, keepdims=True)
        mine = (lane & (HQ - 1)) == h
        stats = jnp.where(mine & (lane < 3 * HQ), lse[:, h : h + 1], stats)
        stats = jnp.where(mine & (lane >= 3 * HQ) & (lane < 6 * HQ), -dterm, stats)
        x_ref[:, at] = half_swap(q, core).astype(BF)
        x_ref[:, pl.ds(WIDTH + h * DH, DH)] = half_swap(g, core).astype(BF)
    high = stats.astype(BF).astype(F32)
    rest = stats - high
    middle = rest.astype(BF).astype(F32)
    group = lax.shift_right_logical(lane, 2)
    first = (group == 0) | (group == 3)
    second = (group == 1) | (group == 4)
    stats = jnp.where(first, high, jnp.where(second, middle, rest - middle))
    x_ref[:, pl.ds(2 * WIDTH, DH)] = stats.astype(BF)
    kv_ref[0] = k_ref[...]
    kv_ref[1] = v_ref[...]


def prep(core, queries, out_grad, outputs, lse_t, keys, values):
    rows = queries.shape[0]
    return pl.pallas_call(
        prep_kernel,
        in_specs=[pl.BlockSpec(memory_space=pltpu.SMEM)] + [pl.BlockSpec(memory_space=pltpu.VMEM)] * 6,
        out_shape=[
            jax.ShapeDtypeStruct((rows, 2 * WIDTH + DH), BF),
            jax.ShapeDtypeStruct((2,) + keys.shape, BF),
        ],
        name="prep",
    )(core, queries, out_grad, outputs, lse_t, keys, values)


def grads_kernel(blocks, chunks, last, *refs):
    refs = list(refs)
    at_ref = refs.pop(0)
    if last:
        x_refs, refs = refs[:blocks], refs[blocks:]
    else:
        x_ref = refs.pop(0)
        x_refs = [x_ref.at[b] for b in range(blocks)]
    kv_refs, refs = refs[:chunks], refs[chunks:]
    if last:
        before_ref, dq_ref, keep_ref, send_ref, q_s, g_s, acc, held, kept, sems, out_sems = refs
        copies = [pltpu.make_async_copy(before_ref.at[j], held.at[j], sems.at[j]) for j in range(chunks)]
        for copy in copies:
            copy.start()
        out_copies = [pltpu.make_async_copy(kept.at[j], keep_ref.at[j], out_sems.at[j]) for j in range(chunks)]
    else:
        dq_ref, after_ref, q_s, g_s, acc, held, sems = refs
        copies = [pltpu.make_async_copy(held.at[j], after_ref.at[j], sems.at[j]) for j in range(chunks)]
    rows = x_refs[0].shape[0]
    _, _, half, cols = kv_refs[0].shape
    lane = lax.broadcasted_iota(jnp.int32, (rows, DH), 1)
    for b in range(blocks):
        stats = x_refs[b][:, 2 * WIDTH : 2 * WIDTH + DH].astype(F32)
        for h in range(HQ):
            to = pl.ds((h * blocks + b) * rows, rows)
            mine = jnp.where((lane & (HQ - 1)) == h, stats, 0.0).astype(BF)
            q_s[to, :DH] = x_refs[b][:, h * DH : (h + 1) * DH]
            g_s[to, :DH] = x_refs[b][:, WIDTH + h * DH : WIDTH + (h + 1) * DH]
            q_s[to, DH:] = mine
            g_s[to, DH:] = mine

    row = lax.broadcasted_iota(jnp.int32, (DH, cols), 0)
    k_ones = jnp.where(row < 3 * HQ, 1.0, 0.0).astype(BF)
    v_ones = jnp.where((row >= 3 * HQ) & (row < 6 * HQ), 1.0, 0.0).astype(BF)
    over_rows = (((0,), (0,)), ((), ()))
    for j in range(chunks):
        k = jnp.concatenate([kv_refs[j][0, 0], kv_refs[j][1, 0]], 0)
        v = jnp.concatenate([kv_refs[j][0, 1], kv_refs[j][1, 1]], 0)
        s = jnp.dot(q_s[...], jnp.concatenate([k, k_ones], 0), preferred_element_type=F32)
        p = jnp.exp2(s * (SCALE * LOG2E))
        dp = jnp.dot(g_s[...], jnp.concatenate([v, v_ones], 0), preferred_element_type=F32)
        ds = (p * dp).astype(BF)
        pb = p.astype(BF)
        dv = lax.dot_general(g_s[:, :DH], pb, over_rows, preferred_element_type=F32)
        dk = lax.dot_general(q_s[:, :DH], ds, over_rows, preferred_element_type=F32) * SCALE
        dq = lax.dot_general(ds, k, (((1,), (1,)), ((), ())), preferred_element_type=F32) * SCALE
        if last:
            copies[j].wait()
            for i, part in enumerate((dk, dv)):
                total = part + held[j, i]
                kept[j, i] = total[:half]
                send_ref[j, i] = total[half:].astype(BF)
            out_copies[j].start()
        else:
            held[j, 0] = dk
            held[j, 1] = dv
            copies[j].start()
        if j == 0:
            acc[...] = dq
        else:
            acc[...] += dq

    for b in range(blocks):
        place = lax.rem(at_ref[0] + blocks - b, blocks) if last else b
        for h in range(HQ):
            at = pl.ds((h * blocks + b) * rows, rows)
            dq_ref[place, :, h * DH : (h + 1) * DH] = acc[at, :].astype(BF)
    for copy in out_copies if last else copies:
        copy.wait()


def grads(place, x, kv, before=None):
    blocks, chunks = len(x), len(kv)
    rows, width = x[0].shape
    _, _, half, cols = kv[0].shape
    total = blocks * rows * HQ
    last = before is not None
    work = total * chunks * cols
    whole = pl.BlockSpec(memory_space=pltpu.VMEM)
    far = pl.BlockSpec(memory_space=pltpu.HBM)
    sums = (chunks, 2, 2 * half, cols)
    roomy = (SPARE * chunks,) + sums[1:]
    halves = (chunks, 2, half, cols)
    dq = jax.ShapeDtypeStruct((blocks, rows, WIDTH), BF)
    if last:
        operands = (place, *x, *kv, before)
        in_specs = [whole] * (len(operands) - 2) + [far]
        out_shape = [dq, jax.ShapeDtypeStruct(halves, F32), jax.ShapeDtypeStruct(halves, BF)]
        out_specs = [whole, far, whole]
        more = [pltpu.VMEM(halves, F32), pltpu.SemaphoreType.DMA((chunks,)), pltpu.SemaphoreType.DMA((chunks,))]
    else:
        operands = (place, x, *kv)
        in_specs = [whole] * (len(operands) - 1)
        out_shape = [dq, jax.ShapeDtypeStruct(roomy, F32)]
        out_specs = [whole, far]
        more = [pltpu.SemaphoreType.DMA((chunks,))]
    return pl.pallas_call(
        lambda *refs: grads_kernel(blocks, chunks, last, *refs),
        in_specs=[pl.BlockSpec(memory_space=pltpu.SMEM)] + in_specs,
        out_specs=out_specs,
        out_shape=out_shape,
        scratch_shapes=[
            pltpu.VMEM((total, 2 * DH), BF),
            pltpu.VMEM((total, 2 * DH), BF),
            pltpu.VMEM((total, DH), F32),
            pltpu.VMEM(sums, F32),
        ]
        + more,
        compiler_params=pltpu.CompilerParams(vmem_limit_bytes=VMEM_GRADS),
        cost_estimate=pl.CostEstimate(flops=10 * work * DH, bytes_accessed=4 << 20, transcendentals=work),
        name="grads",
    )(*operands)


def sum_kernel(parts_ref, out_ref):
    total = parts_ref[0].astype(F32)
    for b in range(1, parts_ref.shape[0]):
        total = total + parts_ref[b].astype(F32)
    out_ref[...] = total.astype(out_ref.dtype)


def total_of(parts, dtype):
    return pl.pallas_call(
        sum_kernel,
        out_shape=jax.ShapeDtypeStruct(parts.shape[1:], dtype),
        compiler_params=SMALL,
        name="total_of",
    )(parts)


def query_kernel(core_ref, parts_ref, far_ref, out_ref):
    core = core_ref[0]
    for h in range(HQ):
        at = pl.ds(h * DH, DH)
        total = far_ref[:, at].astype(F32)
        for b in range(parts_ref.shape[0]):
            total = total + parts_ref[b, :, at].astype(F32)
        out_ref[:, at] = half_swap(total, core).astype(BF)


def query_total(core, parts, far):
    return pl.pallas_call(
        query_kernel,
        in_specs=[pl.BlockSpec(memory_space=pltpu.SMEM)] + [pl.BlockSpec(memory_space=pltpu.VMEM)] * 2,
        out_shape=jax.ShapeDtypeStruct(far.shape, BF),
        compiler_params=SMALL,
        name="query_total",
    )(core, parts, far)


def both_kernel(keep_ref, got_ref, *refs):
    out_refs, (keep, got, sems) = refs[:-3], refs[-3:]
    copies = []
    for r in range(len(out_refs)):
        pair = (
            pltpu.make_async_copy(keep_ref.at[r], keep.at[r], sems.at[0, r]),
            pltpu.make_async_copy(got_ref.at[r], got.at[r], sems.at[1, r]),
        )
        for copy in pair:
            copy.start()
        copies.append(pair)
    for r, out_ref in enumerate(out_refs):
        for copy in copies[r]:
            copy.wait()
        out_ref[...] = (keep[r] + got[r].astype(F32)).astype(out_ref.dtype)


def both_cores(keep, got):
    count = keep.shape[0]
    one = jax.ShapeDtypeStruct(keep.shape[1:], BF)
    return pl.pallas_call(
        both_kernel,
        in_specs=[pl.BlockSpec(memory_space=pltpu.HBM)] * 2,
        out_shape=[one] * count,
        scratch_shapes=[
            pltpu.VMEM(keep.shape, keep.dtype),
            pltpu.VMEM(got.shape, got.dtype),
            pltpu.SemaphoreType.DMA((2, count)),
        ],
        compiler_params=MEDIUM,
        name="both_cores",
    )(keep, got)


def visual_kernel(*refs):
    parts = refs[:-2]
    for i, out_ref in enumerate(refs[-2:]):
        total = parts[0][i].astype(F32)
        for part in parts[1:]:
            total = total + part[i].astype(F32)
        out_ref[...] = total.astype(BF)


def visual_total(parts):
    one = jax.ShapeDtypeStruct(parts[0].shape[1:], BF)
    return pl.pallas_call(
        visual_kernel, out_shape=[one, one], compiler_params=SMALL, name="visual_total"
    )(*parts)


def along(axis, value, steps):
    count = lax.axis_size(axis)
    return lax.ppermute(value, axis, [(i, (i + steps) % count) for i in range(count)])


def to_quad(block):
    count = lax.axis_size("zi")
    return lax.all_to_all(jnp.broadcast_to(block, (count,) + block.shape), "zi", 0, 0)


def per_device(queries, keys, values, outputs, out_grad, logsumexp):
    core = lax.axis_index("core").astype(jnp.int32).reshape(1)
    x, kv = prep(core, queries, out_grad, outputs, logsumexp.T, keys, values)

    far = lax.ppermute(x, "zq", SWAP)
    kv = jnp.stack([kv, lax.ppermute(kv, "core", SWAP)])
    x_near = [x] + [along("zi", x, r) for r in range(1, lax.axis_size("zi"))]
    far, kv, x_near = lax.optimization_barrier((far, kv, x_near))
    kv = [kv] + [along("y", kv, -r) for r in range(1, lax.axis_size("y"))]
    x_far = to_quad(far)

    place = lax.axis_index("zi").astype(jnp.int32).reshape(1)
    dq_far, sums = grads(place, x_far, kv)
    far_parts = lax.all_to_all(dq_far, "zi", 0, 0)
    dq_near, keep, send = grads(place, x_near, kv, sums)
    far_parts, send, dq_near = lax.optimization_barrier((far_parts, send, dq_near))
    both = both_cores(keep, lax.ppermute(send, "core", SWAP))
    near_parts = lax.all_to_all(dq_near, "zi", 0, 0)
    far_sum = lax.ppermute(total_of(far_parts, BF), "zq", SWAP)
    query_grad = query_total(core, near_parts, far_sum)

    parts = [both[0]] + [along("y", both[r], r) for r in range(1, len(both))]
    key_grad, value_grad = visual_total(parts)
    return query_grad, key_grad, value_grad


def solution(mesh):
    devices = mesh.devices.reshape(2, 4, 2, 4, 2, 4)
    inner = Mesh(devices, ("zh", "x", "core", "y", "zq", "zi"))
    head = ("zh", "x", "core")
    seq = ("y", "zq", "zi")
    text = P(seq, head)
    visual = P(head, seq)
    return jax.shard_map(
        per_device,
        mesh=inner,
        in_specs=(text, visual, visual, text, text, text),
        out_specs=(text, visual, visual),
        check_vma=False,
    )
```

time: 97.5 us -> 118 us (1.21)
  starting transfers between devices: 49 us -> 76 us
  blocking collectives: 13.6 us -> 0 us
  waiting for transfers between devices: 7.59 us -> 15.9 us
  local copies, waits for them, and re-layouts: 4.82 us -> 2.55 us
    ppermute x6 -> x12, starting transfers between devices: 18.7 us -> 46.1 us  [the longest x9 34.1 us: along(): lax.ppermute(value, axis, [(i, (i + steps) % count) for i in range(count)])]
    all_gather x1 -> x0, blocking collectives: 13.6 us -> none  [per_device(): own = lax.all_gather(kv, 'y')]
    ppermute x6 -> x12, waiting for transfers between devices: 7.58 us -> 13.5 us  [the longest x9 10.5 us: along(): lax.ppermute(value, axis, [(i, (i + steps) % count) for i in range(count)])]
    ppermute x1, waiting for transfers between devices: 0.01 us -> 2.39 us  [per_device(): far = lax.ppermute(x, 'zq', SWAP)]
    broadcast_in_dim x2 -> x1, local copies, waits for them, and re-layouts: 2.63 us -> 0.8 us  [to_quad(): jnp.broadcast_to(block, (count,) + block.shape)]
    all_to_all x2 -> x1, starting transfers between devices: 11 us -> 10.9 us  [to_quad(): lax.all_to_all(jnp.broadcast_to(block, (count,) + block.shape), 'zi', 0, 0)]
  transfers between devices with their start and end apart: 11 -> 16, of which waited for: 3 -> 5; matrix products, arithmetic and copies ran while one was open for 0% -> 1% of each run, Pallas kernels for 18% -> 10%
where the time goes in v3:
time: 118 us; the launch traced here: 117 us
  starting transfers between devices  76 us (64%)
  Pallas kernels  20.8 us (18%)
  waiting for transfers between devices  15.9 us (13%)
  local copies, waits for them, and re-layouts  2.55 us (2%)
    ppermute x9, starting transfers between devices, along(): lax.ppermute(value, axis, [(i, (i + steps) % count) for i in range(count)])  34.1 us
    pallas_call x2, Pallas kernels, grads(): pl.pallas_call(lambda *refs: grads_kernel(blocks, chunks, last, *refs), i...  15.9 us
    all_to_all x1, starting transfers between devices, to_quad(): lax.all_to_all(jnp.broadcast_to(block, (count,) + block.shape), 'zi', 0, 0)  10.9 us
    ppermute x9, waiting for transfers between devices, along(): lax.ppermute(value, axis, [(i, (i + steps) % count) for i in range(count)])  10.5 us
    ppermute x1, starting transfers between devices, per_device(): far = lax.ppermute(x, 'zq', SWAP)  9.1 us
    ppermute x1, starting transfers between devices, per_device(): far_sum = lax.ppermute(total_of(far_parts, BF), 'zq', SWAP)  8.19 us
    all_to_all x1, starting transfers between devices, per_device(): near_parts = lax.all_to_all(dq_near, 'zi', 0, 0)  5.1 us
    all_to_all x1, starting transfers between devices, per_device(): far_parts = lax.all_to_all(dq_far, 'zi', 0, 0)  4.8 us
  transfers between devices with their start and end apart: 16, of which 5 were waited for; matrix products, arithmetic and copies ran while one was open for 1% of the time, Pallas kernels for 10%

profile of v3, /device:TPU:6, one launch (start us, length us, event | category | flops | bytes accessed | tf_op | source)
XLA Modules:
  0.0 117.0 jit_solution(6161127842156008082)
XLA Ops:
  0.6 2.0 %prep.1 = (bf16[48,1152]{1,0:T(8,128)(2,1)}, bf16[2,64,640]{2,1,0:T(8,128)(2,1)}) custom-call(s32[1]{0:T(128)} %bitcast.core_ref, bf16[48,512]{1,0:T(8,128)(2,1)} %q_ref.1, bf16[48,512]{1,0:T(8,128)(2,1)} %g_ref.1, bf16[48,512]{1,0:T(8,128)(2,1)} %o_ref.1, f32[4,48]{1,0:T(4,128)} %bitcast.7, bf16[64,640]{1,0:T(8,128)(2,1)} %k_ref.1, bf16[64,640]{1,0:T(8,128)(2,1)} %v_ref.1), custom_call_target="tpu_custom_call" | custom-call | tf_op jit(solution)/shard_map/prep/pallas_call | solution.py:57
  2.6 1.9 %collective-permute-start.1 = (bf16[2,64,640]{2,1,0:T(8,128)(2,1)}, bf16[2,64,640]{2,1,0:T(8,128)(2,1)S(1)}, u32[]{:S(2)}, u32[]{:S(2)}) collective-permute-start(bf16[2,64,640]{2,1,0:T(8,128)(2,1)} %get-tuple-element.26), channel_id=1, source_target_pairs={{0,32},{32,0},{1,33},{33,1},{2,34},{34,2},{3,35},{35,3},{4,36},{36... | collective-permute-start | bytes 491528 | tf_op jit(solution)/shard_map/ppermute | solution.py:283
  4.6 6.5 %collective-permute-start.4 = (bf16[48,1152]{1,0:T(8,128)(2,1)}, bf16[48,1152]{1,0:T(8,128)(2,1)S(1)}, u32[]{:S(2)}, u32[]{:S(2)}) collective-permute-start(bf16[48,1152]{1,0:T(8,128)(2,1)} %get-tuple-element.30.refs_1_), channel_id=1, source_target_pairs={{0,3},{1,0},{2,1},{3,2},{4,7},{5,4},{6,5},{7,6},{8,11},{9,8},{10,9... | collective-permute-start | bytes 331784 | tf_op jit(solution)/shard_map/ppermute | solution.py:270
  11.1 1.9 %collective-permute-start.3 = (bf16[48,1152]{1,0:T(8,128)(2,1)}, bf16[48,1152]{1,0:T(8,128)(2,1)S(1)}, u32[]{:S(2)}, u32[]{:S(2)}) collective-permute-start(bf16[48,1152]{1,0:T(8,128)(2,1)} %get-tuple-element.30.refs_1_), channel_id=1, source_target_pairs={{0,2},{1,3},{2,0},{3,1},{4,6},{5,7},{6,4},{7,5},{8,10},{9,11},{10,... | collective-permute-start | bytes 331784 | tf_op jit(solution)/shard_map/ppermute | solution.py:270
  13.0 2.6 %collective-permute-start.2 = (bf16[48,1152]{1,0:T(8,128)(2,1)}, bf16[48,1152]{1,0:T(8,128)(2,1)S(1)}, u32[]{:S(2)}, u32[]{:S(2)}) collective-permute-start(bf16[48,1152]{1,0:T(8,128)(2,1)} %get-tuple-element.30.refs_1_), channel_id=1, source_target_pairs={{0,1},{1,2},{2,3},{3,0},{4,5},{5,6},{6,7},{7,4},{8,9},{9,10},{10,1... | collective-permute-start | bytes 331784 | tf_op jit(solution)/shard_map/ppermute | solution.py:270
  15.6 9.1 %collective-permute-start = (bf16[48,1152]{1,0:T(8,128)(2,1)}, bf16[48,1152]{1,0:T(8,128)(2,1)S(1)}, u32[]{:S(2)}, u32[]{:S(2)}) collective-permute-start(bf16[48,1152]{1,0:T(8,128)(2,1)} %get-tuple-element.30.refs_1_), channel_id=1, source_target_pairs={{0,4},{4,0},{1,5},{5,1},{2,6},{6,2},{3,7},{7,3},{8,12},{12,8},{9,1... | collective-permute-start | bytes 331784 | tf_op jit(solution)/shard_map/ppermute | solution.py:282
  24.7 0.0 collective-permute-done.1
  24.7 1.0 pad_maximum_fusion.refs_2_.refs_5_
  25.7 0.0 collective-permute-done.4.refs_4_
  25.7 0.0 collective-permute-done.3.refs_3_
  25.7 0.0 collective-permute-done.2.refs_2_
  25.7 2.4 %collective-permute-done = bf16[48,1152]{1,0:T(8,128)(2,1)S(1)} collective-permute-done((bf16[48,1152]{1,0:T(8,128)(2,1)}, bf16[48,1152]{1,0:T(8,128)(2,1)S(1)}, u32[]{:S(2)}, u32[]{:S(2)}) %collective-permute-start) | collective-permute-done | bytes 110624 | tf_op jit(solution)/shard_map/ppermute | solution.py:282
  28.1 0.8 broadcast_in_dim.3
  28.9 10.9 %all-to-all-start = ((bf16[4,48,1152]{2,1,0:T(8,128)(2,1)}), bf16[4,48,1152]{2,1,0:T(8,128)(2,1)S(1)}, u32[]{:S(2)}, u32[]{:S(2)}) async-start(bf16[4,48,1152]{2,1,0:T(8,128)(2,1)} %broadcast_in_dim.3), calls=%async_computation | async-start | bytes 884736 | tf_op jit(solution)/shard_map/all_to_all | solution.py:275
  39.8 3.5 %collective-permute-start.7 = (bf16[2,2,64,640]{3,2,1,0:T(8,128)(2,1)S(1)}, bf16[2,2,64,640]{3,2,1,0:T(8,128)(2,1)S(1)}, u32[]{:S(2)}, u32[]{:S(2)}) collective-permute-start(bf16[2,2,64,640]{3,2,1,0:T(8,128)(2,1)S(1)} %pad_maximum_fusion.refs_2_.refs_5_), channel_id=1, source_target_pairs={{0,8},{8,16},{16,24},{24,0},{1,9},{9,17},{17,25},{25,1},{2,10},{10... | collective-permute-start | bytes 983048 | tf_op jit(solution)/shard_map/ppermute | solution.py:270
  43.3 4.8 %collective-permute-start.6 = (bf16[2,2,64,640]{3,2,1,0:T(8,128)(2,1)S(1)}, bf16[2,2,64,640]{3,2,1,0:T(8,128)(2,1)S(1)}, u32[]{:S(2)}, u32[]{:S(2)}) collective-permute-start(bf16[2,2,64,640]{3,2,1,0:T(8,128)(2,1)S(1)} %pad_maximum_fusion.refs_2_.refs_5_), channel_id=1, source_target_pairs={{0,16},{8,24},{16,0},{24,8},{1,17},{9,25},{17,1},{25,9},{2,18},{10... | collective-permute-start | bytes 983048 | tf_op jit(solution)/shard_map/ppermute | solution.py:270
  48.1 3.3 %collective-permute-start.5 = (bf16[2,2,64,640]{3,2,1,0:T(8,128)(2,1)S(1)}, bf16[2,2,64,640]{3,2,1,0:T(8,128)(2,1)S(1)}, u32[]{:S(2)}, u32[]{:S(2)}) collective-permute-start(bf16[2,2,64,640]{3,2,1,0:T(8,128)(2,1)S(1)} %pad_maximum_fusion.refs_2_.refs_5_), channel_id=1, source_target_pairs={{0,24},{8,0},{16,8},{24,16},{1,25},{9,1},{17,9},{25,17},{2,26},{10... | collective-permute-start | bytes 983048 | tf_op jit(solution)/shard_map/ppermute | solution.py:270
  51.3 1.0 collective-permute-done.7.refs_5_.refs_8_
  52.4 8.1 %collective-permute-done.6.refs_4_.refs_7_ = bf16[2,2,64,640]{3,2,1,0:T(8,128)(2,1)S(1)} collective-permute-done((bf16[2,2,64,640]{3,2,1,0:T(8,128)(2,1)S(1)}, bf16[2,2,64,640]{3,2,1,0:T(8,128)(2,1)S(1)}, u32[]{:S(2)}, u32[]{:S(2)}) %collective-permute-start.6) | collective-permute-done | bytes 327712 | tf_op jit(solution)/shard_map/ppermute | solution.py:270
  60.5 1.3 %collective-permute-done.5.refs_3_.refs_6_ = bf16[2,2,64,640]{3,2,1,0:T(8,128)(2,1)S(1)} collective-permute-done((bf16[2,2,64,640]{3,2,1,0:T(8,128)(2,1)S(1)}, bf16[2,2,64,640]{3,2,1,0:T(8,128)(2,1)S(1)}, u32[]{:S(2)}, u32[]{:S(2)}) %collective-permute-start.5) | collective-permute-done | bytes 327712 | tf_op jit(solution)/shard_map/ppermute | solution.py:270
  61.8 0.0 all-to-all-done.refs_1_
  61.8 6.4 %grads.2 = (bf16[4,48,512]{2,1,0:T(8,128)(2,1)}, f32[40,2,128,640]{3,2,1,0:T(8,128)}) custom-call(s32[1]{0:T(128)} %bitcast.1.refs_0_, bf16[4,48,1152]{2,1,0:T(8,128)(2,1)S(1)} %all-to-all-done.refs_1_, bf16[2,2,64,640]{3,2,1,0:T(8,128)(2,1)S(1)} %pad_maximum_fusion.refs_2_.refs_5_, bf16[2,2,64,640]{3,2,1,0:T(8,128)(2,1)S(1)} %collective-permute-done.5.refs_3_.refs_6_, ...), custom_call_target="tpu_custom_call" | custom-call | flops 2516582400 | bytes 4194304 | tf_op jit(solution)/shard_map/grads/pallas_call | solution.py:164
  68.2 4.8 %all-to-all-start.1 = ((bf16[4,48,512]{2,1,0:T(8,128)(2,1)}), bf16[4,48,512]{2,1,0:T(8,128)(2,1)S(1)}, u32[]{:S(2)}, u32[]{:S(2)}) async-start(bf16[4,48,512]{2,1,0:T(8,128)(2,1)} %get-tuple-element.29), calls=%async_computation.1 | async-start | bytes 393216 | tf_op jit(solution)/shard_map/all_to_all | solution.py:291
  73.0 0.0 copy-start
  73.0 0.9 copy-done
  73.9 9.5 %grads.3 = (bf16[4,48,512]{2,1,0:T(8,128)(2,1)}, f32[4,2,64,640]{3,2,1,0:T(8,128)S(1)}, bf16[4,2,64,640]{3,2,1,0:T(8,128)(2,1)S(1)}) custom-call(s32[1]{0:T(128)} %bitcast.1.refs_0_, bf16[48,1152]{1,0:T(8,128)(2,1)S(1)} %copy-done, bf16[48,1152]{1,0:T(8,128)(2,1)S(1)} %collective-permute-done.2.refs_2_, bf16[48,1152]{1,0:T(8,128)(2,1)S(1)} %collective-permute-done.3.refs_3_, ...), custom_call_target="tpu_custom_call" | custom-call | flops 2516582400 | bytes 4194304 | tf_op jit(solution)/shard_map/grads/pallas_call | solution.py:164
  83.4 0.0 copy-start.1
  83.4 0.8 copy-done.1
  84.3 0.0 all-to-all-done.1.parts_ref
  84.3 1.9 %collective-permute-start.9 = (bf16[4,2,64,640]{3,2,1,0:T(8,128)(2,1)}, bf16[4,2,64,640]{3,2,1,0:T(8,128)(2,1)S(1)}, u32[]{:S(2)}, u32[]{:S(2)}) collective-permute-start(bf16[4,2,64,640]{3,2,1,0:T(8,128)(2,1)} %copy-done.1), channel_id=1, source_target_pairs={{0,32},{32,0},{1,33},{33,1},{2,34},{34,2},{3,35},{35,3},{4,36},{36... | collective-permute-start | bytes 1966088 | tf_op jit(solution)/shard_map/ppermute | solution.py:294
  86.2 5.1 %all-to-all-start.2 = ((bf16[4,48,512]{2,1,0:T(8,128)(2,1)}), bf16[4,48,512]{2,1,0:T(8,128)(2,1)S(1)}, u32[]{:S(2)}, u32[]{:S(2)}) async-start(bf16[4,48,512]{2,1,0:T(8,128)(2,1)} %get-tuple-element.37), calls=%async_computation.2 | async-start | bytes 393216 | tf_op jit(solution)/shard_map/all_to_all | solution.py:295
  91.3 0.0 collective-permute-done.9.got_ref
  91.3 1.5 %both_cores.1 = (bf16[2,64,640]{2,1,0:T(8,128)(2,1)S(1)}, bf16[2,64,640]{2,1,0:T(8,128)(2,1)S(1)}, bf16[2,64,640]{2,1,0:T(8,128)(2,1)S(1)}, bf16[2,64,640]{2,1,0:T(8,128)(2,1)S(1)}) custom-call(f32[4,2,64,640]{3,2,1,0:T(8,128)S(1)} %get-tuple-element.39.keep_ref, bf16[4,2,64,640]{3,2,1,0:T(8,128)(2,1)S(1)} %collective-permute-done.9.got_ref), custom_call_target="tpu_custom_call" | custom-call | tf_op jit(solution)/shard_map/both_cores/pallas_call | solution.py:238
  92.8 4.4 %collective-permute-start.10 = (bf16[2,64,640]{2,1,0:T(8,128)(2,1)S(1)}, bf16[2,64,640]{2,1,0:T(8,128)(2,1)S(1)}, u32[]{:S(2)}, u32[]{:S(2)}) collective-permute-start(bf16[2,64,640]{2,1,0:T(8,128)(2,1)S(1)} %get-tuple-element.42), channel_id=1, source_target_pairs={{0,8},{8,16},{16,24},{24,0},{1,9},{9,17},{17,25},{25,1},{2,10},{10... | collective-permute-start | bytes 491528 | tf_op jit(solution)/shard_map/ppermute | solution.py:270
  97.2 3.5 %collective-permute-start.11 = (bf16[2,64,640]{2,1,0:T(8,128)(2,1)S(1)}, bf16[2,64,640]{2,1,0:T(8,128)(2,1)S(1)}, u32[]{:S(2)}, u32[]{:S(2)}) collective-permute-start(bf16[2,64,640]{2,1,0:T(8,128)(2,1)S(1)} %get-tuple-element.43), channel_id=1, source_target_pairs={{0,16},{8,24},{16,0},{24,8},{1,17},{9,25},{17,1},{25,9},{2,18},{10... | collective-permute-start | bytes 491528 | tf_op jit(solution)/shard_map/ppermute | solution.py:270
  100.7 3.6 %collective-permute-start.12 = (bf16[2,64,640]{2,1,0:T(8,128)(2,1)S(1)}, bf16[2,64,640]{2,1,0:T(8,128)(2,1)S(1)}, u32[]{:S(2)}, u32[]{:S(2)}) collective-permute-start(bf16[2,64,640]{2,1,0:T(8,128)(2,1)S(1)} %get-tuple-element.44), channel_id=1, source_target_pairs={{0,24},{8,0},{16,8},{24,16},{1,25},{9,1},{17,9},{25,17},{2,26},{10... | collective-permute-start | bytes 491528 | tf_op jit(solution)/shard_map/ppermute | solution.py:270
  104.3 8.2 %collective-permute-start.8 = (bf16[48,512]{1,0:T(8,128)(2,1)S(1)}, bf16[48,512]{1,0:T(8,128)(2,1)S(1)}, u32[]{:S(2)}, u32[]{:S(2)}) collective-permute-start(bf16[48,512]{1,0:T(8,128)(2,1)S(1)} %total_of.1), channel_id=1, source_target_pairs={{0,4},{4,0},{1,5},{5,1},{2,6},{6,2},{3,7},{7,3},{8,12},{12,8},{9,1... | collective-permute-start | bytes 147464 | tf_op jit(solution)/shard_map/ppermute | solution.py:296
  112.5 3.0 %collective-permute-done.8.far_ref = bf16[48,512]{1,0:T(8,128)(2,1)S(1)} collective-permute-done((bf16[48,512]{1,0:T(8,128)(2,1)S(1)}, bf16[48,512]{1,0:T(8,128)(2,1)S(1)}, u32[]{:S(2)}, u32[]{:S(2)}) %collective-permute-start.8) | collective-permute-done | bytes 49184 | tf_op jit(solution)/shard_map/ppermute | solution.py:296
  115.5 0.0 all-to-all-done.2.parts_ref
  115.5 0.7 query_total.1
  116.2 0.0 collective-permute-done.10.refs_1_
  116.2 0.0 collective-permute-done.11.refs_2_
  116.2 0.0 collective-permute-done.12.refs_3_
  116.3 0.7 visual_total.1
  (1 shorter events, 0.0 us)
Async XLA Ops:
  2.6 22.1 %collective-permute-start.1 = (bf16[2,64,640]{2,1,0:T(8,128)(2,1)}, bf16[2,64,640]{2,1,0:T(8,128)(2,1)S(1)}, u32[]{:S(2)}, u32[]{:S(2)}) collective-permute-start(bf16[2,64,640]{2,1,0:T(8,128)(2,1)} %get-tuple-element.26), channel_id=1, source_target_pairs={{0,32},{32,0},{1,33},{33,1},{2,34},{34,2},{3,35},{35,3},{4,36},{36... | collective-permute-start | bytes 491528 | tf_op jit(solution)/shard_map/ppermute | solution.py:283
  4.6 21.1 %collective-permute-start.4 = (bf16[48,1152]{1,0:T(8,128)(2,1)}, bf16[48,1152]{1,0:T(8,128)(2,1)S(1)}, u32[]{:S(2)}, u32[]{:S(2)}) collective-permute-start(bf16[48,1152]{1,0:T(8,128)(2,1)} %get-tuple-element.30.refs_1_), channel_id=1, source_target_pairs={{0,3},{1,0},{2,1},{3,2},{4,7},{5,4},{6,5},{7,6},{8,11},{9,8},{10,9... | collective-permute-start | bytes 331784 | tf_op jit(solution)/shard_map/ppermute | solution.py:270
  11.1 14.6 %collective-permute-start.3 = (bf16[48,1152]{1,0:T(8,128)(2,1)}, bf16[48,1152]{1,0:T(8,128)(2,1)S(1)}, u32[]{:S(2)}, u32[]{:S(2)}) collective-permute-start(bf16[48,1152]{1,0:T(8,128)(2,1)} %get-tuple-element.30.refs_1_), channel_id=1, source_target_pairs={{0,2},{1,3},{2,0},{3,1},{4,6},{5,7},{6,4},{7,5},{8,10},{9,11},{10,... | collective-permute-start | bytes 331784 | tf_op jit(solution)/shard_map/ppermute | solution.py:270
  13.0 12.7 %collective-permute-start.2 = (bf16[48,1152]{1,0:T(8,128)(2,1)}, bf16[48,1152]{1,0:T(8,128)(2,1)S(1)}, u32[]{:S(2)}, u32[]{:S(2)}) collective-permute-start(bf16[48,1152]{1,0:T(8,128)(2,1)} %get-tuple-element.30.refs_1_), channel_id=1, source_target_pairs={{0,1},{1,2},{2,3},{3,0},{4,5},{5,6},{6,7},{7,4},{8,9},{9,10},{10,1... | collective-permute-start | bytes 331784 | tf_op jit(solution)/shard_map/ppermute | solution.py:270
  15.6 12.5 %collective-permute-start = (bf16[48,1152]{1,0:T(8,128)(2,1)}, bf16[48,1152]{1,0:T(8,128)(2,1)S(1)}, u32[]{:S(2)}, u32[]{:S(2)}) collective-permute-start(bf16[48,1152]{1,0:T(8,128)(2,1)} %get-tuple-element.30.refs_1_), channel_id=1, source_target_pairs={{0,4},{4,0},{1,5},{5,1},{2,6},{6,2},{3,7},{7,3},{8,12},{12,8},{9,1... | collective-permute-start | bytes 331784 | tf_op jit(solution)/shard_map/ppermute | solution.py:282
  28.9 32.9 %all-to-all-start = ((bf16[4,48,1152]{2,1,0:T(8,128)(2,1)}), bf16[4,48,1152]{2,1,0:T(8,128)(2,1)S(1)}, u32[]{:S(2)}, u32[]{:S(2)}) async-start(bf16[4,48,1152]{2,1,0:T(8,128)(2,1)} %broadcast_in_dim.3), calls=%async_computation | async-start | bytes 884736 | tf_op jit(solution)/shard_map/all_to_all | solution.py:275
  39.8 12.6 %collective-permute-start.7 = (bf16[2,2,64,640]{3,2,1,0:T(8,128)(2,1)S(1)}, bf16[2,2,64,640]{3,2,1,0:T(8,128)(2,1)S(1)}, u32[]{:S(2)}, u32[]{:S(2)}) collective-permute-start(bf16[2,2,64,640]{3,2,1,0:T(8,128)(2,1)S(1)} %pad_maximum_fusion.refs_2_.refs_5_), channel_id=1, source_target_pairs={{0,8},{8,16},{16,24},{24,0},{1,9},{9,17},{17,25},{25,1},{2,10},{10... | collective-permute-start | bytes 983048 | tf_op jit(solution)/shard_map/ppermute | solution.py:270
  43.3 17.2 %collective-permute-start.6 = (bf16[2,2,64,640]{3,2,1,0:T(8,128)(2,1)S(1)}, bf16[2,2,64,640]{3,2,1,0:T(8,128)(2,1)S(1)}, u32[]{:S(2)}, u32[]{:S(2)}) collective-permute-start(bf16[2,2,64,640]{3,2,1,0:T(8,128)(2,1)S(1)} %pad_maximum_fusion.refs_2_.refs_5_), channel_id=1, source_target_pairs={{0,16},{8,24},{16,0},{24,8},{1,17},{9,25},{17,1},{25,9},{2,18},{10... | collective-permute-start | bytes 983048 | tf_op jit(solution)/shard_map/ppermute | solution.py:270
  48.1 13.8 %collective-permute-start.5 = (bf16[2,2,64,640]{3,2,1,0:T(8,128)(2,1)S(1)}, bf16[2,2,64,640]{3,2,1,0:T(8,128)(2,1)S(1)}, u32[]{:S(2)}, u32[]{:S(2)}) collective-permute-start(bf16[2,2,64,640]{3,2,1,0:T(8,128)(2,1)S(1)} %pad_maximum_fusion.refs_2_.refs_5_), channel_id=1, source_target_pairs={{0,24},{8,0},{16,8},{24,16},{1,25},{9,1},{17,9},{25,17},{2,26},{10... | collective-permute-start | bytes 983048 | tf_op jit(solution)/shard_map/ppermute | solution.py:270
  68.2 16.1 %all-to-all-start.1 = ((bf16[4,48,512]{2,1,0:T(8,128)(2,1)}), bf16[4,48,512]{2,1,0:T(8,128)(2,1)S(1)}, u32[]{:S(2)}, u32[]{:S(2)}) async-start(bf16[4,48,512]{2,1,0:T(8,128)(2,1)} %get-tuple-element.29), calls=%async_computation.1 | async-start | bytes 393216 | tf_op jit(solution)/shard_map/all_to_all | solution.py:291
  73.0 0.9 copy-start
  83.4 0.9 copy-start.1
  84.3 7.0 %collective-permute-start.9 = (bf16[4,2,64,640]{3,2,1,0:T(8,128)(2,1)}, bf16[4,2,64,640]{3,2,1,0:T(8,128)(2,1)S(1)}, u32[]{:S(2)}, u32[]{:S(2)}) collective-permute-start(bf16[4,2,64,640]{3,2,1,0:T(8,128)(2,1)} %copy-done.1), channel_id=1, source_target_pairs={{0,32},{32,0},{1,33},{33,1},{2,34},{34,2},{3,35},{35,3},{4,36},{36... | collective-permute-start | bytes 1966088 | tf_op jit(solution)/shard_map/ppermute | solution.py:294
  86.2 29.3 %all-to-all-start.2 = ((bf16[4,48,512]{2,1,0:T(8,128)(2,1)}), bf16[4,48,512]{2,1,0:T(8,128)(2,1)S(1)}, u32[]{:S(2)}, u32[]{:S(2)}) async-start(bf16[4,48,512]{2,1,0:T(8,128)(2,1)} %get-tuple-element.37), calls=%async_computation.2 | async-start | bytes 393216 | tf_op jit(solution)/shard_map/all_to_all | solution.py:295
  92.8 23.5 %collective-permute-start.10 = (bf16[2,64,640]{2,1,0:T(8,128)(2,1)S(1)}, bf16[2,64,640]{2,1,0:T(8,128)(2,1)S(1)}, u32[]{:S(2)}, u32[]{:S(2)}) collective-permute-start(bf16[2,64,640]{2,1,0:T(8,128)(2,1)S(1)} %get-tuple-element.42), channel_id=1, source_target_pairs={{0,8},{8,16},{16,24},{24,0},{1,9},{9,17},{17,25},{25,1},{2,10},{10... | collective-permute-start | bytes 491528 | tf_op jit(solution)/shard_map/ppermute | solution.py:270
  97.2 19.1 %collective-permute-start.11 = (bf16[2,64,640]{2,1,0:T(8,128)(2,1)S(1)}, bf16[2,64,640]{2,1,0:T(8,128)(2,1)S(1)}, u32[]{:S(2)}, u32[]{:S(2)}) collective-permute-start(bf16[2,64,640]{2,1,0:T(8,128)(2,1)S(1)} %get-tuple-element.43), channel_id=1, source_target_pairs={{0,16},{8,24},{16,0},{24,8},{1,17},{9,25},{17,1},{25,9},{2,18},{10... | collective-permute-start | bytes 491528 | tf_op jit(solution)/shard_map/ppermute | solution.py:270
  100.7 15.5 %collective-permute-start.12 = (bf16[2,64,640]{2,1,0:T(8,128)(2,1)S(1)}, bf16[2,64,640]{2,1,0:T(8,128)(2,1)S(1)}, u32[]{:S(2)}, u32[]{:S(2)}) collective-permute-start(bf16[2,64,640]{2,1,0:T(8,128)(2,1)S(1)} %get-tuple-element.44), channel_id=1, source_target_pairs={{0,24},{8,0},{16,8},{24,16},{1,25},{9,1},{17,9},{25,17},{2,26},{10... | collective-permute-start | bytes 491528 | tf_op jit(solution)/shard_map/ppermute | solution.py:270
  104.3 11.2 %collective-permute-start.8 = (bf16[48,512]{1,0:T(8,128)(2,1)S(1)}, bf16[48,512]{1,0:T(8,128)(2,1)S(1)}, u32[]{:S(2)}, u32[]{:S(2)}) collective-permute-start(bf16[48,512]{1,0:T(8,128)(2,1)S(1)} %total_of.1), channel_id=1, source_target_pairs={{0,4},{4,0},{1,5},{5,1},{2,6},{6,2},{3,7},{7,3},{8,12},{12,8},{9,1... | collective-permute-start | bytes 147464 | tf_op jit(solution)/shard_map/ppermute | solution.py:296

commit v4 on v3

v4 whole, which is shorter than its diff:
```python
import jax
import jax.numpy as jnp
from jax import lax
from jax.experimental import pallas as pl
from jax.experimental.pallas import tpu as pltpu
from jax.sharding import Mesh, PartitionSpec as P

DH = 128
HQ = 4
WIDTH = HQ * DH
SCALE = DH**-0.5
LOG2E = 1.4426950408889634
BF = jnp.bfloat16
F32 = jnp.float32
SWAP = [(0, 1), (1, 0)]
VMEM_GRADS = 40 << 20
SPARE = 10
MEDIUM = pltpu.CompilerParams(vmem_limit_bytes=12 << 20)
SMALL = pltpu.CompilerParams(vmem_limit_bytes=4 << 20)


def half_swap(value, core):
    rolled = jnp.concatenate([value[:, DH // 2 :], value[:, : DH // 2]], 1)
    return jnp.where(core == 0, value, rolled)


def prep_kernel(core_ref, q_ref, g_ref, o_ref, lse_ref, k_ref, v_ref, x_ref, copies_ref, kv_ref):
    core = core_ref[0]
    rows = q_ref.shape[0]
    lane = lax.broadcasted_iota(jnp.int32, (rows, DH), 1)
    lse = jnp.transpose(lse_ref[...]) * (-1.0 / SCALE)
    stats = jnp.zeros((rows, DH), F32)
    for h in range(HQ):
        at = pl.ds(h * DH, DH)
        q = q_ref[:, at].astype(F32)
        g = g_ref[:, at].astype(F32)
        dterm = jnp.sum(g * o_ref[:, at].astype(F32), axis=1, keepdims=True)
        mine = (lane & (HQ - 1)) == h
        stats = jnp.where(mine & (lane < 3 * HQ), lse[:, h : h + 1], stats)
        stats = jnp.where(mine & (lane >= 3 * HQ) & (lane < 6 * HQ), -dterm, stats)
        x_ref[:, at] = half_swap(q, core).astype(BF)
        x_ref[:, pl.ds(WIDTH + h * DH, DH)] = half_swap(g, core).astype(BF)
    high = stats.astype(BF).astype(F32)
    rest = stats - high
    middle = rest.astype(BF).astype(F32)
    group = lax.shift_right_logical(lane, 2)
    first = (group == 0) | (group == 3)
    second = (group == 1) | (group == 4)
    stats = jnp.where(first, high, jnp.where(second, middle, rest - middle))
    x_ref[:, pl.ds(2 * WIDTH, DH)] = stats.astype(BF)
    for b in range(copies_ref.shape[0]):
        copies_ref[b] = x_ref[...]
    kv_ref[0] = k_ref[...]
    kv_ref[1] = v_ref[...]


def prep(core, queries, out_grad, outputs, lse_t, keys, values):
    rows = queries.shape[0]
    return pl.pallas_call(
        prep_kernel,
        in_specs=[pl.BlockSpec(memory_space=pltpu.SMEM)] + [pl.BlockSpec(memory_space=pltpu.VMEM)] * 6,
        out_shape=[
            jax.ShapeDtypeStruct((rows, 2 * WIDTH + DH), BF),
            jax.ShapeDtypeStruct((lax.axis_size("zi"), rows, 2 * WIDTH + DH), BF),
            jax.ShapeDtypeStruct((2,) + keys.shape, BF),
        ],
        name="prep",
    )(core, queries, out_grad, outputs, lse_t, keys, values)


def grads_kernel(last, *refs):
    if last:
        quad_ref, x_ref, own_ref, other_ref, near_ref, before_ref, *refs = refs
        dq_ref, keep_ref, send_ref, q_s, g_s, acc, held, sems = refs
    else:
        x_ref, own_ref, other_ref, dq_ref, after_ref, q_s, g_s, acc, held, sems = refs
    blocks, rows, _ = x_ref.shape
    chunks, _, half, cols = own_ref.shape
    copies = []
    for j in range(chunks):
        ends = (before_ref.at[j], held.at[j]) if last else (held.at[j], after_ref.at[j])
        copies.append(pltpu.make_async_copy(*ends, sems.at[j]))
        if last:
            copies[j].start()
    lane = lax.broadcasted_iota(jnp.int32, (rows, DH), 1)
    for b in range(blocks):
        stats = x_ref[b, :, 2 * WIDTH : 2 * WIDTH + DH].astype(F32)
        for h in range(HQ):
            to = pl.ds((h * blocks + b) * rows, rows)
            mine = jnp.where((lane & (HQ - 1)) == h, stats, 0.0).astype(BF)
            q_s[to, :DH] = x_ref[b, :, h * DH : (h + 1) * DH]
            g_s[to, :DH] = x_ref[b, :, WIDTH + h * DH : WIDTH + (h + 1) * DH]
            q_s[to, DH:] = mine
            g_s[to, DH:] = mine

    row = lax.broadcasted_iota(jnp.int32, (DH, cols), 0)
    k_ones = jnp.where(row < 3 * HQ, 1.0, 0.0).astype(BF)
    v_ones = jnp.where((row >= 3 * HQ) & (row < 6 * HQ), 1.0, 0.0).astype(BF)
    over_rows = (((0,), (0,)), ((), ()))
    for j in range(chunks):
        k = jnp.concatenate([own_ref[j, 0], other_ref[j, 0]], 0)
        v = jnp.concatenate([own_ref[j, 1], other_ref[j, 1]], 0)
        s = jnp.dot(q_s[...], jnp.concatenate([k, k_ones], 0), preferred_element_type=F32)
        p = jnp.exp2(s * (SCALE * LOG2E))
        dp = jnp.dot(g_s[...], jnp.concatenate([v, v_ones], 0), preferred_element_type=F32)
        ds = (p * dp).astype(BF)
        pb = p.astype(BF)
        dv = lax.dot_general(g_s[:, :DH], pb, over_rows, preferred_element_type=F32)
        dk = lax.dot_general(q_s[:, :DH], ds, over_rows, preferred_element_type=F32) * SCALE
        dq = lax.dot_general(ds, k, (((1,), (1,)), ((), ())), preferred_element_type=F32) * SCALE
        if last:
            copies[j].wait()
            for i, part in enumerate((dk, dv)):
                total = part + held[j, i]
                keep_ref[j, i] = total[:half]
                send_ref[j, i] = total[half:].astype(BF)
        else:
            held[j, 0] = dk
            held[j, 1] = dv
            copies[j].start()
        if j == 0:
            acc[...] = dq
        else:
            acc[...] += dq

    out_ref = dq_ref
    if last:
        near = quad_ref[0]
        dq_ref[near] = near_ref[...]
        out_ref = dq_ref.at[1 - near]
    for b in range(blocks):
        for h in range(HQ):
            at = pl.ds((h * blocks + b) * rows, rows)
            out_ref[b, :, h * DH : (h + 1) * DH] = acc[at, :].astype(BF)
    if not last:
        for copy in copies:
            copy.wait()


def grads(x, own, other, quad=None, before=()):
    blocks, rows, _ = x.shape
    chunks, _, half, cols = own.shape
    total = blocks * rows * HQ
    last = quad is not None
    work = total * chunks * cols
    small = pl.BlockSpec(memory_space=pltpu.SMEM)
    whole = pl.BlockSpec(memory_space=pltpu.VMEM)
    far = pl.BlockSpec(memory_space=pltpu.HBM)
    sums = (chunks, 2, 2 * half, cols)
    halves = (chunks, 2, half, cols)
    if last:
        operands = (quad, x, own, other, *before)
        in_specs = [small] + [whole] * 4 + [far]
        out_shape = [
            jax.ShapeDtypeStruct((2, blocks, rows, WIDTH), BF),
            jax.ShapeDtypeStruct(halves, F32),
            jax.ShapeDtypeStruct(halves, BF),
        ]
        out_specs = [whole] * 3
    else:
        operands = (x, own, other)
        in_specs = [whole] * 3
        out_shape = [
            jax.ShapeDtypeStruct((blocks, rows, WIDTH), BF),
            jax.ShapeDtypeStruct((SPARE * chunks,) + sums[1:], F32),
        ]
        out_specs = [whole, far]
    return pl.pallas_call(
        lambda *refs: grads_kernel(last, *refs),
        in_specs=in_specs,
        out_specs=out_specs,
        out_shape=out_shape,
        scratch_shapes=[
            pltpu.VMEM((total, 2 * DH), BF),
            pltpu.VMEM((total, 2 * DH), BF),
            pltpu.VMEM((total, DH), F32),
            pltpu.VMEM(sums, F32),
            pltpu.SemaphoreType.DMA((chunks,)),
        ],
        compiler_params=pltpu.CompilerParams(vmem_limit_bytes=VMEM_GRADS),
        cost_estimate=pl.CostEstimate(flops=10 * work * DH, bytes_accessed=4 << 20, transcendentals=work),
        name="grads",
    )(*operands)


def query_kernel(core_ref, parts_ref, out_ref):
    core = core_ref[0]
    for h in range(HQ):
        at = pl.ds(h * DH, DH)
        total = parts_ref[0, :, at].astype(F32)
        for b in range(1, parts_ref.shape[0]):
            total = total + parts_ref[b, :, at].astype(F32)
        out_ref[:, at] = half_swap(total, core).astype(BF)


def query_total(core, parts):
    return pl.pallas_call(
        query_kernel,
        in_specs=[pl.BlockSpec(memory_space=pltpu.SMEM), pl.BlockSpec(memory_space=pltpu.VMEM)],
        out_shape=jax.ShapeDtypeStruct(parts.shape[1:], BF),
        compiler_params=SMALL,
        name="query_total",
    )(core, parts)


def both_kernel(y_ref, keep_ref, got_ref, *out_refs):
    count = len(out_refs)
    for r, out_ref in enumerate(out_refs):
        at = lax.rem(y_ref[0] + r, count)
        out_ref[...] = (keep_ref[at] + got_ref[at].astype(F32)).astype(out_ref.dtype)


def both_cores(y, keep, got):
    one = jax.ShapeDtypeStruct(keep.shape[1:], BF)
    return pl.pallas_call(
        both_kernel,
        in_specs=[pl.BlockSpec(memory_space=pltpu.SMEM)] + [pl.BlockSpec(memory_space=pltpu.VMEM)] * 2,
        out_shape=[one] * keep.shape[0],
        compiler_params=MEDIUM,
        name="both_cores",
    )(y, keep, got)


def visual_kernel(*refs):
    parts = refs[:-2]
    for i, out_ref in enumerate(refs[-2:]):
        total = parts[0][i].astype(F32)
        for part in parts[1:]:
            total = total + part[i].astype(F32)
        out_ref[...] = total.astype(BF)


def visual_total(parts):
    one = jax.ShapeDtypeStruct(parts[0].shape[1:], BF)
    return pl.pallas_call(
        visual_kernel, out_shape=[one, one], compiler_params=SMALL, name="visual_total"
    )(*parts)


def along(axis, value, steps):
    count = lax.axis_size(axis)
    return lax.ppermute(value, axis, [(i, (i + steps) % count) for i in range(count)])


def index(axis):
    return lax.axis_index(axis).astype(jnp.int32).reshape(1)


def per_device(queries, keys, values, outputs, out_grad, logsumexp):
    core = index("core")
    x, copies, kv = prep(core, queries, out_grad, outputs, logsumexp.T, keys, values)

    x_near = lax.all_to_all(copies, "zi", 0, 0)
    far = lax.ppermute(x, "zq", SWAP)

    own = lax.all_gather(kv, "y")
    far, own = lax.optimization_barrier((far, own))
    other = lax.ppermute(own, "core", SWAP)
    x_far = lax.all_to_all(jnp.broadcast_to(far, copies.shape), "zi", 0, 0)

    before = grads(x_near, own, other)
    dq, keep, send = grads(x_far, own, other, index("zq"), before)
    dq = dq.reshape((-1,) + dq.shape[2:])
    query_grad = query_total(core, lax.all_to_all(dq, ("zq", "zi"), 0, 0))

    both = both_cores(index("y"), keep, lax.ppermute(send, "core", SWAP))
    parts = [both[0]] + [along("y", both[r], r) for r in range(1, len(both))]
    key_grad, value_grad = visual_total(parts)
    return query_grad, key_grad, value_grad


def solution(mesh):
    devices = mesh.devices.reshape(2, 4, 2, 4, 2, 4)
    inner = Mesh(devices, ("zh", "x", "core", "y", "zq", "zi"))
    head = ("zh", "x", "core")
    seq = ("y", "zq", "zi")
    text = P(seq, head)
    visual = P(head, seq)
    return jax.shard_map(
        per_device,
        mesh=inner,
        in_specs=(text, visual, visual, text, text, text),
        out_specs=(text, visual, visual),
        check_vma=False,
    )
```

time: 118 us -> 86.8 us (0.74)
  starting transfers between devices: 76 us -> 41.5 us
  blocking collectives: 0 us -> 13.8 us
  waiting for transfers between devices: 15.9 us -> 11.1 us
  Pallas kernels: 20.8 us -> 17.5 us
    ppermute x9 -> x3, starting transfers between devices: 34.1 us -> 11.6 us  [along(): lax.ppermute(value, axis, [(i, (i + steps) % count) for i in range(count)])]
    all_gather x0 -> x1, blocking collectives: none -> 13.8 us  [per_device(): own = lax.all_gather(kv, 'y')]
    ppermute x3 -> x2, starting transfers between devices: 12 us -> 3.82 us  [the longest x1 1.91 us: per_device(): other = lax.ppermute(own, 'core', SWAP)]
    ppermute x9 -> x3, waiting for transfers between devices: 10.5 us -> 4.3 us  [along(): lax.ppermute(value, axis, [(i, (i + steps) % count) for i in range(count)])]
    all_to_all x3, starting transfers between devices: 20.8 us -> 17 us  [the longest x1 6.05 us: per_device(): query_grad = query_total(core, lax.all_to_all(dq, ('zq', 'zi'), 0, 0))]
    pallas_call x4 -> x3, Pallas kernels: 17.3 us -> 13.8 us  [the longest x2 13.7 us: grads(): pl.pallas_call(lambda *refs: grads_kernel(last, *refs), in_specs=in_specs...]
    all_to_all x3, waiting for transfers between devices: 0.01 us -> 2.47 us  [the longest x1 1.67 us: per_device(): query_grad = query_total(core, lax.all_to_all(dq, ('zq', 'zi'), 0, 0))]
    ppermute x1, waiting for transfers between devices: 2.39 us -> 0.01 us  [per_device(): far = lax.ppermute(x, 'zq', SWAP)]
  transfers between devices with their start and end apart: 16 -> 9, of which waited for: 5 -> 6; matrix products, arithmetic and copies ran while one was open for 1% -> 0% of each run, Pallas kernels for 10% -> 8%
where the time goes in v4:
time: 86.8 us; the launch traced here: 86.3 us
  starting transfers between devices  41.5 us (48%)
  Pallas kernels  17.5 us (20%)
  blocking collectives  13.8 us (16%)
  waiting for transfers between devices  11.1 us (13%)
  local copies, waits for them, and re-layouts  1.65 us (2%)
    all_gather x1, blocking collectives, per_device(): own = lax.all_gather(kv, 'y')  13.8 us
    pallas_call x2, Pallas kernels, grads(): pl.pallas_call(lambda *refs: grads_kernel(last, *refs), in_specs=in_specs...  13.7 us
    ppermute x3, starting transfers between devices, along(): lax.ppermute(value, axis, [(i, (i + steps) % count) for i in range(count)])  11.6 us
    ppermute x1, starting transfers between devices, per_device(): far = lax.ppermute(x, 'zq', SWAP)  9.08 us
    all_to_all x1, starting transfers between devices, per_device(): query_grad = query_total(core, lax.all_to_all(dq, ('zq', 'zi'), 0, 0))  6.05 us
    all_to_all x1, starting transfers between devices, per_device(): x_near = lax.all_to_all(copies, 'zi', 0, 0)  5.89 us
    all_to_all x1, starting transfers between devices, per_device(): x_far = lax.all_to_all(jnp.broadcast_to(far, copies.shape), 'zi', 0, 0)  5.06 us
    ppermute x3, waiting for transfers between devices, along(): lax.ppermute(value, axis, [(i, (i + steps) % count) for i in range(count)])  4.3 us
  transfers between devices with their start and end apart: 9, of which 6 were waited for; matrix products, arithmetic and copies ran while one was open for 0% of the time, Pallas kernels for 8%

profile of v4, /device:TPU:6, one launch (start us, length us, event | category | flops | bytes accessed | tf_op | source)
XLA Modules:
  0.0 86.3 jit_solution(414408483474024935)
XLA Ops:
  0.6 2.2 %prep.1 = (bf16[48,1152]{1,0:T(8,128)(2,1)}, bf16[4,48,1152]{2,1,0:T(8,128)(2,1)}, bf16[2,64,640]{2,1,0:T(8,128)(2,1)}) custom-call(s32[1]{0:T(128)} %bitcast.core_ref, bf16[48,512]{1,0:T(8,128)(2,1)} %q_ref.1, bf16[48,512]{1,0:T(8,128)(2,1)} %g_ref.1, bf16[48,512]{1,0:T(8,128)(2,1)} %o_ref.1, f32[4,48]{1,0:T(4,128)} %bitcast.9, bf16[64,640]{1,0:T(8,128)(2,1)} %k_ref.1, ...), custom_call_target="tpu_custom_call" | custom-call | tf_op jit(solution)/shard_map/prep/pallas_call | solution.py:59
  2.9 5.9 %all-to-all-start.1 = ((bf16[4,48,1152]{2,1,0:T(8,128)(2,1)}), bf16[4,48,1152]{2,1,0:T(8,128)(2,1)S(1)}, u32[]{:S(2)}, u32[]{:S(2)}) async-start(bf16[4,48,1152]{2,1,0:T(8,128)(2,1)} %get-tuple-element.23), calls=%async_computation.1 | async-start | bytes 884736 | tf_op jit(solution)/shard_map/all_to_all | solution.py:253
  8.8 9.1 %collective-permute-start = (bf16[48,1152]{1,0:T(8,128)(2,1)}, bf16[48,1152]{1,0:T(8,128)(2,1)S(1)}, u32[]{:S(2)}, u32[]{:S(2)}) collective-permute-start(bf16[48,1152]{1,0:T(8,128)(2,1)} %get-tuple-element.19), channel_id=1, source_target_pairs={{0,4},{4,0},{1,5},{5,1},{2,6},{6,2},{3,7},{7,3},{8,12},{12,8},{9,1... | collective-permute-start | bytes 331784 | tf_op jit(solution)/shard_map/ppermute | solution.py:254
  17.9 13.8 %all-gather = bf16[8,64,640]{2,1,0:T(8,128)(2,1)S(1)} all-gather(bf16[2,64,640]{2,1,0:T(8,128)(2,1)} %get-tuple-element.20), channel_id=2, replica_groups=mesh['zh'=2,'x'=4,'core'=2,'y'=4,'zq'=2,'zi'=4] {'y'}, dimensions={0}, use_global_device_ids=true | all-gather | bytes 819200 | tf_op jit(solution)/shard_map/all_gather | solution.py:256
  31.7 0.0 collective-permute-done
  31.7 0.0 all-to-all-done.1.refs_0_
  31.7 0.8 broadcast_in_dim.3
  32.5 5.1 %all-to-all-start = ((bf16[4,48,1152]{2,1,0:T(8,128)(2,1)}), bf16[4,48,1152]{2,1,0:T(8,128)(2,1)S(1)}, u32[]{:S(2)}, u32[]{:S(2)}) async-start(bf16[4,48,1152]{2,1,0:T(8,128)(2,1)} %broadcast_in_dim.3), calls=%async_computation | async-start | bytes 884736 | tf_op jit(solution)/shard_map/all_to_all | solution.py:259
  37.6 1.9 %collective-permute-start.1 = (bf16[4,2,64,640]{3,2,1,0:T(8,128)(2,1)S(1)}, bf16[4,2,64,640]{3,2,1,0:T(8,128)(2,1)S(1)}, u32[]{:S(2)}, u32[]{:S(2)}) collective-permute-start(bf16[4,2,64,640]{3,2,1,0:T(8,128)(2,1)S(1)} %bitcast.6), channel_id=1, source_target_pairs={{0,32},{32,0},{1,33},{33,1},{2,34},{34,2},{3,35},{35,3},{4,36},{36... | collective-permute-start | bytes 1966088 | tf_op jit(solution)/shard_map/ppermute | solution.py:258
  39.5 2.1 %collective-permute-done.1.refs_2_.refs_3_ = bf16[4,2,64,640]{3,2,1,0:T(8,128)(2,1)S(1)} collective-permute-done((bf16[4,2,64,640]{3,2,1,0:T(8,128)(2,1)S(1)}, bf16[4,2,64,640]{3,2,1,0:T(8,128)(2,1)S(1)}, u32[]{:S(2)}, u32[]{:S(2)}) %collective-permute-start.1) | collective-permute-done | bytes 655392 | tf_op jit(solution)/shard_map/ppermute | solution.py:258
  41.5 5.7 %grads.2 = (bf16[4,48,512]{2,1,0:T(8,128)(2,1)S(1)}, f32[40,2,128,640]{3,2,1,0:T(8,128)}) custom-call(bf16[4,48,1152]{2,1,0:T(8,128)(2,1)S(1)} %all-to-all-done.1.refs_0_, bf16[4,2,64,640]{3,2,1,0:T(8,128)(2,1)S(1)} %bitcast.7, bf16[4,2,64,640]{3,2,1,0:T(8,128)(2,1)S(1)} %collective-permute-done.1.refs_2_.refs_3_), custom_call_target="tpu_custom_call" | custom-call | flops 2516582400 | bytes 4194304 | tf_op jit(solution)/shard_map/grads/pallas_call | solution.py:168
  47.3 0.8 all-to-all-done.refs_1_
  48.1 8.0 %grads.3 = (bf16[2,4,48,512]{3,2,1,0:T(8,128)(2,1)}, f32[4,2,64,640]{3,2,1,0:T(8,128)S(1)}, bf16[4,2,64,640]{3,2,1,0:T(8,128)(2,1)S(1)}) custom-call(s32[1]{0:T(128)} %bitcast.1.refs_0_, bf16[4,48,1152]{2,1,0:T(8,128)(2,1)S(1)} %all-to-all-done.refs_1_, bf16[4,2,64,640]{3,2,1,0:T(8,128)(2,1)S(1)} %bitcast.8, ...), custom_call_target="tpu_custom_call" | custom-call | flops 2516582400 | bytes 4194304 | tf_op jit(solution)/shard_map/grads/pallas_call | solution.py:168
  56.1 0.0 copy-start
  56.1 0.8 copy-done
  56.9 6.1 %all-to-all-start.2 = ((bf16[8,48,512]{2,1,0:T(8,128)(2,1)}), bf16[8,48,512]{2,1,0:T(8,128)(2,1)S(1)}, u32[]{:S(2)}, u32[]{:S(2)}) async-start(bf16[8,48,512]{2,1,0:T(8,128)(2,1)} %bitcast.4), calls=%async_computation.2 | async-start | bytes 786432 | tf_op jit(solution)/shard_map/all_to_all | solution.py:264
  63.0 1.9 %collective-permute-start.2 = (bf16[4,2,64,640]{3,2,1,0:T(8,128)(2,1)}, bf16[4,2,64,640]{3,2,1,0:T(8,128)(2,1)S(1)}, u32[]{:S(2)}, u32[]{:S(2)}) collective-permute-start(bf16[4,2,64,640]{3,2,1,0:T(8,128)(2,1)} %copy-done), channel_id=1, source_target_pairs={{0,32},{32,0},{1,33},{33,1},{2,34},{34,2},{3,35},{35,3},{4,36},{36... | collective-permute-start | bytes 1966088 | tf_op jit(solution)/shard_map/ppermute | solution.py:266
  64.9 2.3 %collective-permute-done.2.got_ref = bf16[4,2,64,640]{3,2,1,0:T(8,128)(2,1)S(1)} collective-permute-done((bf16[4,2,64,640]{3,2,1,0:T(8,128)(2,1)}, bf16[4,2,64,640]{3,2,1,0:T(8,128)(2,1)S(1)}, u32[]{:S(2)}, u32[]{:S(2)}) %collective-permute-start.2) | collective-permute-done | bytes 655392 | tf_op jit(solution)/shard_map/ppermute | solution.py:266
  67.2 0.1 both_cores.1
  67.3 3.5 %collective-permute-start.3 = (bf16[2,64,640]{2,1,0:T(8,128)(2,1)S(1)}, bf16[2,64,640]{2,1,0:T(8,128)(2,1)S(1)}, u32[]{:S(2)}, u32[]{:S(2)}) collective-permute-start(bf16[2,64,640]{2,1,0:T(8,128)(2,1)S(1)} %get-tuple-element.30), channel_id=1, source_target_pairs={{0,8},{8,16},{16,24},{24,0},{1,9},{9,17},{17,25},{25,1},{2,10},{10... | collective-permute-start | bytes 491528 | tf_op jit(solution)/shard_map/ppermute | solution.py:242
  70.8 4.8 %collective-permute-start.4 = (bf16[2,64,640]{2,1,0:T(8,128)(2,1)S(1)}, bf16[2,64,640]{2,1,0:T(8,128)(2,1)S(1)}, u32[]{:S(2)}, u32[]{:S(2)}) collective-permute-start(bf16[2,64,640]{2,1,0:T(8,128)(2,1)S(1)} %get-tuple-element.31), channel_id=1, source_target_pairs={{0,16},{8,24},{16,0},{24,8},{1,17},{9,25},{17,1},{25,9},{2,18},{10... | collective-permute-start | bytes 491528 | tf_op jit(solution)/shard_map/ppermute | solution.py:242
  75.6 3.3 %collective-permute-start.5 = (bf16[2,64,640]{2,1,0:T(8,128)(2,1)S(1)}, bf16[2,64,640]{2,1,0:T(8,128)(2,1)S(1)}, u32[]{:S(2)}, u32[]{:S(2)}) collective-permute-start(bf16[2,64,640]{2,1,0:T(8,128)(2,1)S(1)} %get-tuple-element.32), channel_id=1, source_target_pairs={{0,24},{8,0},{16,8},{24,16},{1,25},{9,1},{17,9},{25,17},{2,26},{10... | collective-permute-start | bytes 491528 | tf_op jit(solution)/shard_map/ppermute | solution.py:242
  78.9 0.0 collective-permute-done.3.refs_1_
  78.9 2.5 %collective-permute-done.4.refs_2_ = bf16[2,64,640]{2,1,0:T(8,128)(2,1)S(1)} collective-permute-done((bf16[2,64,640]{2,1,0:T(8,128)(2,1)S(1)}, bf16[2,64,640]{2,1,0:T(8,128)(2,1)S(1)}, u32[]{:S(2)}, u32[]{:S(2)}) %collective-permute-start.4) | collective-permute-done | bytes 163872 | tf_op jit(solution)/shard_map/ppermute | solution.py:242
  81.4 1.8 %collective-permute-done.5.refs_3_ = bf16[2,64,640]{2,1,0:T(8,128)(2,1)S(1)} collective-permute-done((bf16[2,64,640]{2,1,0:T(8,128)(2,1)S(1)}, bf16[2,64,640]{2,1,0:T(8,128)(2,1)S(1)}, u32[]{:S(2)}, u32[]{:S(2)}) %collective-permute-start.5) | collective-permute-done | bytes 163872 | tf_op jit(solution)/shard_map/ppermute | solution.py:242
  83.2 0.7 visual_total.1
  83.9 1.7 %all-to-all-done.2.parts_ref = bf16[8,48,512]{2,1,0:T(8,128)(2,1)S(1)} async-done(((bf16[8,48,512]{2,1,0:T(8,128)(2,1)}), bf16[8,48,512]{2,1,0:T(8,128)(2,1)S(1)}, u32[]{:S(2)}, u32[]{:S(2)}) %all-to-all-start.2) | async-done | bytes 393248 | tf_op jit(solution)/shard_map/all_to_all | solution.py:264
  85.6 0.7 query_total.1
Async XLA Ops:
  2.9 28.8 %all-to-all-start.1 = ((bf16[4,48,1152]{2,1,0:T(8,128)(2,1)}), bf16[4,48,1152]{2,1,0:T(8,128)(2,1)S(1)}, u32[]{:S(2)}, u32[]{:S(2)}) async-start(bf16[4,48,1152]{2,1,0:T(8,128)(2,1)} %get-tuple-element.23), calls=%async_computation.1 | async-start | bytes 884736 | tf_op jit(solution)/shard_map/all_to_all | solution.py:253
  8.8 22.9 %collective-permute-start = (bf16[48,1152]{1,0:T(8,128)(2,1)}, bf16[48,1152]{1,0:T(8,128)(2,1)S(1)}, u32[]{:S(2)}, u32[]{:S(2)}) collective-permute-start(bf16[48,1152]{1,0:T(8,128)(2,1)} %get-tuple-element.19), channel_id=1, source_target_pairs={{0,4},{4,0},{1,5},{5,1},{2,6},{6,2},{3,7},{7,3},{8,12},{12,8},{9,1... | collective-permute-start | bytes 331784 | tf_op jit(solution)/shard_map/ppermute | solution.py:254
  32.5 15.6 %all-to-all-start = ((bf16[4,48,1152]{2,1,0:T(8,128)(2,1)}), bf16[4,48,1152]{2,1,0:T(8,128)(2,1)S(1)}, u32[]{:S(2)}, u32[]{:S(2)}) async-start(bf16[4,48,1152]{2,1,0:T(8,128)(2,1)} %broadcast_in_dim.3), calls=%async_computation | async-start | bytes 884736 | tf_op jit(solution)/shard_map/all_to_all | solution.py:259
  37.6 4.0 %collective-permute-start.1 = (bf16[4,2,64,640]{3,2,1,0:T(8,128)(2,1)S(1)}, bf16[4,2,64,640]{3,2,1,0:T(8,128)(2,1)S(1)}, u32[]{:S(2)}, u32[]{:S(2)}) collective-permute-start(bf16[4,2,64,640]{3,2,1,0:T(8,128)(2,1)S(1)} %bitcast.6), channel_id=1, source_target_pairs={{0,32},{32,0},{1,33},{33,1},{2,34},{34,2},{3,35},{35,3},{4,36},{36... | collective-permute-start | bytes 1966088 | tf_op jit(solution)/shard_map/ppermute | solution.py:258
  56.1 0.8 copy-start
  56.9 28.6 %all-to-all-start.2 = ((bf16[8,48,512]{2,1,0:T(8,128)(2,1)}), bf16[8,48,512]{2,1,0:T(8,128)(2,1)S(1)}, u32[]{:S(2)}, u32[]{:S(2)}) async-start(bf16[8,48,512]{2,1,0:T(8,128)(2,1)} %bitcast.4), calls=%async_computation.2 | async-start | bytes 786432 | tf_op jit(solution)/shard_map/all_to_all | solution.py:264
  63.0 4.2 %collective-permute-start.2 = (bf16[4,2,64,640]{3,2,1,0:T(8,128)(2,1)}, bf16[4,2,64,640]{3,2,1,0:T(8,128)(2,1)S(1)}, u32[]{:S(2)}, u32[]{:S(2)}) collective-permute-start(bf16[4,2,64,640]{3,2,1,0:T(8,128)(2,1)} %copy-done), channel_id=1, source_target_pairs={{0,32},{32,0},{1,33},{33,1},{2,34},{34,2},{3,35},{35,3},{4,36},{36... | collective-permute-start | bytes 1966088 | tf_op jit(solution)/shard_map/ppermute | solution.py:266
  67.3 11.6 %collective-permute-start.3 = (bf16[2,64,640]{2,1,0:T(8,128)(2,1)S(1)}, bf16[2,64,640]{2,1,0:T(8,128)(2,1)S(1)}, u32[]{:S(2)}, u32[]{:S(2)}) collective-permute-start(bf16[2,64,640]{2,1,0:T(8,128)(2,1)S(1)} %get-tuple-element.30), channel_id=1, source_target_pairs={{0,8},{8,16},{16,24},{24,0},{1,9},{9,17},{17,25},{25,1},{2,10},{10... | collective-permute-start | bytes 491528 | tf_op jit(solution)/shard_map/ppermute | solution.py:242
  70.8 10.6 %collective-permute-start.4 = (bf16[2,64,640]{2,1,0:T(8,128)(2,1)S(1)}, bf16[2,64,640]{2,1,0:T(8,128)(2,1)S(1)}, u32[]{:S(2)}, u32[]{:S(2)}) collective-permute-start(bf16[2,64,640]{2,1,0:T(8,128)(2,1)S(1)} %get-tuple-element.31), channel_id=1, source_target_pairs={{0,16},{8,24},{16,0},{24,8},{1,17},{9,25},{17,1},{25,9},{2,18},{10... | collective-permute-start | bytes 491528 | tf_op jit(solution)/shard_map/ppermute | solution.py:242
  75.6 7.6 %collective-permute-start.5 = (bf16[2,64,640]{2,1,0:T(8,128)(2,1)S(1)}, bf16[2,64,640]{2,1,0:T(8,128)(2,1)S(1)}, u32[]{:S(2)}, u32[]{:S(2)}) collective-permute-start(bf16[2,64,640]{2,1,0:T(8,128)(2,1)S(1)} %get-tuple-element.32), channel_id=1, source_target_pairs={{0,24},{8,0},{16,8},{24,16},{1,25},{9,1},{17,9},{25,17},{2,26},{10... | collective-permute-start | bytes 491528 | tf_op jit(solution)/shard_map/ppermute | solution.py:242

commit v5 on v4

--- a/solution.py
+++ b/solution.py
@@ -8,6 +8,7 @@
 DH = 128
 HQ = 4
 WIDTH = HQ * DH
+STATS = 4 * HQ
 SCALE = DH**-0.5
 LOG2E = 1.4426950408889634
 BF = jnp.bfloat16
@@ -24,32 +25,29 @@
     return jnp.where(core == 0, value, rolled)
 
 
-def prep_kernel(core_ref, q_ref, g_ref, o_ref, lse_ref, k_ref, v_ref, x_ref, copies_ref, kv_ref):
+def prep_kernel(core_ref, q_ref, g_ref, o_ref, lse_ref, k_ref, v_ref, copies_ref, kv_ref):
     core = core_ref[0]
     rows = q_ref.shape[0]
     lane = lax.broadcasted_iota(jnp.int32, (rows, DH), 1)
     lse = jnp.transpose(lse_ref[...]) * (-1.0 / SCALE)
     stats = jnp.zeros((rows, DH), F32)
+    block = copies_ref.at[0]
     for h in range(HQ):
         at = pl.ds(h * DH, DH)
         q = q_ref[:, at].astype(F32)
         g = g_ref[:, at].astype(F32)
         dterm = jnp.sum(g * o_ref[:, at].astype(F32), axis=1, keepdims=True)
         mine = (lane & (HQ - 1)) == h
-        stats = jnp.where(mine & (lane < 3 * HQ), lse[:, h : h + 1], stats)
-        stats = jnp.where(mine & (lane >= 3 * HQ) & (lane < 6 * HQ), -dterm, stats)
-        x_ref[:, at] = half_swap(q, core).astype(BF)
-        x_ref[:, pl.ds(WIDTH + h * DH, DH)] = half_swap(g, core).astype(BF)
+        stats = jnp.where(mine & (lane < 2 * HQ), lse[:, h : h + 1], stats)
+        stats = jnp.where(mine & (lane >= 2 * HQ) & (lane < STATS), -dterm, stats)
+        block[h * rows : (h + 1) * rows, :] = half_swap(q, core).astype(BF)
+        block[(HQ + h) * rows : (HQ + h + 1) * rows, :] = half_swap(g, core).astype(BF)
     high = stats.astype(BF).astype(F32)
-    rest = stats - high
-    middle = rest.astype(BF).astype(F32)
-    group = lax.shift_right_logical(lane, 2)
-    first = (group == 0) | (group == 3)
-    second = (group == 1) | (group == 4)
-    stats = jnp.where(first, high, jnp.where(second, middle, rest - middle))
-    x_ref[:, pl.ds(2 * WIDTH, DH)] = stats.astype(BF)
-    for b in range(copies_ref.shape[0]):
-        copies_ref[b] = x_ref[...]
+    stats = jnp.where((lane & HQ) == 0, high, stats - high)
+    stats = jnp.concatenate([stats, jnp.zeros((DH - rows, DH), F32)], 0)
+    block[2 * HQ * rows :, :] = jnp.transpose(stats)[:STATS].astype(BF)
+    for b in range(1, copies_ref.shape[0]):
+        copies_ref[b] = copies_ref[0]
     kv_ref[0] = k_ref[...]
     kv_ref[1] = v_ref[...]
 
@@ -60,8 +58,7 @@
         prep_kernel,
         in_specs=[pl.BlockSpec(memory_space=pltpu.SMEM)] + [pl.BlockSpec(memory_space=pltpu.VMEM)] * 6,
         out_shape=[
-            jax.ShapeDtypeStruct((rows, 2 * WIDTH + DH), BF),
-            jax.ShapeDtypeStruct((lax.axis_size("zi"), rows, 2 * WIDTH + DH), BF),
+            jax.ShapeDtypeStruct((lax.axis_size("z4"), 2 * HQ * rows + STATS, DH), BF),
             jax.ShapeDtypeStruct((2,) + keys.shape, BF),
         ],
         name="prep",
@@ -70,11 +67,12 @@
 
 def grads_kernel(last, *refs):
     if last:
-        quad_ref, x_ref, own_ref, other_ref, near_ref, before_ref, *refs = refs
+        side_ref, x_ref, own_ref, other_ref, near_ref, before_ref, *refs = refs
         dq_ref, keep_ref, send_ref, q_s, g_s, acc, held, sems = refs
     else:
         x_ref, own_ref, other_ref, dq_ref, after_ref, q_s, g_s, acc, held, sems = refs
-    blocks, rows, _ = x_ref.shape
+    blocks = x_ref.shape[0]
+    rows = (x_ref.shape[1] - STATS) // (2 * HQ)
     chunks, _, half, cols = own_ref.shape
     copies = []
     for j in range(chunks):
@@ -84,18 +82,20 @@
             copies[j].start()
     lane = lax.broadcasted_iota(jnp.int32, (rows, DH), 1)
     for b in range(blocks):
-        stats = x_ref[b, :, 2 * WIDTH : 2 * WIDTH + DH].astype(F32)
+        stats = x_ref[b, 2 * HQ * rows :, :].astype(F32)
+        stats = jnp.concatenate([stats, jnp.zeros((DH - STATS, DH), F32)], 0)
+        stats = jnp.transpose(stats)[:rows]
         for h in range(HQ):
             to = pl.ds((h * blocks + b) * rows, rows)
             mine = jnp.where((lane & (HQ - 1)) == h, stats, 0.0).astype(BF)
-            q_s[to, :DH] = x_ref[b, :, h * DH : (h + 1) * DH]
-            g_s[to, :DH] = x_ref[b, :, WIDTH + h * DH : WIDTH + (h + 1) * DH]
+            q_s[to, :DH] = x_ref[b, h * rows : (h + 1) * rows, :]
+            g_s[to, :DH] = x_ref[b, (HQ + h) * rows : (HQ + h + 1) * rows, :]
             q_s[to, DH:] = mine
             g_s[to, DH:] = mine
 
     row = lax.broadcasted_iota(jnp.int32, (DH, cols), 0)
-    k_ones = jnp.where(row < 3 * HQ, 1.0, 0.0).astype(BF)
-    v_ones = jnp.where((row >= 3 * HQ) & (row < 6 * HQ), 1.0, 0.0).astype(BF)
+    k_ones = jnp.where(row < STATS // 2, 1.0, 0.0).astype(BF)
+    v_ones = jnp.where((row >= STATS // 2) & (row < STATS), 1.0, 0.0).astype(BF)
     over_rows = (((0,), (0,)), ((), ()))
     for j in range(chunks):
         k = jnp.concatenate([own_ref[j, 0], other_ref[j, 0]], 0)
@@ -123,25 +123,26 @@
         else:
             acc[...] += dq
 
-    out_ref = dq_ref
     if last:
-        near = quad_ref[0]
-        dq_ref[near] = near_ref[...]
-        out_ref = dq_ref.at[1 - near]
+        side = side_ref[0]
+        for b in range(blocks):
+            dq_ref[b, side] = near_ref[b]
     for b in range(blocks):
+        out_ref = dq_ref.at[b, 1 - side] if last else dq_ref.at[b]
         for h in range(HQ):
             at = pl.ds((h * blocks + b) * rows, rows)
-            out_ref[b, :, h * DH : (h + 1) * DH] = acc[at, :].astype(BF)
+            out_ref[:, h * DH : (h + 1) * DH] = acc[at, :].astype(BF)
     if not last:
         for copy in copies:
             copy.wait()
 
 
-def grads(x, own, other, quad=None, before=()):
-    blocks, rows, _ = x.shape
+def grads(x, own, other, side=None, before=()):
+    blocks = x.shape[0]
+    rows = (x.shape[1] - STATS) // (2 * HQ)
     chunks, _, half, cols = own.shape
     total = blocks * rows * HQ
-    last = quad is not None
+    last = side is not None
     work = total * chunks * cols
     small = pl.BlockSpec(memory_space=pltpu.SMEM)
     whole = pl.BlockSpec(memory_space=pltpu.VMEM)
@@ -149,10 +150,10 @@
     sums = (chunks, 2, 2 * half, cols)
     halves = (chunks, 2, half, cols)
     if last:
-        operands = (quad, x, own, other, *before)
+        operands = (side, x, own, other, *before)
         in_specs = [small] + [whole] * 4 + [far]
         out_shape = [
-            jax.ShapeDtypeStruct((2, blocks, rows, WIDTH), BF),
+            jax.ShapeDtypeStruct((blocks, 2, rows, WIDTH), BF),
             jax.ShapeDtypeStruct(halves, F32),
             jax.ShapeDtypeStruct(halves, BF),
         ]
@@ -248,20 +249,19 @@
 
 def per_device(queries, keys, values, outputs, out_grad, logsumexp):
     core = index("core")
-    x, copies, kv = prep(core, queries, out_grad, outputs, logsumexp.T, keys, values)
-
-    x_near = lax.all_to_all(copies, "zi", 0, 0)
-    far = lax.ppermute(x, "zq", SWAP)
+    copies, kv = prep(core, queries, out_grad, outputs, logsumexp.T, keys, values)
+
+    x = lax.all_to_all(copies, "z4", 0, 0)
 
     own = lax.all_gather(kv, "y")
-    far, own = lax.optimization_barrier((far, own))
     other = lax.ppermute(own, "core", SWAP)
-    x_far = lax.all_to_all(jnp.broadcast_to(far, copies.shape), "zi", 0, 0)
-
-    before = grads(x_near, own, other)
-    dq, keep, send = grads(x_far, own, other, index("zq"), before)
+    x, own, other = lax.optimization_barrier((x, own, other))
+    beside = lax.ppermute(x, "z2", SWAP)
+
+    before = grads(x, own, other)
+    dq, keep, send = grads(beside, own, other, index("z2"), before)
     dq = dq.reshape((-1,) + dq.shape[2:])
-    query_grad = query_total(core, lax.all_to_all(dq, ("zq", "zi"), 0, 0))
+    query_grad = query_total(core, lax.all_to_all(dq, ("z4", "z2"), 0, 0))
 
     both = both_cores(index("y"), keep, lax.ppermute(send, "core", SWAP))
     parts = [both[0]] + [along("y", both[r], r) for r in range(1, len(both))]
@@ -270,10 +270,10 @@
 
 
 def solution(mesh):
-    devices = mesh.devices.reshape(2, 4, 2, 4, 2, 4)
-    inner = Mesh(devices, ("zh", "x", "core", "y", "zq", "zi"))
+    devices = mesh.devices.reshape(2, 4, 2, 4, 4, 2)
+    inner = Mesh(devices, ("zh", "x", "core", "y", "z4", "z2"))
     head = ("zh", "x", "core")
-    seq = ("y", "zq", "zi")
+    seq = ("y", "z4", "z2")
     text = P(seq, head)
     visual = P(head, seq)
     return jax.shard_map(

time: 86.8 us -> 88.7 us (1.022)
  waiting for transfers between devices: 11.1 us -> 19.2 us
  starting transfers between devices: 41.5 us -> 35.5 us
    ppermute x1, starting transfers between devices: 9.08 us -> 1.91 us  [per_device(): beside = lax.ppermute(x, 'z2', SWAP)]
    all_to_all x3 -> x2, waiting for transfers between devices: 2.47 us -> 7.44 us  [the longest x1 6.07 us: per_device(): x = lax.all_to_all(copies, 'z4', 0, 0)]
    ppermute x1, waiting for transfers between devices: 0.01 us -> 3.01 us  [per_device(): beside = lax.ppermute(x, 'z2', SWAP)]
    all_to_all x3 -> x2, starting transfers between devices: 17 us -> 18.2 us  [the longest x1 11.2 us: per_device(): x = lax.all_to_all(copies, 'z4', 0, 0)]
  transfers between devices with their start and end apart: 9 -> 8, of which waited for: 6 -> 7; matrix products, arithmetic and copies ran while one was open for 0% -> 0% of each run, Pallas kernels for 8% -> 8%
where the time goes in v5:
time: 88.7 us; the launch traced here: 87.7 us
  starting transfers between devices  35.5 us (40%)
  waiting for transfers between devices  19.2 us (22%)
  Pallas kernels  17.7 us (20%)
  blocking collectives  13.8 us (16%)
    pallas_call x2, Pallas kernels, grads(): pl.pallas_call(lambda *refs: grads_kernel(last, *refs), in_specs=in_specs...  13.9 us
    all_gather x1, blocking collectives, per_device(): own = lax.all_gather(kv, 'y')  13.8 us
    ppermute x3, starting transfers between devices, along(): lax.ppermute(value, axis, [(i, (i + steps) % count) for i in range(count)])  11.6 us
    all_to_all x1, starting transfers between devices, per_device(): x = lax.all_to_all(copies, 'z4', 0, 0)  11.2 us
    all_to_all x1, starting transfers between devices, per_device(): query_grad = query_total(core, lax.all_to_all(dq, ('z4', 'z2'), 0, 0))  7.02 us
    all_to_all x1, waiting for transfers between devices, per_device(): x = lax.all_to_all(copies, 'z4', 0, 0)  6.07 us
    ppermute x3, waiting for transfers between devices, along(): lax.ppermute(value, axis, [(i, (i + steps) % count) for i in range(count)])  4.45 us
    ppermute x1, waiting for transfers between devices, per_device(): beside = lax.ppermute(x, 'z2', SWAP)  3.01 us
  transfers between devices with their start and end apart: 8, of which 7 were waited for; matrix products, arithmetic and copies ran while one was open for 0% of the time, Pallas kernels for 8%

profile of v5, /device:TPU:6, one launch (start us, length us, event | category | flops | bytes accessed | tf_op | source)
XLA Modules:
  0.0 87.7 jit_solution(3751042627099479804)
XLA Ops:
  0.6 2.2 %prep.1 = (bf16[4,400,128]{2,1,0:T(8,128)(2,1)}, bf16[2,64,640]{2,1,0:T(8,128)(2,1)}) custom-call(s32[1]{0:T(128)} %bitcast.core_ref, bf16[48,512]{1,0:T(8,128)(2,1)} %q_ref.1, bf16[48,512]{1,0:T(8,128)(2,1)} %g_ref.1, bf16[48,512]{1,0:T(8,128)(2,1)} %o_ref.1, f32[4,48]{1,0:T(4,128)} %bitcast.9, bf16[64,640]{1,0:T(8,128)(2,1)} %k_ref.1, bf16[64,640]{1,0:T(8,128)(2,1)} %v_ref.1), custom_call_target="tpu_custom_call" | custom-call | tf_op jit(solution)/shard_map/prep/pallas_call | solution.py:57
  2.8 11.2 %all-to-all-start = ((bf16[4,400,128]{2,1,0:T(8,128)(2,1)}), bf16[4,400,128]{2,1,0:T(8,128)(2,1)S(1)}, u32[]{:S(2)}, u32[]{:S(2)}) async-start(bf16[4,400,128]{2,1,0:T(8,128)(2,1)} %get-tuple-element.19), calls=%async_computation | async-start | bytes 819200 | tf_op jit(solution)/shard_map/all_to_all | solution.py:254
  14.0 13.8 %all-gather = bf16[8,64,640]{2,1,0:T(8,128)(2,1)S(1)} all-gather(bf16[2,64,640]{2,1,0:T(8,128)(2,1)} %get-tuple-element.20), channel_id=2, replica_groups=mesh['zh'=2,'x'=4,'core'=2,'y'=4,'z4'=4,'z2'=2] {'y'}, dimensions={0}, use_global_device_ids=true | all-gather | bytes 819200 | tf_op jit(solution)/shard_map/all_gather | solution.py:256
  27.8 1.9 %collective-permute-start = (bf16[4,2,64,640]{3,2,1,0:T(8,128)(2,1)S(1)}, bf16[4,2,64,640]{3,2,1,0:T(8,128)(2,1)S(1)}, u32[]{:S(2)}, u32[]{:S(2)}) collective-permute-start(bf16[4,2,64,640]{3,2,1,0:T(8,128)(2,1)S(1)} %bitcast.6), channel_id=1, source_target_pairs={{0,32},{32,0},{1,33},{33,1},{2,34},{34,2},{3,35},{35,3},{4,36},{36... | collective-permute-start | bytes 1966088 | tf_op jit(solution)/shard_map/ppermute | solution.py:257
  29.7 2.1 %collective-permute-done.refs_2_.refs_3_ = bf16[4,2,64,640]{3,2,1,0:T(8,128)(2,1)S(1)} collective-permute-done((bf16[4,2,64,640]{3,2,1,0:T(8,128)(2,1)S(1)}, bf16[4,2,64,640]{3,2,1,0:T(8,128)(2,1)S(1)}, u32[]{:S(2)}, u32[]{:S(2)}) %collective-permute-start) | collective-permute-done | bytes 655392 | tf_op jit(solution)/shard_map/ppermute | solution.py:257
  31.7 6.1 %all-to-all-done.refs_0_ = bf16[4,400,128]{2,1,0:T(8,128)(2,1)S(1)} async-done(((bf16[4,400,128]{2,1,0:T(8,128)(2,1)}), bf16[4,400,128]{2,1,0:T(8,128)(2,1)S(1)}, u32[]{:S(2)}, u32[]{:S(2)}) %all-to-all-start) | async-done | bytes 409632 | tf_op jit(solution)/shard_map/all_to_all | solution.py:254
  37.8 1.9 %collective-permute-start.1 = (bf16[4,400,128]{2,1,0:T(8,128)(2,1)S(1)}, bf16[4,400,128]{2,1,0:T(8,128)(2,1)S(1)}, u32[]{:S(2)}, u32[]{:S(2)}) collective-permute-start(bf16[4,400,128]{2,1,0:T(8,128)(2,1)S(1)} %all-to-all-done.refs_0_), channel_id=1, source_target_pairs={{0,1},{1,0},{2,3},{3,2},{4,5},{5,4},{6,7},{7,6},{8,9},{9,8},{10,11... | collective-permute-start | bytes 1228808 | tf_op jit(solution)/shard_map/ppermute | solution.py:259
  39.7 5.9 %grads.2 = (bf16[4,48,512]{2,1,0:T(8,128)(2,1)S(1)}, f32[40,2,128,640]{3,2,1,0:T(8,128)}) custom-call(bf16[4,400,128]{2,1,0:T(8,128)(2,1)S(1)} %all-to-all-done.refs_0_, bf16[4,2,64,640]{3,2,1,0:T(8,128)(2,1)S(1)} %bitcast.7, bf16[4,2,64,640]{3,2,1,0:T(8,128)(2,1)S(1)} %collective-permute-done.refs_2_.refs_3_), custom_call_target="tpu_custom_call" | custom-call | flops 2516582400 | bytes 4194304 | tf_op jit(solution)/shard_map/grads/pallas_call | solution.py:169
  45.6 3.0 %collective-permute-done.1.refs_1_ = bf16[4,400,128]{2,1,0:T(8,128)(2,1)S(1)} collective-permute-done((bf16[4,400,128]{2,1,0:T(8,128)(2,1)S(1)}, bf16[4,400,128]{2,1,0:T(8,128)(2,1)S(1)}, u32[]{:S(2)}, u32[]{:S(2)}) %collective-permute-start.1) | collective-permute-done | bytes 409632 | tf_op jit(solution)/shard_map/ppermute | solution.py:259
  48.6 8.0 %grads.3 = (bf16[4,2,48,512]{3,2,1,0:T(8,128)(2,1)}, f32[4,2,64,640]{3,2,1,0:T(8,128)S(1)}, bf16[4,2,64,640]{3,2,1,0:T(8,128)(2,1)S(1)}) custom-call(s32[1]{0:T(128)} %bitcast.1.refs_0_, bf16[4,400,128]{2,1,0:T(8,128)(2,1)S(1)} %collective-permute-done.1.refs_1_, bf16[4,2,64,640]{3,2,1,0:T(8,128)(2,1)S(1)} %bitcast.8, ...), custom_call_target="tpu_custom_call" | custom-call | flops 2516582400 | bytes 4194304 | tf_op jit(solution)/shard_map/grads/pallas_call | solution.py:169
  56.6 0.0 copy-start
  56.7 0.8 copy-done
  57.5 7.0 %all-to-all-start.1 = ((bf16[8,48,512]{2,1,0:T(8,128)(2,1)}), bf16[8,48,512]{2,1,0:T(8,128)(2,1)S(1)}, u32[]{:S(2)}, u32[]{:S(2)}) async-start(bf16[8,48,512]{2,1,0:T(8,128)(2,1)} %bitcast.4), calls=%async_computation.1 | async-start | bytes 786432 | tf_op jit(solution)/shard_map/all_to_all | solution.py:264
  64.5 1.9 %collective-permute-start.2 = (bf16[4,2,64,640]{3,2,1,0:T(8,128)(2,1)}, bf16[4,2,64,640]{3,2,1,0:T(8,128)(2,1)S(1)}, u32[]{:S(2)}, u32[]{:S(2)}) collective-permute-start(bf16[4,2,64,640]{3,2,1,0:T(8,128)(2,1)} %copy-done), channel_id=1, source_target_pairs={{0,32},{32,0},{1,33},{33,1},{2,34},{34,2},{3,35},{35,3},{4,36},{36... | collective-permute-start | bytes 1966088 | tf_op jit(solution)/shard_map/ppermute | solution.py:266
  66.4 2.3 %collective-permute-done.2.got_ref = bf16[4,2,64,640]{3,2,1,0:T(8,128)(2,1)S(1)} collective-permute-done((bf16[4,2,64,640]{3,2,1,0:T(8,128)(2,1)}, bf16[4,2,64,640]{3,2,1,0:T(8,128)(2,1)S(1)}, u32[]{:S(2)}, u32[]{:S(2)}) %collective-permute-start.2) | collective-permute-done | bytes 655392 | tf_op jit(solution)/shard_map/ppermute | solution.py:266
  68.7 0.1 both_cores.1
  68.8 3.9 %collective-permute-start.3 = (bf16[2,64,640]{2,1,0:T(8,128)(2,1)S(1)}, bf16[2,64,640]{2,1,0:T(8,128)(2,1)S(1)}, u32[]{:S(2)}, u32[]{:S(2)}) collective-permute-start(bf16[2,64,640]{2,1,0:T(8,128)(2,1)S(1)} %get-tuple-element.30), channel_id=1, source_target_pairs={{0,8},{8,16},{16,24},{24,0},{1,9},{9,17},{17,25},{25,1},{2,10},{10... | collective-permute-start | bytes 491528 | tf_op jit(solution)/shard_map/ppermute | solution.py:243
  72.7 4.6 %collective-permute-start.4 = (bf16[2,64,640]{2,1,0:T(8,128)(2,1)S(1)}, bf16[2,64,640]{2,1,0:T(8,128)(2,1)S(1)}, u32[]{:S(2)}, u32[]{:S(2)}) collective-permute-start(bf16[2,64,640]{2,1,0:T(8,128)(2,1)S(1)} %get-tuple-element.31), channel_id=1, source_target_pairs={{0,16},{8,24},{16,0},{24,8},{1,17},{9,25},{17,1},{25,9},{2,18},{10... | collective-permute-start | bytes 491528 | tf_op jit(solution)/shard_map/ppermute | solution.py:243
  77.3 3.1 %collective-permute-start.5 = (bf16[2,64,640]{2,1,0:T(8,128)(2,1)S(1)}, bf16[2,64,640]{2,1,0:T(8,128)(2,1)S(1)}, u32[]{:S(2)}, u32[]{:S(2)}) collective-permute-start(bf16[2,64,640]{2,1,0:T(8,128)(2,1)S(1)} %get-tuple-element.32), channel_id=1, source_target_pairs={{0,24},{8,0},{16,8},{24,16},{1,25},{9,1},{17,9},{25,17},{2,26},{10... | collective-permute-start | bytes 491528 | tf_op jit(solution)/shard_map/ppermute | solution.py:243
  80.4 0.0 collective-permute-done.3.refs_1_
  80.4 2.7 %collective-permute-done.4.refs_2_ = bf16[2,64,640]{2,1,0:T(8,128)(2,1)S(1)} collective-permute-done((bf16[2,64,640]{2,1,0:T(8,128)(2,1)S(1)}, bf16[2,64,640]{2,1,0:T(8,128)(2,1)S(1)}, u32[]{:S(2)}, u32[]{:S(2)}) %collective-permute-start.4) | collective-permute-done | bytes 163872 | tf_op jit(solution)/shard_map/ppermute | solution.py:243
  83.1 1.8 %collective-permute-done.5.refs_3_ = bf16[2,64,640]{2,1,0:T(8,128)(2,1)S(1)} collective-permute-done((bf16[2,64,640]{2,1,0:T(8,128)(2,1)S(1)}, bf16[2,64,640]{2,1,0:T(8,128)(2,1)S(1)}, u32[]{:S(2)}, u32[]{:S(2)}) %collective-permute-start.5) | collective-permute-done | bytes 163872 | tf_op jit(solution)/shard_map/ppermute | solution.py:243
  84.8 0.7 visual_total.1
  85.6 1.4 %all-to-all-done.1.parts_ref = bf16[8,48,512]{2,1,0:T(8,128)(2,1)S(1)} async-done(((bf16[8,48,512]{2,1,0:T(8,128)(2,1)}), bf16[8,48,512]{2,1,0:T(8,128)(2,1)S(1)}, u32[]{:S(2)}, u32[]{:S(2)}) %all-to-all-start.1) | async-done | bytes 393248 | tf_op jit(solution)/shard_map/all_to_all | solution.py:264
  86.9 0.7 query_total.1
Async XLA Ops:
  2.8 35.0 %all-to-all-start = ((bf16[4,400,128]{2,1,0:T(8,128)(2,1)}), bf16[4,400,128]{2,1,0:T(8,128)(2,1)S(1)}, u32[]{:S(2)}, u32[]{:S(2)}) async-start(bf16[4,400,128]{2,1,0:T(8,128)(2,1)} %get-tuple-element.19), calls=%async_computation | async-start | bytes 819200 | tf_op jit(solution)/shard_map/all_to_all | solution.py:254
  27.8 4.0 %collective-permute-start = (bf16[4,2,64,640]{3,2,1,0:T(8,128)(2,1)S(1)}, bf16[4,2,64,640]{3,2,1,0:T(8,128)(2,1)S(1)}, u32[]{:S(2)}, u32[]{:S(2)}) collective-permute-start(bf16[4,2,64,640]{3,2,1,0:T(8,128)(2,1)S(1)} %bitcast.6), channel_id=1, source_target_pairs={{0,32},{32,0},{1,33},{33,1},{2,34},{34,2},{3,35},{35,3},{4,36},{36... | collective-permute-start | bytes 1966088 | tf_op jit(solution)/shard_map/ppermute | solution.py:257
  37.8 10.8 %collective-permute-start.1 = (bf16[4,400,128]{2,1,0:T(8,128)(2,1)S(1)}, bf16[4,400,128]{2,1,0:T(8,128)(2,1)S(1)}, u32[]{:S(2)}, u32[]{:S(2)}) collective-permute-start(bf16[4,400,128]{2,1,0:T(8,128)(2,1)S(1)} %all-to-all-done.refs_0_), channel_id=1, source_target_pairs={{0,1},{1,0},{2,3},{3,2},{4,5},{5,4},{6,7},{7,6},{8,9},{9,8},{10,11... | collective-permute-start | bytes 1228808 | tf_op jit(solution)/shard_map/ppermute | solution.py:259
  56.6 0.8 copy-start
  57.5 29.5 %all-to-all-start.1 = ((bf16[8,48,512]{2,1,0:T(8,128)(2,1)}), bf16[8,48,512]{2,1,0:T(8,128)(2,1)S(1)}, u32[]{:S(2)}, u32[]{:S(2)}) async-start(bf16[8,48,512]{2,1,0:T(8,128)(2,1)} %bitcast.4), calls=%async_computation.1 | async-start | bytes 786432 | tf_op jit(solution)/shard_map/all_to_all | solution.py:264
  64.5 4.2 %collective-permute-start.2 = (bf16[4,2,64,640]{3,2,1,0:T(8,128)(2,1)}, bf16[4,2,64,640]{3,2,1,0:T(8,128)(2,1)S(1)}, u32[]{:S(2)}, u32[]{:S(2)}) collective-permute-start(bf16[4,2,64,640]{3,2,1,0:T(8,128)(2,1)} %copy-done), channel_id=1, source_target_pairs={{0,32},{32,0},{1,33},{33,1},{2,34},{34,2},{3,35},{35,3},{4,36},{36... | collective-permute-start | bytes 1966088 | tf_op jit(solution)/shard_map/ppermute | solution.py:266
  68.8 11.6 %collective-permute-start.3 = (bf16[2,64,640]{2,1,0:T(8,128)(2,1)S(1)}, bf16[2,64,640]{2,1,0:T(8,128)(2,1)S(1)}, u32[]{:S(2)}, u32[]{:S(2)}) collective-permute-start(bf16[2,64,640]{2,1,0:T(8,128)(2,1)S(1)} %get-tuple-element.30), channel_id=1, source_target_pairs={{0,8},{8,16},{16,24},{24,0},{1,9},{9,17},{17,25},{25,1},{2,10},{10... | collective-permute-start | bytes 491528 | tf_op jit(solution)/shard_map/ppermute | solution.py:243
  72.7 10.4 %collective-permute-start.4 = (bf16[2,64,640]{2,1,0:T(8,128)(2,1)S(1)}, bf16[2,64,640]{2,1,0:T(8,128)(2,1)S(1)}, u32[]{:S(2)}, u32[]{:S(2)}) collective-permute-start(bf16[2,64,640]{2,1,0:T(8,128)(2,1)S(1)} %get-tuple-element.31), channel_id=1, source_target_pairs={{0,16},{8,24},{16,0},{24,8},{1,17},{9,25},{17,1},{25,9},{2,18},{10... | collective-permute-start | bytes 491528 | tf_op jit(solution)/shard_map/ppermute | solution.py:243
  77.3 7.6 %collective-permute-start.5 = (bf16[2,64,640]{2,1,0:T(8,128)(2,1)S(1)}, bf16[2,64,640]{2,1,0:T(8,128)(2,1)S(1)}, u32[]{:S(2)}, u32[]{:S(2)}) collective-permute-start(bf16[2,64,640]{2,1,0:T(8,128)(2,1)S(1)} %get-tuple-element.32), channel_id=1, source_target_pairs={{0,24},{8,0},{16,8},{24,16},{1,25},{9,1},{17,9},{25,17},{2,26},{10... | collective-permute-start | bytes 491528 | tf_op jit(solution)/shard_map/ppermute | solution.py:243

commit v6 on v5

--- a/solution.py
+++ b/solution.py
@@ -25,13 +25,12 @@
     return jnp.where(core == 0, value, rolled)
 
 
-def prep_kernel(core_ref, q_ref, g_ref, o_ref, lse_ref, k_ref, v_ref, copies_ref, kv_ref):
+def prep_kernel(core_ref, q_ref, g_ref, o_ref, lse_ref, k_ref, v_ref, x_ref, copies_ref, kv_ref):
     core = core_ref[0]
     rows = q_ref.shape[0]
     lane = lax.broadcasted_iota(jnp.int32, (rows, DH), 1)
     lse = jnp.transpose(lse_ref[...]) * (-1.0 / SCALE)
     stats = jnp.zeros((rows, DH), F32)
-    block = copies_ref.at[0]
     for h in range(HQ):
         at = pl.ds(h * DH, DH)
         q = q_ref[:, at].astype(F32)
@@ -40,14 +39,14 @@
         mine = (lane & (HQ - 1)) == h
         stats = jnp.where(mine & (lane < 2 * HQ), lse[:, h : h + 1], stats)
         stats = jnp.where(mine & (lane >= 2 * HQ) & (lane < STATS), -dterm, stats)
-        block[h * rows : (h + 1) * rows, :] = half_swap(q, core).astype(BF)
-        block[(HQ + h) * rows : (HQ + h + 1) * rows, :] = half_swap(g, core).astype(BF)
+        x_ref[h * rows : (h + 1) * rows, :] = half_swap(q, core).astype(BF)
+        x_ref[(HQ + h) * rows : (HQ + h + 1) * rows, :] = half_swap(g, core).astype(BF)
     high = stats.astype(BF).astype(F32)
     stats = jnp.where((lane & HQ) == 0, high, stats - high)
     stats = jnp.concatenate([stats, jnp.zeros((DH - rows, DH), F32)], 0)
-    block[2 * HQ * rows :, :] = jnp.transpose(stats)[:STATS].astype(BF)
-    for b in range(1, copies_ref.shape[0]):
-        copies_ref[b] = copies_ref[0]
+    x_ref[2 * HQ * rows :, :] = jnp.transpose(stats)[:STATS].astype(BF)
+    for b in range(copies_ref.shape[0]):
+        copies_ref[b] = x_ref[...]
     kv_ref[0] = k_ref[...]
     kv_ref[1] = v_ref[...]
 
@@ -58,7 +57,8 @@
         prep_kernel,
         in_specs=[pl.BlockSpec(memory_space=pltpu.SMEM)] + [pl.BlockSpec(memory_space=pltpu.VMEM)] * 6,
         out_shape=[
-            jax.ShapeDtypeStruct((lax.axis_size("z4"), 2 * HQ * rows + STATS, DH), BF),
+            jax.ShapeDtypeStruct((2 * HQ * rows + STATS, DH), BF),
+            jax.ShapeDtypeStruct((lax.axis_size("zi"), 2 * HQ * rows + STATS, DH), BF),
             jax.ShapeDtypeStruct((2,) + keys.shape, BF),
         ],
         name="prep",
@@ -68,7 +68,7 @@
 def grads_kernel(last, *refs):
     if last:
         side_ref, x_ref, own_ref, other_ref, near_ref, before_ref, *refs = refs
-        dq_ref, keep_ref, send_ref, q_s, g_s, acc, held, sems = refs
+        dq_ref, keep_ref, send_ref, q_s, g_s, acc, held, sems, got = refs
     else:
         x_ref, own_ref, other_ref, dq_ref, after_ref, q_s, g_s, acc, held, sems = refs
     blocks = x_ref.shape[0]
@@ -76,7 +76,7 @@
     chunks, _, half, cols = own_ref.shape
     copies = []
     for j in range(chunks):
-        ends = (before_ref.at[j], held.at[j]) if last else (held.at[j], after_ref.at[j])
+        ends = (before_ref.at[j], got.at[j]) if last else (held.at[j], after_ref.at[j])
         copies.append(pltpu.make_async_copy(*ends, sems.at[j]))
         if last:
             copies[j].start()
@@ -108,15 +108,9 @@
         dv = lax.dot_general(g_s[:, :DH], pb, over_rows, preferred_element_type=F32)
         dk = lax.dot_general(q_s[:, :DH], ds, over_rows, preferred_element_type=F32) * SCALE
         dq = lax.dot_general(ds, k, (((1,), (1,)), ((), ())), preferred_element_type=F32) * SCALE
-        if last:
-            copies[j].wait()
-            for i, part in enumerate((dk, dv)):
-                total = part + held[j, i]
-                keep_ref[j, i] = total[:half]
-                send_ref[j, i] = total[half:].astype(BF)
-        else:
-            held[j, 0] = dk
-            held[j, 1] = dv
+        held[j, 0] = dk
+        held[j, 1] = dv
+        if not last:
             copies[j].start()
         if j == 0:
             acc[...] = dq
@@ -125,16 +119,18 @@
 
     if last:
         side = side_ref[0]
-        for b in range(blocks):
-            dq_ref[b, side] = near_ref[b]
+        dq_ref[side] = near_ref[...]
     for b in range(blocks):
-        out_ref = dq_ref.at[b, 1 - side] if last else dq_ref.at[b]
+        out_ref = dq_ref.at[1 - side, b] if last else dq_ref.at[b]
         for h in range(HQ):
             at = pl.ds((h * blocks + b) * rows, rows)
             out_ref[:, h * DH : (h + 1) * DH] = acc[at, :].astype(BF)
-    if not last:
-        for copy in copies:
-            copy.wait()
+    for j, copy in enumerate(copies):
+        copy.wait()
+        if last:
+            total = held[j] + got[j]
+            keep_ref[j] = total[:, :half]
+            send_ref[j] = total[:, half:].astype(BF)
 
 
 def grads(x, own, other, side=None, before=()):
@@ -153,7 +149,7 @@
         operands = (side, x, own, other, *before)
         in_specs = [small] + [whole] * 4 + [far]
         out_shape = [
-            jax.ShapeDtypeStruct((blocks, 2, rows, WIDTH), BF),
+            jax.ShapeDtypeStruct((2, blocks, rows, WIDTH), BF),
             jax.ShapeDtypeStruct(halves, F32),
             jax.ShapeDtypeStruct(halves, BF),
         ]
@@ -177,7 +173,8 @@
             pltpu.VMEM((total, DH), F32),
             pltpu.VMEM(sums, F32),
             pltpu.SemaphoreType.DMA((chunks,)),
-        ],
+        ]
+        + [pltpu.VMEM(sums, F32)] * last,
         compiler_params=pltpu.CompilerParams(vmem_limit_bytes=VMEM_GRADS),
         cost_estimate=pl.CostEstimate(flops=10 * work * DH, bytes_accessed=4 << 20, transcendentals=work),
         name="grads",
@@ -249,31 +246,32 @@
 
 def per_device(queries, keys, values, outputs, out_grad, logsumexp):
     core = index("core")
-    copies, kv = prep(core, queries, out_grad, outputs, logsumexp.T, keys, values)
-
-    x = lax.all_to_all(copies, "z4", 0, 0)
+    x, copies, kv = prep(core, queries, out_grad, outputs, logsumexp.T, keys, values)
+
+    far = lax.ppermute(x, "zq", SWAP)
+    x_near = lax.all_to_all(copies, "zi", 0, 0)
 
     own = lax.all_gather(kv, "y")
+    far, own = lax.optimization_barrier((far, own))
     other = lax.ppermute(own, "core", SWAP)
-    x, own, other = lax.optimization_barrier((x, own, other))
-    beside = lax.ppermute(x, "z2", SWAP)
-
-    before = grads(x, own, other)
-    dq, keep, send = grads(beside, own, other, index("z2"), before)
+    x_far = lax.all_to_all(jnp.broadcast_to(far, copies.shape), "zi", 0, 0)
+
+    before = grads(x_near, own, other)
+    dq, keep, send = grads(x_far, own, other, index("zq"), before)
     dq = dq.reshape((-1,) + dq.shape[2:])
-    query_grad = query_total(core, lax.all_to_all(dq, ("z4", "z2"), 0, 0))
+    query_grad = query_total(core, lax.all_to_all(dq, ("zq", "zi"), 0, 0))
 
     both = both_cores(index("y"), keep, lax.ppermute(send, "core", SWAP))
-    parts = [both[0]] + [along("y", both[r], r) for r in range(1, len(both))]
+    parts = [both[0]] + [along("y", both[r], r) for r in (1, 3, 2)]
     key_grad, value_grad = visual_total(parts)
     return query_grad, key_grad, value_grad
 
 
 def solution(mesh):
-    devices = mesh.devices.reshape(2, 4, 2, 4, 4, 2)
-    inner = Mesh(devices, ("zh", "x", "core", "y", "z4", "z2"))
+    devices = mesh.devices.reshape(2, 4, 2, 4, 2, 4)
+    inner = Mesh(devices, ("zh", "x", "core", "y", "zq", "zi"))
     head = ("zh", "x", "core")
-    seq = ("y", "z4", "z2")
+    seq = ("y", "zq", "zi")
     text = P(seq, head)
     visual = P(head, seq)
     return jax.shard_map(

time: 88.7 us -> 84.7 us (0.955)
  waiting for transfers between devices: 19.2 us -> 11.9 us
  starting transfers between devices: 35.5 us -> 40.1 us
  Pallas kernels: 17.7 us -> 16 us
    ppermute x1, starting transfers between devices: 1.91 us -> 9.08 us  [per_device(): far = lax.ppermute(x, 'zq', SWAP)]
    all_to_all x2 -> x3, waiting for transfers between devices: 7.44 us -> 2.24 us  [the longest x1 2.23 us: per_device(): query_grad = query_total(core, lax.all_to_all(dq, ('zq', 'zi'), 0, 0))]
    ppermute x1, waiting for transfers between devices: 3.01 us -> 0.01 us  [per_device(): far = lax.ppermute(x, 'zq', SWAP)]
    all_to_all x2 -> x3, starting transfers between devices: 18.2 us -> 16.4 us  [the longest x1 5.89 us: per_device(): x_near = lax.all_to_all(copies, 'zi', 0, 0)]
    pallas_call x2, Pallas kernels: 13.9 us -> 12.2 us  [grads(): pl.pallas_call(lambda *refs: grads_kernel(last, *refs), in_specs=in_specs...]
  transfers between devices with their start and end apart: 8 -> 9, of which waited for: 7 -> 5; matrix products, arithmetic and copies ran while one was open for 0% -> 0% of each run, Pallas kernels for 8% -> 8%
where the time goes in v6:
time: 84.7 us; the launch traced here: 84.2 us
  starting transfers between devices  40.1 us (47%)
  Pallas kernels  16 us (19%)
  blocking collectives  13.8 us (16%)
  waiting for transfers between devices  11.9 us (14%)
  local copies, waits for them, and re-layouts  1.66 us (2%)
    all_gather x1, blocking collectives, per_device(): own = lax.all_gather(kv, 'y')  13.8 us
    pallas_call x2, Pallas kernels, grads(): pl.pallas_call(lambda *refs: grads_kernel(last, *refs), in_specs=in_specs...  12.2 us
    ppermute x3, starting transfers between devices, along(): lax.ppermute(value, axis, [(i, (i + steps) % count) for i in range(count)])  10.8 us
    ppermute x1, starting transfers between devices, per_device(): far = lax.ppermute(x, 'zq', SWAP)  9.08 us
    all_to_all x1, starting transfers between devices, per_device(): x_near = lax.all_to_all(copies, 'zi', 0, 0)  5.89 us
    all_to_all x1, starting transfers between devices, per_device(): x_far = lax.all_to_all(jnp.broadcast_to(far, copies.shape), 'zi', 0, 0)  5.37 us
    ppermute x3, waiting for transfers between devices, along(): lax.ppermute(value, axis, [(i, (i + steps) % count) for i in range(count)])  5.3 us
    all_to_all x1, starting transfers between devices, per_device(): query_grad = query_total(core, lax.all_to_all(dq, ('zq', 'zi'), 0, 0))  5.1 us
  transfers between devices with their start and end apart: 9, of which 5 were waited for; matrix products, arithmetic and copies ran while one was open for 0% of the time, Pallas kernels for 8%

profile of v6, /device:TPU:6, one launch (start us, length us, event | category | flops | bytes accessed | tf_op | source)
XLA Modules:
  0.0 84.2 jit_solution(15135940584159430685)
XLA Ops:
  0.6 2.3 %prep.1 = (bf16[400,128]{1,0:T(8,128)(2,1)}, bf16[4,400,128]{2,1,0:T(8,128)(2,1)}, bf16[2,64,640]{2,1,0:T(8,128)(2,1)}) custom-call(s32[1]{0:T(128)} %bitcast.core_ref, bf16[48,512]{1,0:T(8,128)(2,1)} %q_ref.1, bf16[48,512]{1,0:T(8,128)(2,1)} %g_ref.1, bf16[48,512]{1,0:T(8,128)(2,1)} %o_ref.1, f32[4,48]{1,0:T(4,128)} %bitcast.9, bf16[64,640]{1,0:T(8,128)(2,1)} %k_ref.1, ...), custom_call_target="tpu_custom_call" | custom-call | tf_op jit(solution)/shard_map/prep/pallas_call | solution.py:56
  2.9 5.9 %all-to-all-start.1 = ((bf16[4,400,128]{2,1,0:T(8,128)(2,1)}), bf16[4,400,128]{2,1,0:T(8,128)(2,1)S(1)}, u32[]{:S(2)}, u32[]{:S(2)}) async-start(bf16[4,400,128]{2,1,0:T(8,128)(2,1)} %get-tuple-element.23), calls=%async_computation.1 | async-start | bytes 819200 | tf_op jit(solution)/shard_map/all_to_all | solution.py:252
  8.8 9.1 %collective-permute-start = (bf16[400,128]{1,0:T(8,128)(2,1)}, bf16[400,128]{1,0:T(8,128)(2,1)S(1)}, u32[]{:S(2)}, u32[]{:S(2)}) collective-permute-start(bf16[400,128]{1,0:T(8,128)(2,1)} %get-tuple-element.19), channel_id=1, source_target_pairs={{0,4},{4,0},{1,5},{5,1},{2,6},{6,2},{3,7},{7,3},{8,12},{12,8},{9,1... | collective-permute-start | bytes 307208 | tf_op jit(solution)/shard_map/ppermute | solution.py:251
  17.9 13.8 %all-gather = bf16[8,64,640]{2,1,0:T(8,128)(2,1)S(1)} all-gather(bf16[2,64,640]{2,1,0:T(8,128)(2,1)} %get-tuple-element.20), channel_id=2, replica_groups=mesh['zh'=2,'x'=4,'core'=2,'y'=4,'zq'=2,'zi'=4] {'y'}, dimensions={0}, use_global_device_ids=true | all-gather | bytes 819200 | tf_op jit(solution)/shard_map/all_gather | solution.py:254
  31.7 0.0 collective-permute-done
  31.7 0.0 all-to-all-done.1.refs_0_
  31.7 0.8 broadcast_in_dim.3
  32.5 5.4 %all-to-all-start = ((bf16[4,400,128]{2,1,0:T(8,128)(2,1)}), bf16[4,400,128]{2,1,0:T(8,128)(2,1)S(1)}, u32[]{:S(2)}, u32[]{:S(2)}) async-start(bf16[4,400,128]{2,1,0:T(8,128)(2,1)} %broadcast_in_dim.3), calls=%async_computation | async-start | bytes 819200 | tf_op jit(solution)/shard_map/all_to_all | solution.py:257
  37.9 1.9 %collective-permute-start.1 = (bf16[4,2,64,640]{3,2,1,0:T(8,128)(2,1)S(1)}, bf16[4,2,64,640]{3,2,1,0:T(8,128)(2,1)S(1)}, u32[]{:S(2)}, u32[]{:S(2)}) collective-permute-start(bf16[4,2,64,640]{3,2,1,0:T(8,128)(2,1)S(1)} %bitcast.6), channel_id=1, source_target_pairs={{0,32},{32,0},{1,33},{33,1},{2,34},{34,2},{3,35},{35,3},{4,36},{36... | collective-permute-start | bytes 1966088 | tf_op jit(solution)/shard_map/ppermute | solution.py:256
  39.8 2.1 %collective-permute-done.1.refs_2_.refs_3_ = bf16[4,2,64,640]{3,2,1,0:T(8,128)(2,1)S(1)} collective-permute-done((bf16[4,2,64,640]{3,2,1,0:T(8,128)(2,1)S(1)}, bf16[4,2,64,640]{3,2,1,0:T(8,128)(2,1)S(1)}, u32[]{:S(2)}, u32[]{:S(2)}) %collective-permute-start.1) | collective-permute-done | bytes 655392 | tf_op jit(solution)/shard_map/ppermute | solution.py:256
  41.9 5.9 %grads.2 = (bf16[4,48,512]{2,1,0:T(8,128)(2,1)S(1)}, f32[40,2,128,640]{3,2,1,0:T(8,128)}) custom-call(bf16[4,400,128]{2,1,0:T(8,128)(2,1)S(1)} %all-to-all-done.1.refs_0_, bf16[4,2,64,640]{3,2,1,0:T(8,128)(2,1)S(1)} %bitcast.7, bf16[4,2,64,640]{3,2,1,0:T(8,128)(2,1)S(1)} %collective-permute-done.1.refs_2_.refs_3_), custom_call_target="tpu_custom_call" | custom-call | flops 2516582400 | bytes 4194304 | tf_op jit(solution)/shard_map/grads/pallas_call | solution.py:165
  47.8 0.0 all-to-all-done.refs_1_
  47.8 6.3 %grads.3 = (bf16[2,4,48,512]{3,2,1,0:T(8,128)(2,1)}, f32[4,2,64,640]{3,2,1,0:T(8,128)S(1)}, bf16[4,2,64,640]{3,2,1,0:T(8,128)(2,1)S(1)}) custom-call(s32[1]{0:T(128)} %bitcast.1.refs_0_, bf16[4,400,128]{2,1,0:T(8,128)(2,1)S(1)} %all-to-all-done.refs_1_, bf16[4,2,64,640]{3,2,1,0:T(8,128)(2,1)S(1)} %bitcast.8, ...), custom_call_target="tpu_custom_call" | custom-call | flops 2516582400 | bytes 4194304 | tf_op jit(solution)/shard_map/grads/pallas_call | solution.py:165
  54.1 0.0 copy-start
  54.1 0.8 copy-done
  54.9 5.1 %all-to-all-start.2 = ((bf16[8,48,512]{2,1,0:T(8,128)(2,1)}), bf16[8,48,512]{2,1,0:T(8,128)(2,1)S(1)}, u32[]{:S(2)}, u32[]{:S(2)}) async-start(bf16[8,48,512]{2,1,0:T(8,128)(2,1)} %bitcast.4), calls=%async_computation.2 | async-start | bytes 786432 | tf_op jit(solution)/shard_map/all_to_all | solution.py:262
  60.0 1.9 %collective-permute-start.2 = (bf16[4,2,64,640]{3,2,1,0:T(8,128)(2,1)}, bf16[4,2,64,640]{3,2,1,0:T(8,128)(2,1)S(1)}, u32[]{:S(2)}, u32[]{:S(2)}) collective-permute-start(bf16[4,2,64,640]{3,2,1,0:T(8,128)(2,1)} %copy-done), channel_id=1, source_target_pairs={{0,32},{32,0},{1,33},{33,1},{2,34},{34,2},{3,35},{35,3},{4,36},{36... | collective-permute-start | bytes 1966088 | tf_op jit(solution)/shard_map/ppermute | solution.py:264
  61.9 2.3 %collective-permute-done.2.got_ref = bf16[4,2,64,640]{3,2,1,0:T(8,128)(2,1)S(1)} collective-permute-done((bf16[4,2,64,640]{3,2,1,0:T(8,128)(2,1)}, bf16[4,2,64,640]{3,2,1,0:T(8,128)(2,1)S(1)}, u32[]{:S(2)}, u32[]{:S(2)}) %collective-permute-start.2) | collective-permute-done | bytes 655392 | tf_op jit(solution)/shard_map/ppermute | solution.py:264
  64.2 0.1 both_cores.1
  64.3 3.4 %collective-permute-start.3 = (bf16[2,64,640]{2,1,0:T(8,128)(2,1)S(1)}, bf16[2,64,640]{2,1,0:T(8,128)(2,1)S(1)}, u32[]{:S(2)}, u32[]{:S(2)}) collective-permute-start(bf16[2,64,640]{2,1,0:T(8,128)(2,1)S(1)} %get-tuple-element.30), channel_id=1, source_target_pairs={{0,8},{8,16},{16,24},{24,0},{1,9},{9,17},{17,25},{25,1},{2,10},{10... | collective-permute-start | bytes 491528 | tf_op jit(solution)/shard_map/ppermute | solution.py:240
  67.7 3.7 %collective-permute-start.4 = (bf16[2,64,640]{2,1,0:T(8,128)(2,1)S(1)}, bf16[2,64,640]{2,1,0:T(8,128)(2,1)S(1)}, u32[]{:S(2)}, u32[]{:S(2)}) collective-permute-start(bf16[2,64,640]{2,1,0:T(8,128)(2,1)S(1)} %get-tuple-element.31), channel_id=1, source_target_pairs={{0,24},{8,0},{16,8},{24,16},{1,25},{9,1},{17,9},{25,17},{2,26},{10... | collective-permute-start | bytes 491528 | tf_op jit(solution)/shard_map/ppermute | solution.py:240
  71.4 3.8 %collective-permute-start.5 = (bf16[2,64,640]{2,1,0:T(8,128)(2,1)S(1)}, bf16[2,64,640]{2,1,0:T(8,128)(2,1)S(1)}, u32[]{:S(2)}, u32[]{:S(2)}) collective-permute-start(bf16[2,64,640]{2,1,0:T(8,128)(2,1)S(1)} %get-tuple-element.32), channel_id=1, source_target_pairs={{0,16},{8,24},{16,0},{24,8},{1,17},{9,25},{17,1},{25,9},{2,18},{10... | collective-permute-start | bytes 491528 | tf_op jit(solution)/shard_map/ppermute | solution.py:240
  75.2 0.0 collective-permute-done.3.refs_1_
  75.2 0.4 collective-permute-done.4.refs_2_
  75.6 4.9 %collective-permute-done.5.refs_3_ = bf16[2,64,640]{2,1,0:T(8,128)(2,1)S(1)} collective-permute-done((bf16[2,64,640]{2,1,0:T(8,128)(2,1)S(1)}, bf16[2,64,640]{2,1,0:T(8,128)(2,1)S(1)}, u32[]{:S(2)}, u32[]{:S(2)}) %collective-permute-start.5) | collective-permute-done | bytes 163872 | tf_op jit(solution)/shard_map/ppermute | solution.py:240
  80.5 0.7 visual_total.1
  81.2 2.2 %all-to-all-done.2.parts_ref = bf16[8,48,512]{2,1,0:T(8,128)(2,1)S(1)} async-done(((bf16[8,48,512]{2,1,0:T(8,128)(2,1)}), bf16[8,48,512]{2,1,0:T(8,128)(2,1)S(1)}, u32[]{:S(2)}, u32[]{:S(2)}) %all-to-all-start.2) | async-done | bytes 393248 | tf_op jit(solution)/shard_map/all_to_all | solution.py:262
  83.4 0.7 query_total.1
Async XLA Ops:
  2.9 28.8 %all-to-all-start.1 = ((bf16[4,400,128]{2,1,0:T(8,128)(2,1)}), bf16[4,400,128]{2,1,0:T(8,128)(2,1)S(1)}, u32[]{:S(2)}, u32[]{:S(2)}) async-start(bf16[4,400,128]{2,1,0:T(8,128)(2,1)} %get-tuple-element.23), calls=%async_computation.1 | async-start | bytes 819200 | tf_op jit(solution)/shard_map/all_to_all | solution.py:252
  8.8 22.9 %collective-permute-start = (bf16[400,128]{1,0:T(8,128)(2,1)}, bf16[400,128]{1,0:T(8,128)(2,1)S(1)}, u32[]{:S(2)}, u32[]{:S(2)}) collective-permute-start(bf16[400,128]{1,0:T(8,128)(2,1)} %get-tuple-element.19), channel_id=1, source_target_pairs={{0,4},{4,0},{1,5},{5,1},{2,6},{6,2},{3,7},{7,3},{8,12},{12,8},{9,1... | collective-permute-start | bytes 307208 | tf_op jit(solution)/shard_map/ppermute | solution.py:251
  32.5 15.2 %all-to-all-start = ((bf16[4,400,128]{2,1,0:T(8,128)(2,1)}), bf16[4,400,128]{2,1,0:T(8,128)(2,1)S(1)}, u32[]{:S(2)}, u32[]{:S(2)}) async-start(bf16[4,400,128]{2,1,0:T(8,128)(2,1)} %broadcast_in_dim.3), calls=%async_computation | async-start | bytes 819200 | tf_op jit(solution)/shard_map/all_to_all | solution.py:257
  37.9 4.0 %collective-permute-start.1 = (bf16[4,2,64,640]{3,2,1,0:T(8,128)(2,1)S(1)}, bf16[4,2,64,640]{3,2,1,0:T(8,128)(2,1)S(1)}, u32[]{:S(2)}, u32[]{:S(2)}) collective-permute-start(bf16[4,2,64,640]{3,2,1,0:T(8,128)(2,1)S(1)} %bitcast.6), channel_id=1, source_target_pairs={{0,32},{32,0},{1,33},{33,1},{2,34},{34,2},{3,35},{35,3},{4,36},{36... | collective-permute-start | bytes 1966088 | tf_op jit(solution)/shard_map/ppermute | solution.py:256
  54.1 0.8 %copy-start = (bf16[4,2,64,640]{3,2,1,0:T(8,128)(2,1)}, bf16[4,2,64,640]{3,2,1,0:T(8,128)(2,1)S(1)}, u32[]{:S(2)}) copy-start(bf16[4,2,64,640]{3,2,1,0:T(8,128)(2,1)S(1)} %get-tuple-element.28) | copy-start | bytes 1966084
  54.9 28.5 %all-to-all-start.2 = ((bf16[8,48,512]{2,1,0:T(8,128)(2,1)}), bf16[8,48,512]{2,1,0:T(8,128)(2,1)S(1)}, u32[]{:S(2)}, u32[]{:S(2)}) async-start(bf16[8,48,512]{2,1,0:T(8,128)(2,1)} %bitcast.4), calls=%async_computation.2 | async-start | bytes 786432 | tf_op jit(solution)/shard_map/all_to_all | solution.py:262
  60.0 4.2 %collective-permute-start.2 = (bf16[4,2,64,640]{3,2,1,0:T(8,128)(2,1)}, bf16[4,2,64,640]{3,2,1,0:T(8,128)(2,1)S(1)}, u32[]{:S(2)}, u32[]{:S(2)}) collective-permute-start(bf16[4,2,64,640]{3,2,1,0:T(8,128)(2,1)} %copy-done), channel_id=1, source_target_pairs={{0,32},{32,0},{1,33},{33,1},{2,34},{34,2},{3,35},{35,3},{4,36},{36... | collective-permute-start | bytes 1966088 | tf_op jit(solution)/shard_map/ppermute | solution.py:264
  64.3 10.8 %collective-permute-start.3 = (bf16[2,64,640]{2,1,0:T(8,128)(2,1)S(1)}, bf16[2,64,640]{2,1,0:T(8,128)(2,1)S(1)}, u32[]{:S(2)}, u32[]{:S(2)}) collective-permute-start(bf16[2,64,640]{2,1,0:T(8,128)(2,1)S(1)} %get-tuple-element.30), channel_id=1, source_target_pairs={{0,8},{8,16},{16,24},{24,0},{1,9},{9,17},{17,25},{25,1},{2,10},{10... | collective-permute-start | bytes 491528 | tf_op jit(solution)/shard_map/ppermute | solution.py:240
  67.7 7.9 %collective-permute-start.4 = (bf16[2,64,640]{2,1,0:T(8,128)(2,1)S(1)}, bf16[2,64,640]{2,1,0:T(8,128)(2,1)S(1)}, u32[]{:S(2)}, u32[]{:S(2)}) collective-permute-start(bf16[2,64,640]{2,1,0:T(8,128)(2,1)S(1)} %get-tuple-element.31), channel_id=1, source_target_pairs={{0,24},{8,0},{16,8},{24,16},{1,25},{9,1},{17,9},{25,17},{2,26},{10... | collective-permute-start | bytes 491528 | tf_op jit(solution)/shard_map/ppermute | solution.py:240
  71.4 9.1 %collective-permute-start.5 = (bf16[2,64,640]{2,1,0:T(8,128)(2,1)S(1)}, bf16[2,64,640]{2,1,0:T(8,128)(2,1)S(1)}, u32[]{:S(2)}, u32[]{:S(2)}) collective-permute-start(bf16[2,64,640]{2,1,0:T(8,128)(2,1)S(1)} %get-tuple-element.32), channel_id=1, source_target_pairs={{0,16},{8,24},{16,0},{24,8},{1,17},{9,25},{17,1},{25,9},{2,18},{10... | collective-permute-start | bytes 491528 | tf_op jit(solution)/shard_map/ppermute | solution.py:240

commit v7 on v6

--- a/solution.py
+++ b/solution.py
@@ -9,6 +9,7 @@
 HQ = 4
 WIDTH = HQ * DH
 STATS = 4 * HQ
+GROUP = 2
 SCALE = DH**-0.5
 LOG2E = 1.4426950408889634
 BF = jnp.bfloat16
@@ -67,7 +68,7 @@
 
 def grads_kernel(last, *refs):
     if last:
-        side_ref, x_ref, own_ref, other_ref, near_ref, before_ref, *refs = refs
+        x_ref, own_ref, other_ref, near_ref, before_ref, *refs = refs
         dq_ref, keep_ref, send_ref, q_s, g_s, acc, held, sems, got = refs
     else:
         x_ref, own_ref, other_ref, dq_ref, after_ref, q_s, g_s, acc, held, sems = refs
@@ -93,13 +94,14 @@
             q_s[to, DH:] = mine
             g_s[to, DH:] = mine
 
-    row = lax.broadcasted_iota(jnp.int32, (DH, cols), 0)
+    row = lax.broadcasted_iota(jnp.int32, (DH, GROUP * cols), 0)
     k_ones = jnp.where(row < STATS // 2, 1.0, 0.0).astype(BF)
     v_ones = jnp.where((row >= STATS // 2) & (row < STATS), 1.0, 0.0).astype(BF)
     over_rows = (((0,), (0,)), ((), ()))
-    for j in range(chunks):
-        k = jnp.concatenate([own_ref[j, 0], other_ref[j, 0]], 0)
-        v = jnp.concatenate([own_ref[j, 1], other_ref[j, 1]], 0)
+    for j in range(0, chunks, GROUP):
+        group = range(j, j + GROUP)
+        k = jnp.concatenate([jnp.concatenate([own_ref[i, 0], other_ref[i, 0]], 0) for i in group], 1)
+        v = jnp.concatenate([jnp.concatenate([own_ref[i, 1], other_ref[i, 1]], 0) for i in group], 1)
         s = jnp.dot(q_s[...], jnp.concatenate([k, k_ones], 0), preferred_element_type=F32)
         p = jnp.exp2(s * (SCALE * LOG2E))
         dp = jnp.dot(g_s[...], jnp.concatenate([v, v_ones], 0), preferred_element_type=F32)
@@ -108,20 +110,21 @@
         dv = lax.dot_general(g_s[:, :DH], pb, over_rows, preferred_element_type=F32)
         dk = lax.dot_general(q_s[:, :DH], ds, over_rows, preferred_element_type=F32) * SCALE
         dq = lax.dot_general(ds, k, (((1,), (1,)), ((), ())), preferred_element_type=F32) * SCALE
-        held[j, 0] = dk
-        held[j, 1] = dv
-        if not last:
-            copies[j].start()
+        for n, i in enumerate(group):
+            held[i, 0] = dk[:, n * cols : (n + 1) * cols]
+            held[i, 1] = dv[:, n * cols : (n + 1) * cols]
+            if not last:
+                copies[i].start()
         if j == 0:
             acc[...] = dq
         else:
             acc[...] += dq
 
     if last:
-        side = side_ref[0]
-        dq_ref[side] = near_ref[...]
+        for b in range(blocks):
+            dq_ref[b, 0] = near_ref[b]
     for b in range(blocks):
-        out_ref = dq_ref.at[1 - side, b] if last else dq_ref.at[b]
+        out_ref = dq_ref.at[b, 1] if last else dq_ref.at[b]
         for h in range(HQ):
             at = pl.ds((h * blocks + b) * rows, rows)
             out_ref[:, h * DH : (h + 1) * DH] = acc[at, :].astype(BF)
@@ -133,23 +136,22 @@
             send_ref[j] = total[:, half:].astype(BF)
 
 
-def grads(x, own, other, side=None, before=()):
+def grads(x, own, other, before=()):
     blocks = x.shape[0]
     rows = (x.shape[1] - STATS) // (2 * HQ)
     chunks, _, half, cols = own.shape
     total = blocks * rows * HQ
-    last = side is not None
+    last = len(before) > 0
     work = total * chunks * cols
-    small = pl.BlockSpec(memory_space=pltpu.SMEM)
     whole = pl.BlockSpec(memory_space=pltpu.VMEM)
     far = pl.BlockSpec(memory_space=pltpu.HBM)
     sums = (chunks, 2, 2 * half, cols)
     halves = (chunks, 2, half, cols)
     if last:
-        operands = (side, x, own, other, *before)
-        in_specs = [small] + [whole] * 4 + [far]
+        operands = (x, own, other, *before)
+        in_specs = [whole] * 4 + [far]
         out_shape = [
-            jax.ShapeDtypeStruct((2, blocks, rows, WIDTH), BF),
+            jax.ShapeDtypeStruct((blocks, 2, rows, WIDTH), BF),
             jax.ShapeDtypeStruct(halves, F32),
             jax.ShapeDtypeStruct(halves, BF),
         ]
@@ -181,24 +183,40 @@
     )(*operands)
 
 
-def query_kernel(core_ref, parts_ref, out_ref):
+def far_kernel(parts_ref, out_ref):
+    total = parts_ref[0, 1].astype(F32)
+    for b in range(1, parts_ref.shape[0]):
+        total = total + parts_ref[b, 1].astype(F32)
+    out_ref[...] = total.astype(BF)
+
+
+def far_total(parts):
+    return pl.pallas_call(
+        far_kernel,
+        out_shape=jax.ShapeDtypeStruct(parts.shape[2:], BF),
+        compiler_params=SMALL,
+        name="far_total",
+    )(parts)
+
+
+def query_kernel(core_ref, parts_ref, far_ref, out_ref):
     core = core_ref[0]
     for h in range(HQ):
         at = pl.ds(h * DH, DH)
-        total = parts_ref[0, :, at].astype(F32)
-        for b in range(1, parts_ref.shape[0]):
-            total = total + parts_ref[b, :, at].astype(F32)
+        total = far_ref[:, at].astype(F32)
+        for b in range(parts_ref.shape[0]):
+            total = total + parts_ref[b, 0, :, at].astype(F32)
         out_ref[:, at] = half_swap(total, core).astype(BF)
 
 
-def query_total(core, parts):
+def query_total(core, parts, far):
     return pl.pallas_call(
         query_kernel,
-        in_specs=[pl.BlockSpec(memory_space=pltpu.SMEM), pl.BlockSpec(memory_space=pltpu.VMEM)],
-        out_shape=jax.ShapeDtypeStruct(parts.shape[1:], BF),
+        in_specs=[pl.BlockSpec(memory_space=pltpu.SMEM)] + [pl.BlockSpec(memory_space=pltpu.VMEM)] * 2,
+        out_shape=jax.ShapeDtypeStruct(far.shape, BF),
         compiler_params=SMALL,
         name="query_total",
-    )(core, parts)
+    )(core, parts, far)
 
 
 def both_kernel(y_ref, keep_ref, got_ref, *out_refs):
@@ -256,10 +274,9 @@
     other = lax.ppermute(own, "core", SWAP)
     x_far = lax.all_to_all(jnp.broadcast_to(far, copies.shape), "zi", 0, 0)
 
-    before = grads(x_near, own, other)
-    dq, keep, send = grads(x_far, own, other, index("zq"), before)
-    dq = dq.reshape((-1,) + dq.shape[2:])
-    query_grad = query_total(core, lax.all_to_all(dq, ("zq", "zi"), 0, 0))
+    dq, keep, send = grads(x_far, own, other, grads(x_near, own, other))
+    parts = lax.all_to_all(dq, "zi", 0, 0)
+    query_grad = query_total(core, parts, lax.ppermute(far_total(parts), "zq", SWAP))
 
     both = both_cores(index("y"), keep, lax.ppermute(send, "core", SWAP))
     parts = [both[0]] + [along("y", both[r], r) for r in (1, 3, 2)]

time: 84.7 us -> 87.3 us (1.031)
  starting transfers between devices: 40.1 us -> 43.7 us
    ppermute x0 -> x1, waiting for transfers between devices: none -> 5.61 us  [per_device(): lax.ppermute(far_total(parts), 'zq', SWAP)]
    ppermute x0 -> x1, starting transfers between devices: none -> 4.53 us  [per_device(): lax.ppermute(far_total(parts), 'zq', SWAP)]
    ppermute x3, waiting for transfers between devices: 5.3 us -> 1.64 us  [along(): lax.ppermute(value, axis, [(i, (i + steps) % count) for i in range(count)])]
    all_to_all x1, waiting for transfers between devices: 2.23 us -> 0.01 us  [per_device(): parts = lax.all_to_all(dq, 'zi', 0, 0)]
    ppermute x3, starting transfers between devices: 10.8 us -> 9.88 us  [along(): lax.ppermute(value, axis, [(i, (i + steps) % count) for i in range(count)])]
  transfers between devices with their start and end apart: 9 -> 10, of which waited for: 5 -> 4; matrix products, arithmetic and copies ran while one was open for 0% -> 0% of each run, Pallas kernels for 8% -> 7%
where the time goes in v7:
time: 87.3 us; the launch traced here: 86.8 us
  starting transfers between devices  43.7 us (50%)
  Pallas kernels  15.3 us (18%)
  blocking collectives  13.8 us (16%)
  waiting for transfers between devices  11.6 us (13%)
  local copies, waits for them, and re-layouts  1.65 us (2%)
    all_gather x1, blocking collectives, per_device(): own = lax.all_gather(kv, 'y')  13.8 us
    pallas_call x2, Pallas kernels, grads(): pl.pallas_call(lambda *refs: grads_kernel(last, *refs), in_specs=in_specs...  11.4 us
    ppermute x3, starting transfers between devices, along(): lax.ppermute(value, axis, [(i, (i + steps) % count) for i in range(count)])  9.88 us
    ppermute x1, starting transfers between devices, per_device(): far = lax.ppermute(x, 'zq', SWAP)  9.08 us
    all_to_all x1, starting transfers between devices, per_device(): x_near = lax.all_to_all(copies, 'zi', 0, 0)  5.89 us
    ppermute x1, waiting for transfers between devices, per_device(): lax.ppermute(far_total(parts), 'zq', SWAP)  5.61 us
    all_to_all x1, starting transfers between devices, per_device(): x_far = lax.all_to_all(jnp.broadcast_to(far, copies.shape), 'zi', 0, 0)  5.37 us
    all_to_all x1, starting transfers between devices, per_device(): parts = lax.all_to_all(dq, 'zi', 0, 0)  5.1 us
  transfers between devices with their start and end apart: 10, of which 4 were waited for; matrix products, arithmetic and copies ran while one was open for 0% of the time, Pallas kernels for 7%

profile of v7, /device:TPU:6, one launch (start us, length us, event | category | flops | bytes accessed | tf_op | source)
XLA Modules:
  0.0 86.8 jit_solution(3597811959395315792)
XLA Ops:
  0.6 2.3 %prep.1 = (bf16[400,128]{1,0:T(8,128)(2,1)}, bf16[4,400,128]{2,1,0:T(8,128)(2,1)}, bf16[2,64,640]{2,1,0:T(8,128)(2,1)}) custom-call(s32[1]{0:T(128)} %bitcast.core_ref, bf16[48,512]{1,0:T(8,128)(2,1)} %q_ref.1, bf16[48,512]{1,0:T(8,128)(2,1)} %g_ref.1, bf16[48,512]{1,0:T(8,128)(2,1)} %o_ref.1, f32[4,48]{1,0:T(4,128)} %bitcast.7, bf16[64,640]{1,0:T(8,128)(2,1)} %k_ref.1, ...), custom_call_target="tpu_custom_call" | custom-call | tf_op jit(solution)/shard_map/prep/pallas_call | solution.py:57
  2.9 5.9 %all-to-all-start.1 = ((bf16[4,400,128]{2,1,0:T(8,128)(2,1)}), bf16[4,400,128]{2,1,0:T(8,128)(2,1)S(1)}, u32[]{:S(2)}, u32[]{:S(2)}) async-start(bf16[4,400,128]{2,1,0:T(8,128)(2,1)} %get-tuple-element.23), calls=%async_computation.1 | async-start | bytes 819200 | tf_op jit(solution)/shard_map/all_to_all | solution.py:270
  8.8 9.1 %collective-permute-start = (bf16[400,128]{1,0:T(8,128)(2,1)}, bf16[400,128]{1,0:T(8,128)(2,1)S(1)}, u32[]{:S(2)}, u32[]{:S(2)}) collective-permute-start(bf16[400,128]{1,0:T(8,128)(2,1)} %get-tuple-element.19), channel_id=1, source_target_pairs={{0,4},{4,0},{1,5},{5,1},{2,6},{6,2},{3,7},{7,3},{8,12},{12,8},{9,1... | collective-permute-start | bytes 307208 | tf_op jit(solution)/shard_map/ppermute | solution.py:269
  17.9 13.8 %all-gather = bf16[8,64,640]{2,1,0:T(8,128)(2,1)S(1)} all-gather(bf16[2,64,640]{2,1,0:T(8,128)(2,1)} %get-tuple-element.20), channel_id=2, replica_groups=mesh['zh'=2,'x'=4,'core'=2,'y'=4,'zq'=2,'zi'=4] {'y'}, dimensions={0}, use_global_device_ids=true | all-gather | bytes 819200 | tf_op jit(solution)/shard_map/all_gather | solution.py:272
  31.7 0.0 collective-permute-done
  31.7 0.0 all-to-all-done.1.refs_0_
  31.7 0.8 broadcast_in_dim.3
  32.6 5.4 %all-to-all-start = ((bf16[4,400,128]{2,1,0:T(8,128)(2,1)}), bf16[4,400,128]{2,1,0:T(8,128)(2,1)S(1)}, u32[]{:S(2)}, u32[]{:S(2)}) async-start(bf16[4,400,128]{2,1,0:T(8,128)(2,1)} %broadcast_in_dim.3), calls=%async_computation | async-start | bytes 819200 | tf_op jit(solution)/shard_map/all_to_all | solution.py:275
  37.9 1.9 %collective-permute-start.1 = (bf16[4,2,64,640]{3,2,1,0:T(8,128)(2,1)S(1)}, bf16[4,2,64,640]{3,2,1,0:T(8,128)(2,1)S(1)}, u32[]{:S(2)}, u32[]{:S(2)}) collective-permute-start(bf16[4,2,64,640]{3,2,1,0:T(8,128)(2,1)S(1)} %bitcast.4), channel_id=1, source_target_pairs={{0,32},{32,0},{1,33},{33,1},{2,34},{34,2},{3,35},{35,3},{4,36},{36... | collective-permute-start | bytes 1966088 | tf_op jit(solution)/shard_map/ppermute | solution.py:274
  39.8 2.1 %collective-permute-done.1.refs_2_ = bf16[4,2,64,640]{3,2,1,0:T(8,128)(2,1)S(1)} collective-permute-done((bf16[4,2,64,640]{3,2,1,0:T(8,128)(2,1)S(1)}, bf16[4,2,64,640]{3,2,1,0:T(8,128)(2,1)S(1)}, u32[]{:S(2)}, u32[]{:S(2)}) %collective-permute-start.1) | collective-permute-done | bytes 655392 | tf_op jit(solution)/shard_map/ppermute | solution.py:274
  41.9 5.4 %grads.2 = (bf16[4,48,512]{2,1,0:T(8,128)(2,1)S(1)}, f32[40,2,128,640]{3,2,1,0:T(8,128)}) custom-call(bf16[4,400,128]{2,1,0:T(8,128)(2,1)S(1)} %all-to-all-done.1.refs_0_, bf16[4,2,64,640]{3,2,1,0:T(8,128)(2,1)S(1)} %bitcast.5, bf16[4,2,64,640]{3,2,1,0:T(8,128)(2,1)S(1)} %collective-permute-done.1.refs_2_), custom_call_target="tpu_custom_call" | custom-call | flops 2516582400 | bytes 4194304 | tf_op jit(solution)/shard_map/grads/pallas_call | solution.py:167
  47.4 0.0 all-to-all-done.refs_0_
  47.4 6.0 %grads.3 = (bf16[4,2,48,512]{3,2,1,0:T(8,128)(2,1)}, f32[4,2,64,640]{3,2,1,0:T(8,128)S(1)}, bf16[4,2,64,640]{3,2,1,0:T(8,128)(2,1)S(1)}) custom-call(bf16[4,400,128]{2,1,0:T(8,128)(2,1)S(1)} %all-to-all-done.refs_0_, bf16[4,2,64,640]{3,2,1,0:T(8,128)(2,1)S(1)} %bitcast.6, bf16[4,2,64,640]{3,2,1,0:T(8,128)(2,1)S(1)} %collective-permute-done.1.refs_2_, ...), custom_call_target="tpu_custom_call" | custom-call | flops 2516582400 | bytes 4194304 | tf_op jit(solution)/shard_map/grads/pallas_call | solution.py:167
  53.3 0.0 copy-start
  53.3 0.8 copy-done
  54.2 5.1 %all-to-all-start.2 = ((bf16[4,2,48,512]{3,2,1,0:T(8,128)(2,1)}), bf16[4,2,48,512]{3,2,1,0:T(8,128)(2,1)S(1)}, u32[]{:S(2)}, u32[]{:S(2)}) async-start(bf16[4,2,48,512]{3,2,1,0:T(8,128)(2,1)} %get-tuple-element.26), calls=%async_computation.2 | async-start | bytes 786432 | tf_op jit(solution)/shard_map/all_to_all | solution.py:278
  59.3 1.9 %collective-permute-start.3 = (bf16[4,2,64,640]{3,2,1,0:T(8,128)(2,1)}, bf16[4,2,64,640]{3,2,1,0:T(8,128)(2,1)S(1)}, u32[]{:S(2)}, u32[]{:S(2)}) collective-permute-start(bf16[4,2,64,640]{3,2,1,0:T(8,128)(2,1)} %copy-done), channel_id=1, source_target_pairs={{0,32},{32,0},{1,33},{33,1},{2,34},{34,2},{3,35},{35,3},{4,36},{36... | collective-permute-start | bytes 1966088 | tf_op jit(solution)/shard_map/ppermute | solution.py:281
  61.2 2.3 %collective-permute-done.3.got_ref = bf16[4,2,64,640]{3,2,1,0:T(8,128)(2,1)S(1)} collective-permute-done((bf16[4,2,64,640]{3,2,1,0:T(8,128)(2,1)}, bf16[4,2,64,640]{3,2,1,0:T(8,128)(2,1)S(1)}, u32[]{:S(2)}, u32[]{:S(2)}) %collective-permute-start.3) | collective-permute-done | bytes 655392 | tf_op jit(solution)/shard_map/ppermute | solution.py:281
  63.5 0.1 both_cores.1
  63.6 3.4 %collective-permute-start.4 = (bf16[2,64,640]{2,1,0:T(8,128)(2,1)S(1)}, bf16[2,64,640]{2,1,0:T(8,128)(2,1)S(1)}, u32[]{:S(2)}, u32[]{:S(2)}) collective-permute-start(bf16[2,64,640]{2,1,0:T(8,128)(2,1)S(1)} %get-tuple-element.30), channel_id=1, source_target_pairs={{0,8},{8,16},{16,24},{24,0},{1,9},{9,17},{17,25},{25,1},{2,10},{10... | collective-permute-start | bytes 491528 | tf_op jit(solution)/shard_map/ppermute | solution.py:258
  67.0 3.7 %collective-permute-start.5 = (bf16[2,64,640]{2,1,0:T(8,128)(2,1)S(1)}, bf16[2,64,640]{2,1,0:T(8,128)(2,1)S(1)}, u32[]{:S(2)}, u32[]{:S(2)}) collective-permute-start(bf16[2,64,640]{2,1,0:T(8,128)(2,1)S(1)} %get-tuple-element.31), channel_id=1, source_target_pairs={{0,24},{8,0},{16,8},{24,16},{1,25},{9,1},{17,9},{25,17},{2,26},{10... | collective-permute-start | bytes 491528 | tf_op jit(solution)/shard_map/ppermute | solution.py:258
  70.6 2.8 %collective-permute-start.6 = (bf16[2,64,640]{2,1,0:T(8,128)(2,1)S(1)}, bf16[2,64,640]{2,1,0:T(8,128)(2,1)S(1)}, u32[]{:S(2)}, u32[]{:S(2)}) collective-permute-start(bf16[2,64,640]{2,1,0:T(8,128)(2,1)S(1)} %get-tuple-element.32), channel_id=1, source_target_pairs={{0,16},{8,24},{16,0},{24,8},{1,17},{9,25},{17,1},{25,9},{2,18},{10... | collective-permute-start | bytes 491528 | tf_op jit(solution)/shard_map/ppermute | solution.py:258
  73.5 0.0 all-to-all-done.2.parts_ref
  73.5 4.5 %collective-permute-start.2 = (bf16[48,512]{1,0:T(8,128)(2,1)S(1)}, bf16[48,512]{1,0:T(8,128)(2,1)S(1)}, u32[]{:S(2)}, u32[]{:S(2)}) collective-permute-start(bf16[48,512]{1,0:T(8,128)(2,1)S(1)} %far_total.1), channel_id=1, source_target_pairs={{0,4},{4,0},{1,5},{5,1},{2,6},{6,2},{3,7},{7,3},{8,12},{12,8},{9,1... | collective-permute-start | bytes 147464 | tf_op jit(solution)/shard_map/ppermute | solution.py:279
  78.1 0.0 collective-permute-done.4.refs_1_
  78.1 0.0 collective-permute-done.5.refs_2_
  78.1 1.6 %collective-permute-done.6.refs_3_ = bf16[2,64,640]{2,1,0:T(8,128)(2,1)S(1)} collective-permute-done((bf16[2,64,640]{2,1,0:T(8,128)(2,1)S(1)}, bf16[2,64,640]{2,1,0:T(8,128)(2,1)S(1)}, u32[]{:S(2)}, u32[]{:S(2)}) %collective-permute-start.6) | collective-permute-done | bytes 163872 | tf_op jit(solution)/shard_map/ppermute | solution.py:258
  79.7 0.7 visual_total.1
  80.4 5.6 %collective-permute-done.2.far_ref = bf16[48,512]{1,0:T(8,128)(2,1)S(1)} collective-permute-done((bf16[48,512]{1,0:T(8,128)(2,1)S(1)}, bf16[48,512]{1,0:T(8,128)(2,1)S(1)}, u32[]{:S(2)}, u32[]{:S(2)}) %collective-permute-start.2) | collective-permute-done | bytes 49184 | tf_op jit(solution)/shard_map/ppermute | solution.py:279
  86.1 0.7 query_total.1
  (1 shorter events, 0.0 us)
Async XLA Ops:
  2.9 28.8 %all-to-all-start.1 = ((bf16[4,400,128]{2,1,0:T(8,128)(2,1)}), bf16[4,400,128]{2,1,0:T(8,128)(2,1)S(1)}, u32[]{:S(2)}, u32[]{:S(2)}) async-start(bf16[4,400,128]{2,1,0:T(8,128)(2,1)} %get-tuple-element.23), calls=%async_computation.1 | async-start | bytes 819200 | tf_op jit(solution)/shard_map/all_to_all | solution.py:270
  8.8 22.9 %collective-permute-start = (bf16[400,128]{1,0:T(8,128)(2,1)}, bf16[400,128]{1,0:T(8,128)(2,1)S(1)}, u32[]{:S(2)}, u32[]{:S(2)}) collective-permute-start(bf16[400,128]{1,0:T(8,128)(2,1)} %get-tuple-element.19), channel_id=1, source_target_pairs={{0,4},{4,0},{1,5},{5,1},{2,6},{6,2},{3,7},{7,3},{8,12},{12,8},{9,1... | collective-permute-start | bytes 307208 | tf_op jit(solution)/shard_map/ppermute | solution.py:269
  32.6 14.8 %all-to-all-start = ((bf16[4,400,128]{2,1,0:T(8,128)(2,1)}), bf16[4,400,128]{2,1,0:T(8,128)(2,1)S(1)}, u32[]{:S(2)}, u32[]{:S(2)}) async-start(bf16[4,400,128]{2,1,0:T(8,128)(2,1)} %broadcast_in_dim.3), calls=%async_computation | async-start | bytes 819200 | tf_op jit(solution)/shard_map/all_to_all | solution.py:275
  37.9 4.0 %collective-permute-start.1 = (bf16[4,2,64,640]{3,2,1,0:T(8,128)(2,1)S(1)}, bf16[4,2,64,640]{3,2,1,0:T(8,128)(2,1)S(1)}, u32[]{:S(2)}, u32[]{:S(2)}) collective-permute-start(bf16[4,2,64,640]{3,2,1,0:T(8,128)(2,1)S(1)} %bitcast.4), channel_id=1, source_target_pairs={{0,32},{32,0},{1,33},{33,1},{2,34},{34,2},{3,35},{35,3},{4,36},{36... | collective-permute-start | bytes 1966088 | tf_op jit(solution)/shard_map/ppermute | solution.py:274
  53.3 0.8 copy-start
  54.2 19.3 %all-to-all-start.2 = ((bf16[4,2,48,512]{3,2,1,0:T(8,128)(2,1)}), bf16[4,2,48,512]{3,2,1,0:T(8,128)(2,1)S(1)}, u32[]{:S(2)}, u32[]{:S(2)}) async-start(bf16[4,2,48,512]{3,2,1,0:T(8,128)(2,1)} %get-tuple-element.26), calls=%async_computation.2 | async-start | bytes 786432 | tf_op jit(solution)/shard_map/all_to_all | solution.py:278
  59.3 4.2 %collective-permute-start.3 = (bf16[4,2,64,640]{3,2,1,0:T(8,128)(2,1)}, bf16[4,2,64,640]{3,2,1,0:T(8,128)(2,1)S(1)}, u32[]{:S(2)}, u32[]{:S(2)}) collective-permute-start(bf16[4,2,64,640]{3,2,1,0:T(8,128)(2,1)} %copy-done), channel_id=1, source_target_pairs={{0,32},{32,0},{1,33},{33,1},{2,34},{34,2},{3,35},{35,3},{4,36},{36... | collective-permute-start | bytes 1966088 | tf_op jit(solution)/shard_map/ppermute | solution.py:281
  63.6 14.5 %collective-permute-start.4 = (bf16[2,64,640]{2,1,0:T(8,128)(2,1)S(1)}, bf16[2,64,640]{2,1,0:T(8,128)(2,1)S(1)}, u32[]{:S(2)}, u32[]{:S(2)}) collective-permute-start(bf16[2,64,640]{2,1,0:T(8,128)(2,1)S(1)} %get-tuple-element.30), channel_id=1, source_target_pairs={{0,8},{8,16},{16,24},{24,0},{1,9},{9,17},{17,25},{25,1},{2,10},{10... | collective-permute-start | bytes 491528 | tf_op jit(solution)/shard_map/ppermute | solution.py:258
  67.0 11.1 %collective-permute-start.5 = (bf16[2,64,640]{2,1,0:T(8,128)(2,1)S(1)}, bf16[2,64,640]{2,1,0:T(8,128)(2,1)S(1)}, u32[]{:S(2)}, u32[]{:S(2)}) collective-permute-start(bf16[2,64,640]{2,1,0:T(8,128)(2,1)S(1)} %get-tuple-element.31), channel_id=1, source_target_pairs={{0,24},{8,0},{16,8},{24,16},{1,25},{9,1},{17,9},{25,17},{2,26},{10... | collective-permute-start | bytes 491528 | tf_op jit(solution)/shard_map/ppermute | solution.py:258
  70.6 9.1 %collective-permute-start.6 = (bf16[2,64,640]{2,1,0:T(8,128)(2,1)S(1)}, bf16[2,64,640]{2,1,0:T(8,128)(2,1)S(1)}, u32[]{:S(2)}, u32[]{:S(2)}) collective-permute-start(bf16[2,64,640]{2,1,0:T(8,128)(2,1)S(1)} %get-tuple-element.32), channel_id=1, source_target_pairs={{0,16},{8,24},{16,0},{24,8},{1,17},{9,25},{17,1},{25,9},{2,18},{10... | collective-permute-start | bytes 491528 | tf_op jit(solution)/shard_map/ppermute | solution.py:258
  73.5 12.5 %collective-permute-start.2 = (bf16[48,512]{1,0:T(8,128)(2,1)S(1)}, bf16[48,512]{1,0:T(8,128)(2,1)S(1)}, u32[]{:S(2)}, u32[]{:S(2)}) collective-permute-start(bf16[48,512]{1,0:T(8,128)(2,1)S(1)} %far_total.1), channel_id=1, source_target_pairs={{0,4},{4,0},{1,5},{5,1},{2,6},{6,2},{3,7},{7,3},{8,12},{12,8},{9,1... | collective-permute-start | bytes 147464 | tf_op jit(solution)/shard_map/ppermute | solution.py:279

commit v8 on v6

--- a/solution.py
+++ b/solution.py
@@ -9,6 +9,7 @@
 HQ = 4
 WIDTH = HQ * DH
 STATS = 4 * HQ
+GROUP = 2
 SCALE = DH**-0.5
 LOG2E = 1.4426950408889634
 BF = jnp.bfloat16
@@ -93,13 +94,14 @@
             q_s[to, DH:] = mine
             g_s[to, DH:] = mine
 
-    row = lax.broadcasted_iota(jnp.int32, (DH, cols), 0)
+    row = lax.broadcasted_iota(jnp.int32, (DH, GROUP * cols), 0)
     k_ones = jnp.where(row < STATS // 2, 1.0, 0.0).astype(BF)
     v_ones = jnp.where((row >= STATS // 2) & (row < STATS), 1.0, 0.0).astype(BF)
     over_rows = (((0,), (0,)), ((), ()))
-    for j in range(chunks):
-        k = jnp.concatenate([own_ref[j, 0], other_ref[j, 0]], 0)
-        v = jnp.concatenate([own_ref[j, 1], other_ref[j, 1]], 0)
+    for j in range(0, chunks, GROUP):
+        group = range(j, j + GROUP)
+        k = jnp.concatenate([jnp.concatenate([own_ref[i, 0], other_ref[i, 0]], 0) for i in group], 1)
+        v = jnp.concatenate([jnp.concatenate([own_ref[i, 1], other_ref[i, 1]], 0) for i in group], 1)
         s = jnp.dot(q_s[...], jnp.concatenate([k, k_ones], 0), preferred_element_type=F32)
         p = jnp.exp2(s * (SCALE * LOG2E))
         dp = jnp.dot(g_s[...], jnp.concatenate([v, v_ones], 0), preferred_element_type=F32)
@@ -108,10 +110,11 @@
         dv = lax.dot_general(g_s[:, :DH], pb, over_rows, preferred_element_type=F32)
         dk = lax.dot_general(q_s[:, :DH], ds, over_rows, preferred_element_type=F32) * SCALE
         dq = lax.dot_general(ds, k, (((1,), (1,)), ((), ())), preferred_element_type=F32) * SCALE
-        held[j, 0] = dk
-        held[j, 1] = dv
-        if not last:
-            copies[j].start()
+        for n, i in enumerate(group):
+            held[i, 0] = dk[:, n * cols : (n + 1) * cols]
+            held[i, 1] = dv[:, n * cols : (n + 1) * cols]
+            if not last:
+                copies[i].start()
         if j == 0:
             acc[...] = dq
         else:

time: 84.7 us -> 84 us (level)
  no operation moved by 1% of the time
where the time goes in v8:
time: 84 us; the launch traced here: 83.4 us
  starting transfers between devices  40.5 us (48%)
  Pallas kernels  15.2 us (18%)
  blocking collectives  13.8 us (16%)
  waiting for transfers between devices  11.5 us (14%)
  local copies, waits for them, and re-layouts  1.66 us (2%)
    all_gather x1, blocking collectives, per_device(): own = lax.all_gather(kv, 'y')  13.8 us
    pallas_call x2, Pallas kernels, grads(): pl.pallas_call(lambda *refs: grads_kernel(last, *refs), in_specs=in_specs...  11.4 us
    ppermute x3, starting transfers between devices, along(): lax.ppermute(value, axis, [(i, (i + steps) % count) for i in range(count)])  10.9 us
    ppermute x1, starting transfers between devices, per_device(): far = lax.ppermute(x, 'zq', SWAP)  9.08 us
    all_to_all x1, starting transfers between devices, per_device(): x_near = lax.all_to_all(copies, 'zi', 0, 0)  5.89 us
    all_to_all x1, starting transfers between devices, per_device(): x_far = lax.all_to_all(jnp.broadcast_to(far, copies.shape), 'zi', 0, 0)  5.37 us
    all_to_all x1, starting transfers between devices, per_device(): query_grad = query_total(core, lax.all_to_all(dq, ('zq', 'zi'), 0, 0))  5.34 us
    ppermute x3, waiting for transfers between devices, along(): lax.ppermute(value, axis, [(i, (i + steps) % count) for i in range(count)])  5.24 us
  transfers between devices with their start and end apart: 9, of which 5 were waited for; matrix products, arithmetic and copies ran while one was open for 0% of the time, Pallas kernels for 8%

profile of v8, /device:TPU:6, one launch (start us, length us, event | category | flops | bytes accessed | tf_op | source)
XLA Modules:
  0.0 83.4 jit_solution(4386455967829813347)
XLA Ops:
  0.6 2.3 %prep.1 = (bf16[400,128]{1,0:T(8,128)(2,1)}, bf16[4,400,128]{2,1,0:T(8,128)(2,1)}, bf16[2,64,640]{2,1,0:T(8,128)(2,1)}) custom-call(s32[1]{0:T(128)} %bitcast.core_ref, bf16[48,512]{1,0:T(8,128)(2,1)} %q_ref.1, bf16[48,512]{1,0:T(8,128)(2,1)} %g_ref.1, bf16[48,512]{1,0:T(8,128)(2,1)} %o_ref.1, f32[4,48]{1,0:T(4,128)} %bitcast.9, bf16[64,640]{1,0:T(8,128)(2,1)} %k_ref.1, ...), custom_call_target="tpu_custom_call" | custom-call | tf_op jit(solution)/shard_map/prep/pallas_call | solution.py:57
  2.9 5.9 %all-to-all-start.1 = ((bf16[4,400,128]{2,1,0:T(8,128)(2,1)}), bf16[4,400,128]{2,1,0:T(8,128)(2,1)S(1)}, u32[]{:S(2)}, u32[]{:S(2)}) async-start(bf16[4,400,128]{2,1,0:T(8,128)(2,1)} %get-tuple-element.23), calls=%async_computation.1 | async-start | bytes 819200 | tf_op jit(solution)/shard_map/all_to_all | solution.py:255
  8.8 9.1 %collective-permute-start = (bf16[400,128]{1,0:T(8,128)(2,1)}, bf16[400,128]{1,0:T(8,128)(2,1)S(1)}, u32[]{:S(2)}, u32[]{:S(2)}) collective-permute-start(bf16[400,128]{1,0:T(8,128)(2,1)} %get-tuple-element.19), channel_id=1, source_target_pairs={{0,4},{4,0},{1,5},{5,1},{2,6},{6,2},{3,7},{7,3},{8,12},{12,8},{9,1... | collective-permute-start | bytes 307208 | tf_op jit(solution)/shard_map/ppermute | solution.py:254
  17.9 13.8 %all-gather = bf16[8,64,640]{2,1,0:T(8,128)(2,1)S(1)} all-gather(bf16[2,64,640]{2,1,0:T(8,128)(2,1)} %get-tuple-element.20), channel_id=2, replica_groups=mesh['zh'=2,'x'=4,'core'=2,'y'=4,'zq'=2,'zi'=4] {'y'}, dimensions={0}, use_global_device_ids=true | all-gather | bytes 819200 | tf_op jit(solution)/shard_map/all_gather | solution.py:257
  31.7 0.0 collective-permute-done
  31.7 0.0 all-to-all-done.1.refs_0_
  31.7 0.8 broadcast_in_dim.3
  32.5 5.4 %all-to-all-start = ((bf16[4,400,128]{2,1,0:T(8,128)(2,1)}), bf16[4,400,128]{2,1,0:T(8,128)(2,1)S(1)}, u32[]{:S(2)}, u32[]{:S(2)}) async-start(bf16[4,400,128]{2,1,0:T(8,128)(2,1)} %broadcast_in_dim.3), calls=%async_computation | async-start | bytes 819200 | tf_op jit(solution)/shard_map/all_to_all | solution.py:260
  37.9 1.9 %collective-permute-start.1 = (bf16[4,2,64,640]{3,2,1,0:T(8,128)(2,1)S(1)}, bf16[4,2,64,640]{3,2,1,0:T(8,128)(2,1)S(1)}, u32[]{:S(2)}, u32[]{:S(2)}) collective-permute-start(bf16[4,2,64,640]{3,2,1,0:T(8,128)(2,1)S(1)} %bitcast.6), channel_id=1, source_target_pairs={{0,32},{32,0},{1,33},{33,1},{2,34},{34,2},{3,35},{35,3},{4,36},{36... | collective-permute-start | bytes 1966088 | tf_op jit(solution)/shard_map/ppermute | solution.py:259
  39.8 2.1 %collective-permute-done.1.refs_2_.refs_3_ = bf16[4,2,64,640]{3,2,1,0:T(8,128)(2,1)S(1)} collective-permute-done((bf16[4,2,64,640]{3,2,1,0:T(8,128)(2,1)S(1)}, bf16[4,2,64,640]{3,2,1,0:T(8,128)(2,1)S(1)}, u32[]{:S(2)}, u32[]{:S(2)}) %collective-permute-start.1) | collective-permute-done | bytes 655392 | tf_op jit(solution)/shard_map/ppermute | solution.py:259
  41.9 5.4 %grads.2 = (bf16[4,48,512]{2,1,0:T(8,128)(2,1)S(1)}, f32[40,2,128,640]{3,2,1,0:T(8,128)}) custom-call(bf16[4,400,128]{2,1,0:T(8,128)(2,1)S(1)} %all-to-all-done.1.refs_0_, bf16[4,2,64,640]{3,2,1,0:T(8,128)(2,1)S(1)} %bitcast.7, bf16[4,2,64,640]{3,2,1,0:T(8,128)(2,1)S(1)} %collective-permute-done.1.refs_2_.refs_3_), custom_call_target="tpu_custom_call" | custom-call | flops 2516582400 | bytes 4194304 | tf_op jit(solution)/shard_map/grads/pallas_call | solution.py:168
  47.3 0.0 all-to-all-done.refs_1_
  47.4 6.0 %grads.3 = (bf16[2,4,48,512]{3,2,1,0:T(8,128)(2,1)}, f32[4,2,64,640]{3,2,1,0:T(8,128)S(1)}, bf16[4,2,64,640]{3,2,1,0:T(8,128)(2,1)S(1)}) custom-call(s32[1]{0:T(128)} %bitcast.1.refs_0_, bf16[4,400,128]{2,1,0:T(8,128)(2,1)S(1)} %all-to-all-done.refs_1_, bf16[4,2,64,640]{3,2,1,0:T(8,128)(2,1)S(1)} %bitcast.8, ...), custom_call_target="tpu_custom_call" | custom-call | flops 2516582400 | bytes 4194304 | tf_op jit(solution)/shard_map/grads/pallas_call | solution.py:168
  53.3 0.0 copy-start
  53.3 0.8 copy-done
  54.2 5.3 %all-to-all-start.2 = ((bf16[8,48,512]{2,1,0:T(8,128)(2,1)}), bf16[8,48,512]{2,1,0:T(8,128)(2,1)S(1)}, u32[]{:S(2)}, u32[]{:S(2)}) async-start(bf16[8,48,512]{2,1,0:T(8,128)(2,1)} %bitcast.4), calls=%async_computation.2 | async-start | bytes 786432 | tf_op jit(solution)/shard_map/all_to_all | solution.py:265
  59.5 1.9 %collective-permute-start.2 = (bf16[4,2,64,640]{3,2,1,0:T(8,128)(2,1)}, bf16[4,2,64,640]{3,2,1,0:T(8,128)(2,1)S(1)}, u32[]{:S(2)}, u32[]{:S(2)}) collective-permute-start(bf16[4,2,64,640]{3,2,1,0:T(8,128)(2,1)} %copy-done), channel_id=1, source_target_pairs={{0,32},{32,0},{1,33},{33,1},{2,34},{34,2},{3,35},{35,3},{4,36},{36... | collective-permute-start | bytes 1966088 | tf_op jit(solution)/shard_map/ppermute | solution.py:267
  61.4 2.3 %collective-permute-done.2.got_ref = bf16[4,2,64,640]{3,2,1,0:T(8,128)(2,1)S(1)} collective-permute-done((bf16[4,2,64,640]{3,2,1,0:T(8,128)(2,1)}, bf16[4,2,64,640]{3,2,1,0:T(8,128)(2,1)S(1)}, u32[]{:S(2)}, u32[]{:S(2)}) %collective-permute-start.2) | collective-permute-done | bytes 655392 | tf_op jit(solution)/shard_map/ppermute | solution.py:267
  63.7 0.1 both_cores.1
  63.8 3.5 %collective-permute-start.3 = (bf16[2,64,640]{2,1,0:T(8,128)(2,1)S(1)}, bf16[2,64,640]{2,1,0:T(8,128)(2,1)S(1)}, u32[]{:S(2)}, u32[]{:S(2)}) collective-permute-start(bf16[2,64,640]{2,1,0:T(8,128)(2,1)S(1)} %get-tuple-element.30), channel_id=1, source_target_pairs={{0,8},{8,16},{16,24},{24,0},{1,9},{9,17},{17,25},{25,1},{2,10},{10... | collective-permute-start | bytes 491528 | tf_op jit(solution)/shard_map/ppermute | solution.py:243
  67.3 3.6 %collective-permute-start.4 = (bf16[2,64,640]{2,1,0:T(8,128)(2,1)S(1)}, bf16[2,64,640]{2,1,0:T(8,128)(2,1)S(1)}, u32[]{:S(2)}, u32[]{:S(2)}) collective-permute-start(bf16[2,64,640]{2,1,0:T(8,128)(2,1)S(1)} %get-tuple-element.31), channel_id=1, source_target_pairs={{0,24},{8,0},{16,8},{24,16},{1,25},{9,1},{17,9},{25,17},{2,26},{10... | collective-permute-start | bytes 491528 | tf_op jit(solution)/shard_map/ppermute | solution.py:243
  70.9 3.9 %collective-permute-start.5 = (bf16[2,64,640]{2,1,0:T(8,128)(2,1)S(1)}, bf16[2,64,640]{2,1,0:T(8,128)(2,1)S(1)}, u32[]{:S(2)}, u32[]{:S(2)}) collective-permute-start(bf16[2,64,640]{2,1,0:T(8,128)(2,1)S(1)} %get-tuple-element.32), channel_id=1, source_target_pairs={{0,16},{8,24},{16,0},{24,8},{1,17},{9,25},{17,1},{25,9},{2,18},{10... | collective-permute-start | bytes 491528 | tf_op jit(solution)/shard_map/ppermute | solution.py:243
  74.8 0.0 collective-permute-done.3.refs_1_
  74.8 0.4 collective-permute-done.4.refs_2_
  75.2 4.9 %collective-permute-done.5.refs_3_ = bf16[2,64,640]{2,1,0:T(8,128)(2,1)S(1)} collective-permute-done((bf16[2,64,640]{2,1,0:T(8,128)(2,1)S(1)}, bf16[2,64,640]{2,1,0:T(8,128)(2,1)S(1)}, u32[]{:S(2)}, u32[]{:S(2)}) %collective-permute-start.5) | collective-permute-done | bytes 163872 | tf_op jit(solution)/shard_map/ppermute | solution.py:243
  80.0 0.7 visual_total.1
  80.8 1.9 %all-to-all-done.2.parts_ref = bf16[8,48,512]{2,1,0:T(8,128)(2,1)S(1)} async-done(((bf16[8,48,512]{2,1,0:T(8,128)(2,1)}), bf16[8,48,512]{2,1,0:T(8,128)(2,1)S(1)}, u32[]{:S(2)}, u32[]{:S(2)}) %all-to-all-start.2) | async-done | bytes 393248 | tf_op jit(solution)/shard_map/all_to_all | solution.py:265
  82.7 0.7 query_total.1
Async XLA Ops:
  2.9 28.8 %all-to-all-start.1 = ((bf16[4,400,128]{2,1,0:T(8,128)(2,1)}), bf16[4,400,128]{2,1,0:T(8,128)(2,1)S(1)}, u32[]{:S(2)}, u32[]{:S(2)}) async-start(bf16[4,400,128]{2,1,0:T(8,128)(2,1)} %get-tuple-element.23), calls=%async_computation.1 | async-start | bytes 819200 | tf_op jit(solution)/shard_map/all_to_all | solution.py:255
  8.8 22.9 %collective-permute-start = (bf16[400,128]{1,0:T(8,128)(2,1)}, bf16[400,128]{1,0:T(8,128)(2,1)S(1)}, u32[]{:S(2)}, u32[]{:S(2)}) collective-permute-start(bf16[400,128]{1,0:T(8,128)(2,1)} %get-tuple-element.19), channel_id=1, source_target_pairs={{0,4},{4,0},{1,5},{5,1},{2,6},{6,2},{3,7},{7,3},{8,12},{12,8},{9,1... | collective-permute-start | bytes 307208 | tf_op jit(solution)/shard_map/ppermute | solution.py:254
  32.5 14.8 %all-to-all-start = ((bf16[4,400,128]{2,1,0:T(8,128)(2,1)}), bf16[4,400,128]{2,1,0:T(8,128)(2,1)S(1)}, u32[]{:S(2)}, u32[]{:S(2)}) async-start(bf16[4,400,128]{2,1,0:T(8,128)(2,1)} %broadcast_in_dim.3), calls=%async_computation | async-start | bytes 819200 | tf_op jit(solution)/shard_map/all_to_all | solution.py:260
  37.9 4.0 %collective-permute-start.1 = (bf16[4,2,64,640]{3,2,1,0:T(8,128)(2,1)S(1)}, bf16[4,2,64,640]{3,2,1,0:T(8,128)(2,1)S(1)}, u32[]{:S(2)}, u32[]{:S(2)}) collective-permute-start(bf16[4,2,64,640]{3,2,1,0:T(8,128)(2,1)S(1)} %bitcast.6), channel_id=1, source_target_pairs={{0,32},{32,0},{1,33},{33,1},{2,34},{34,2},{3,35},{35,3},{4,36},{36... | collective-permute-start | bytes 1966088 | tf_op jit(solution)/shard_map/ppermute | solution.py:259
  53.3 0.8 %copy-start = (bf16[4,2,64,640]{3,2,1,0:T(8,128)(2,1)}, bf16[4,2,64,640]{3,2,1,0:T(8,128)(2,1)S(1)}, u32[]{:S(2)}) copy-start(bf16[4,2,64,640]{3,2,1,0:T(8,128)(2,1)S(1)} %get-tuple-element.28) | copy-start | bytes 1966084
  54.2 28.5 %all-to-all-start.2 = ((bf16[8,48,512]{2,1,0:T(8,128)(2,1)}), bf16[8,48,512]{2,1,0:T(8,128)(2,1)S(1)}, u32[]{:S(2)}, u32[]{:S(2)}) async-start(bf16[8,48,512]{2,1,0:T(8,128)(2,1)} %bitcast.4), calls=%async_computation.2 | async-start | bytes 786432 | tf_op jit(solution)/shard_map/all_to_all | solution.py:265
  59.5 4.2 %collective-permute-start.2 = (bf16[4,2,64,640]{3,2,1,0:T(8,128)(2,1)}, bf16[4,2,64,640]{3,2,1,0:T(8,128)(2,1)S(1)}, u32[]{:S(2)}, u32[]{:S(2)}) collective-permute-start(bf16[4,2,64,640]{3,2,1,0:T(8,128)(2,1)} %copy-done), channel_id=1, source_target_pairs={{0,32},{32,0},{1,33},{33,1},{2,34},{34,2},{3,35},{35,3},{4,36},{36... | collective-permute-start | bytes 1966088 | tf_op jit(solution)/shard_map/ppermute | solution.py:267
  63.8 11.0 %collective-permute-start.3 = (bf16[2,64,640]{2,1,0:T(8,128)(2,1)S(1)}, bf16[2,64,640]{2,1,0:T(8,128)(2,1)S(1)}, u32[]{:S(2)}, u32[]{:S(2)}) collective-permute-start(bf16[2,64,640]{2,1,0:T(8,128)(2,1)S(1)} %get-tuple-element.30), channel_id=1, source_target_pairs={{0,8},{8,16},{16,24},{24,0},{1,9},{9,17},{17,25},{25,1},{2,10},{10... | collective-permute-start | bytes 491528 | tf_op jit(solution)/shard_map/ppermute | solution.py:243
  67.3 7.9 %collective-permute-start.4 = (bf16[2,64,640]{2,1,0:T(8,128)(2,1)S(1)}, bf16[2,64,640]{2,1,0:T(8,128)(2,1)S(1)}, u32[]{:S(2)}, u32[]{:S(2)}) collective-permute-start(bf16[2,64,640]{2,1,0:T(8,128)(2,1)S(1)} %get-tuple-element.31), channel_id=1, source_target_pairs={{0,24},{8,0},{16,8},{24,16},{1,25},{9,1},{17,9},{25,17},{2,26},{10... | collective-permute-start | bytes 491528 | tf_op jit(solution)/shard_map/ppermute | solution.py:243
  70.9 9.2 %collective-permute-start.5 = (bf16[2,64,640]{2,1,0:T(8,128)(2,1)S(1)}, bf16[2,64,640]{2,1,0:T(8,128)(2,1)S(1)}, u32[]{:S(2)}, u32[]{:S(2)}) collective-permute-start(bf16[2,64,640]{2,1,0:T(8,128)(2,1)S(1)} %get-tuple-element.32), channel_id=1, source_target_pairs={{0,16},{8,24},{16,0},{24,8},{1,17},{9,25},{17,1},{25,9},{2,18},{10... | collective-permute-start | bytes 491528 | tf_op jit(solution)/shard_map/ppermute | solution.py:243

commit v9 on v8

--- a/solution.py
+++ b/solution.py
@@ -26,7 +26,7 @@
     return jnp.where(core == 0, value, rolled)
 
 
-def prep_kernel(core_ref, q_ref, g_ref, o_ref, lse_ref, k_ref, v_ref, x_ref, copies_ref, kv_ref):
+def prep_kernel(core_ref, q_ref, g_ref, o_ref, lse_ref, k_ref, v_ref, x_ref, kv_ref):
     core = core_ref[0]
     rows = q_ref.shape[0]
     lane = lax.broadcasted_iota(jnp.int32, (rows, DH), 1)
@@ -46,10 +46,9 @@
     stats = jnp.where((lane & HQ) == 0, high, stats - high)
     stats = jnp.concatenate([stats, jnp.zeros((DH - rows, DH), F32)], 0)
     x_ref[2 * HQ * rows :, :] = jnp.transpose(stats)[:STATS].astype(BF)
-    for b in range(copies_ref.shape[0]):
-        copies_ref[b] = x_ref[...]
-    kv_ref[0] = k_ref[...]
-    kv_ref[1] = v_ref[...]
+    for y in range(kv_ref.shape[0]):
+        kv_ref[y, 0] = k_ref[...]
+        kv_ref[y, 1] = v_ref[...]
 
 
 def prep(core, queries, out_grad, outputs, lse_t, keys, values):
@@ -59,8 +58,7 @@
         in_specs=[pl.BlockSpec(memory_space=pltpu.SMEM)] + [pl.BlockSpec(memory_space=pltpu.VMEM)] * 6,
         out_shape=[
             jax.ShapeDtypeStruct((2 * HQ * rows + STATS, DH), BF),
-            jax.ShapeDtypeStruct((lax.axis_size("zi"), 2 * HQ * rows + STATS, DH), BF),
-            jax.ShapeDtypeStruct((2,) + keys.shape, BF),
+            jax.ShapeDtypeStruct((lax.axis_size("y"), 2) + keys.shape, BF),
         ],
         name="prep",
     )(core, queries, out_grad, outputs, lse_t, keys, values)
@@ -249,15 +247,14 @@
 
 def per_device(queries, keys, values, outputs, out_grad, logsumexp):
     core = index("core")
-    x, copies, kv = prep(core, queries, out_grad, outputs, logsumexp.T, keys, values)
-
+    x, kv = prep(core, queries, out_grad, outputs, logsumexp.T, keys, values)
+
+    own = lax.all_to_all(kv, "y", 0, 0)
     far = lax.ppermute(x, "zq", SWAP)
-    x_near = lax.all_to_all(copies, "zi", 0, 0)
-
-    own = lax.all_gather(kv, "y")
-    far, own = lax.optimization_barrier((far, own))
+    x_near = lax.all_gather(x, "zi")
+    far, x_near, own = lax.optimization_barrier((far, x_near, own))
     other = lax.ppermute(own, "core", SWAP)
-    x_far = lax.all_to_all(jnp.broadcast_to(far, copies.shape), "zi", 0, 0)
+    x_far = lax.all_to_all(jnp.broadcast_to(far, x_near.shape), "zi", 0, 0)
 
     before = grads(x_near, own, other)
     dq, keep, send = grads(x_far, own, other, index("zq"), before)

time: 84 us -> 90.2 us (1.074)
  the two profiles are of different devices: /device:TPU:6 before, /device:TPU:8 now
where the time goes in v9:
time: 90.2 us; the launch traced here: 89.7 us
  starting transfers between devices  40.4 us (45%)
  blocking collectives  17.4 us (19%)
  Pallas kernels  15.2 us (17%)
  waiting for transfers between devices  14.3 us (16%)
  local copies, waits for them, and re-layouts  1.66 us (2%)
    all_gather x1, blocking collectives, per_device(): x_near = lax.all_gather(x, 'zi')  17.4 us
    pallas_call x2, Pallas kernels, grads(): pl.pallas_call(lambda *refs: grads_kernel(last, *refs), in_specs=in_specs...  11.4 us
    ppermute x3, starting transfers between devices, along(): lax.ppermute(value, axis, [(i, (i + steps) % count) for i in range(count)])  9.82 us
    all_to_all x1, starting transfers between devices, per_device(): own = lax.all_to_all(kv, 'y', 0, 0)  9.27 us
    all_to_all x1, starting transfers between devices, per_device(): query_grad = query_total(core, lax.all_to_all(dq, ('zq', 'zi'), 0, 0))  7.67 us
    ppermute x3, waiting for transfers between devices, along(): lax.ppermute(value, axis, [(i, (i + steps) % count) for i in range(count)])  5.5 us
    all_to_all x1, starting transfers between devices, per_device(): x_far = lax.all_to_all(jnp.broadcast_to(far, x_near.shape), 'zi', 0, 0)  5.05 us
    ppermute x1, starting transfers between devices, per_device(): far = lax.ppermute(x, 'zq', SWAP)  4.72 us
  transfers between devices with their start and end apart: 9, of which 6 were waited for; matrix products, arithmetic and copies ran while one was open for 0% of the time, Pallas kernels for 7%

profile of v9, /device:TPU:8, one launch (start us, length us, event | category | flops | bytes accessed | tf_op | source)
XLA Modules:
  0.0 89.7 jit_solution(2059510198497557442)
XLA Ops:
  0.6 2.3 %prep.1 = (bf16[400,128]{1,0:T(8,128)(2,1)}, bf16[4,2,64,640]{3,2,1,0:T(8,128)(2,1)}) custom-call(s32[1]{0:T(128)} %bitcast.core_ref, bf16[48,512]{1,0:T(8,128)(2,1)} %q_ref.1, bf16[48,512]{1,0:T(8,128)(2,1)} %g_ref.1, bf16[48,512]{1,0:T(8,128)(2,1)} %o_ref.1, f32[4,48]{1,0:T(4,128)} %bitcast.7, bf16[64,640]{1,0:T(8,128)(2,1)} %k_ref.1, bf16[64,640]{1,0:T(8,128)(2,1)} %v_ref.1), custom_call_target="tpu_custom_call" | custom-call | tf_op jit(solution)/shard_map/prep/pallas_call | solution.py:56
  2.9 9.3 %all-to-all-start = ((bf16[4,2,64,640]{3,2,1,0:T(8,128)(2,1)}), bf16[4,2,64,640]{3,2,1,0:T(8,128)(2,1)S(1)}, u32[]{:S(2)}, u32[]{:S(2)}) async-start(bf16[4,2,64,640]{3,2,1,0:T(8,128)(2,1)} %get-tuple-element.20), calls=%async_computation | async-start | bytes 1310720 | tf_op jit(solution)/shard_map/all_to_all | solution.py:252
  12.2 4.7 %collective-permute-start = (bf16[400,128]{1,0:T(8,128)(2,1)}, bf16[400,128]{1,0:T(8,128)(2,1)S(1)}, u32[]{:S(2)}, u32[]{:S(2)}) collective-permute-start(bf16[400,128]{1,0:T(8,128)(2,1)} %get-tuple-element.19), channel_id=1, source_target_pairs={{0,4},{4,0},{1,5},{5,1},{2,6},{6,2},{3,7},{7,3},{8,12},{12,8},{9,1... | collective-permute-start | bytes 307208 | tf_op jit(solution)/shard_map/ppermute | solution.py:253
  16.9 17.4 %all-gather = bf16[1600,128]{1,0:T(8,128)(2,1)S(1)} all-gather(bf16[400,128]{1,0:T(8,128)(2,1)} %get-tuple-element.19), channel_id=2, replica_groups=mesh['zh'=2,'x'=4,'core'=2,'y'=4,'zq'=2,'zi'=4] {'zi'}, dimensions={0}, use_global_device_ids=true | all-gather | bytes 512000 | tf_op jit(solution)/shard_map/all_gather | solution.py:254
  34.3 0.0 collective-permute-done
  34.3 0.0 all-to-all-done.refs_1_.refs_2_
  34.3 0.8 broadcast_in_dim.3
  35.2 5.1 %all-to-all-start.1 = ((bf16[4,400,128]{2,1,0:T(8,128)(2,1)}), bf16[4,400,128]{2,1,0:T(8,128)(2,1)S(1)}, u32[]{:S(2)}, u32[]{:S(2)}) async-start(bf16[4,400,128]{2,1,0:T(8,128)(2,1)} %broadcast_in_dim.3), calls=%async_computation.1 | async-start | bytes 819200 | tf_op jit(solution)/shard_map/all_to_all | solution.py:257
  40.2 1.9 %collective-permute-start.1 = (bf16[4,2,64,640]{3,2,1,0:T(8,128)(2,1)S(1)}, bf16[4,2,64,640]{3,2,1,0:T(8,128)(2,1)S(1)}, u32[]{:S(2)}, u32[]{:S(2)}) collective-permute-start(bf16[4,2,64,640]{3,2,1,0:T(8,128)(2,1)S(1)} %all-to-all-done.refs_1_.refs_2_), channel_id=1, source_target_pairs={{0,32},{32,0},{1,33},{33,1},{2,34},{34,2},{3,35},{35,3},{4,36},{36... | collective-permute-start | bytes 1966088 | tf_op jit(solution)/shard_map/ppermute | solution.py:256
  42.1 2.1 %collective-permute-done.1.refs_2_.refs_3_ = bf16[4,2,64,640]{3,2,1,0:T(8,128)(2,1)S(1)} collective-permute-done((bf16[4,2,64,640]{3,2,1,0:T(8,128)(2,1)S(1)}, bf16[4,2,64,640]{3,2,1,0:T(8,128)(2,1)S(1)}, u32[]{:S(2)}, u32[]{:S(2)}) %collective-permute-start.1) | collective-permute-done | bytes 655392 | tf_op jit(solution)/shard_map/ppermute | solution.py:256
  44.2 5.4 %grads.2 = (bf16[4,48,512]{2,1,0:T(8,128)(2,1)S(1)}, f32[40,2,128,640]{3,2,1,0:T(8,128)}) custom-call(bf16[4,400,128]{2,1,0:T(8,128)(2,1)S(1)} %bitcast.6, bf16[4,2,64,640]{3,2,1,0:T(8,128)(2,1)S(1)} %all-to-all-done.refs_1_.refs_2_, bf16[4,2,64,640]{3,2,1,0:T(8,128)(2,1)S(1)} %collective-permute-done.1.refs_2_.refs_3_), custom_call_target="tpu_custom_call" | custom-call | flops 2516582400 | bytes 4194304 | tf_op jit(solution)/shard_map/grads/pallas_call | solution.py:166
  49.6 1.4 %all-to-all-done.1.refs_1_ = bf16[4,400,128]{2,1,0:T(8,128)(2,1)S(1)} async-done(((bf16[4,400,128]{2,1,0:T(8,128)(2,1)}), bf16[4,400,128]{2,1,0:T(8,128)(2,1)S(1)}, u32[]{:S(2)}, u32[]{:S(2)}) %all-to-all-start.1) | async-done | bytes 409632 | tf_op jit(solution)/shard_map/all_to_all | solution.py:257
  51.0 6.0 %grads.3 = (bf16[2,4,48,512]{3,2,1,0:T(8,128)(2,1)}, f32[4,2,64,640]{3,2,1,0:T(8,128)S(1)}, bf16[4,2,64,640]{3,2,1,0:T(8,128)(2,1)S(1)}) custom-call(s32[1]{0:T(128)} %bitcast.1.refs_0_, bf16[4,400,128]{2,1,0:T(8,128)(2,1)S(1)} %all-to-all-done.1.refs_1_, bf16[4,2,64,640]{3,2,1,0:T(8,128)(2,1)S(1)} %all-to-all-done.refs_1_.refs_2_, ...), custom_call_target="tpu_custom_call" | custom-call | flops 2516582400 | bytes 4194304 | tf_op jit(solution)/shard_map/grads/pallas_call | solution.py:166
  57.0 0.0 copy-start
  57.0 0.8 copy-done
  57.8 7.7 %all-to-all-start.2 = ((bf16[8,48,512]{2,1,0:T(8,128)(2,1)}), bf16[8,48,512]{2,1,0:T(8,128)(2,1)S(1)}, u32[]{:S(2)}, u32[]{:S(2)}) async-start(bf16[8,48,512]{2,1,0:T(8,128)(2,1)} %bitcast.4), calls=%async_computation.2 | async-start | bytes 786432 | tf_op jit(solution)/shard_map/all_to_all | solution.py:262
  65.5 1.9 %collective-permute-start.2 = (bf16[4,2,64,640]{3,2,1,0:T(8,128)(2,1)}, bf16[4,2,64,640]{3,2,1,0:T(8,128)(2,1)S(1)}, u32[]{:S(2)}, u32[]{:S(2)}) collective-permute-start(bf16[4,2,64,640]{3,2,1,0:T(8,128)(2,1)} %copy-done), channel_id=1, source_target_pairs={{0,32},{32,0},{1,33},{33,1},{2,34},{34,2},{3,35},{35,3},{4,36},{36... | collective-permute-start | bytes 1966088 | tf_op jit(solution)/shard_map/ppermute | solution.py:264
  67.4 2.3 %collective-permute-done.2.got_ref = bf16[4,2,64,640]{3,2,1,0:T(8,128)(2,1)S(1)} collective-permute-done((bf16[4,2,64,640]{3,2,1,0:T(8,128)(2,1)}, bf16[4,2,64,640]{3,2,1,0:T(8,128)(2,1)S(1)}, u32[]{:S(2)}, u32[]{:S(2)}) %collective-permute-start.2) | collective-permute-done | bytes 655392 | tf_op jit(solution)/shard_map/ppermute | solution.py:264
  69.7 0.1 both_cores.1
  69.8 3.4 %collective-permute-start.3 = (bf16[2,64,640]{2,1,0:T(8,128)(2,1)S(1)}, bf16[2,64,640]{2,1,0:T(8,128)(2,1)S(1)}, u32[]{:S(2)}, u32[]{:S(2)}) collective-permute-start(bf16[2,64,640]{2,1,0:T(8,128)(2,1)S(1)} %get-tuple-element.30), channel_id=1, source_target_pairs={{0,8},{8,16},{16,24},{24,0},{1,9},{9,17},{17,25},{25,1},{2,10},{10... | collective-permute-start | bytes 491528 | tf_op jit(solution)/shard_map/ppermute | solution.py:241
  73.2 2.5 %collective-permute-start.4 = (bf16[2,64,640]{2,1,0:T(8,128)(2,1)S(1)}, bf16[2,64,640]{2,1,0:T(8,128)(2,1)S(1)}, u32[]{:S(2)}, u32[]{:S(2)}) collective-permute-start(bf16[2,64,640]{2,1,0:T(8,128)(2,1)S(1)} %get-tuple-element.31), channel_id=1, source_target_pairs={{0,24},{8,0},{16,8},{24,16},{1,25},{9,1},{17,9},{25,17},{2,26},{10... | collective-permute-start | bytes 491528 | tf_op jit(solution)/shard_map/ppermute | solution.py:241
  75.7 4.0 %collective-permute-start.5 = (bf16[2,64,640]{2,1,0:T(8,128)(2,1)S(1)}, bf16[2,64,640]{2,1,0:T(8,128)(2,1)S(1)}, u32[]{:S(2)}, u32[]{:S(2)}) collective-permute-start(bf16[2,64,640]{2,1,0:T(8,128)(2,1)S(1)} %get-tuple-element.32), channel_id=1, source_target_pairs={{0,16},{8,24},{16,0},{24,8},{1,17},{9,25},{17,1},{25,9},{2,18},{10... | collective-permute-start | bytes 491528 | tf_op jit(solution)/shard_map/ppermute | solution.py:241
  79.7 0.0 collective-permute-done.3.refs_1_
  79.7 1.4 %collective-permute-done.4.refs_2_ = bf16[2,64,640]{2,1,0:T(8,128)(2,1)S(1)} collective-permute-done((bf16[2,64,640]{2,1,0:T(8,128)(2,1)S(1)}, bf16[2,64,640]{2,1,0:T(8,128)(2,1)S(1)}, u32[]{:S(2)}, u32[]{:S(2)}) %collective-permute-start.4) | collective-permute-done | bytes 163872 | tf_op jit(solution)/shard_map/ppermute | solution.py:241
  81.1 4.1 %collective-permute-done.5.refs_3_ = bf16[2,64,640]{2,1,0:T(8,128)(2,1)S(1)} collective-permute-done((bf16[2,64,640]{2,1,0:T(8,128)(2,1)S(1)}, bf16[2,64,640]{2,1,0:T(8,128)(2,1)S(1)}, u32[]{:S(2)}, u32[]{:S(2)}) %collective-permute-start.5) | collective-permute-done | bytes 163872 | tf_op jit(solution)/shard_map/ppermute | solution.py:241
  85.2 0.7 visual_total.1
  85.9 3.0 %all-to-all-done.2.parts_ref = bf16[8,48,512]{2,1,0:T(8,128)(2,1)S(1)} async-done(((bf16[8,48,512]{2,1,0:T(8,128)(2,1)}), bf16[8,48,512]{2,1,0:T(8,128)(2,1)S(1)}, u32[]{:S(2)}, u32[]{:S(2)}) %all-to-all-start.2) | async-done | bytes 393248 | tf_op jit(solution)/shard_map/all_to_all | solution.py:262
  88.9 0.7 query_total.1
Async XLA Ops:
  2.9 31.4 %all-to-all-start = ((bf16[4,2,64,640]{3,2,1,0:T(8,128)(2,1)}), bf16[4,2,64,640]{3,2,1,0:T(8,128)(2,1)S(1)}, u32[]{:S(2)}, u32[]{:S(2)}) async-start(bf16[4,2,64,640]{3,2,1,0:T(8,128)(2,1)} %get-tuple-element.20), calls=%async_computation | async-start | bytes 1310720 | tf_op jit(solution)/shard_map/all_to_all | solution.py:252
  12.2 22.2 %collective-permute-start = (bf16[400,128]{1,0:T(8,128)(2,1)}, bf16[400,128]{1,0:T(8,128)(2,1)S(1)}, u32[]{:S(2)}, u32[]{:S(2)}) collective-permute-start(bf16[400,128]{1,0:T(8,128)(2,1)} %get-tuple-element.19), channel_id=1, source_target_pairs={{0,4},{4,0},{1,5},{5,1},{2,6},{6,2},{3,7},{7,3},{8,12},{12,8},{9,1... | collective-permute-start | bytes 307208 | tf_op jit(solution)/shard_map/ppermute | solution.py:253
  35.2 15.9 %all-to-all-start.1 = ((bf16[4,400,128]{2,1,0:T(8,128)(2,1)}), bf16[4,400,128]{2,1,0:T(8,128)(2,1)S(1)}, u32[]{:S(2)}, u32[]{:S(2)}) async-start(bf16[4,400,128]{2,1,0:T(8,128)(2,1)} %broadcast_in_dim.3), calls=%async_computation.1 | async-start | bytes 819200 | tf_op jit(solution)/shard_map/all_to_all | solution.py:257
  40.2 4.0 %collective-permute-start.1 = (bf16[4,2,64,640]{3,2,1,0:T(8,128)(2,1)S(1)}, bf16[4,2,64,640]{3,2,1,0:T(8,128)(2,1)S(1)}, u32[]{:S(2)}, u32[]{:S(2)}) collective-permute-start(bf16[4,2,64,640]{3,2,1,0:T(8,128)(2,1)S(1)} %all-to-all-done.refs_1_.refs_2_), channel_id=1, source_target_pairs={{0,32},{32,0},{1,33},{33,1},{2,34},{34,2},{3,35},{35,3},{4,36},{36... | collective-permute-start | bytes 1966088 | tf_op jit(solution)/shard_map/ppermute | solution.py:256
  57.0 0.8 copy-start
  57.8 31.1 %all-to-all-start.2 = ((bf16[8,48,512]{2,1,0:T(8,128)(2,1)}), bf16[8,48,512]{2,1,0:T(8,128)(2,1)S(1)}, u32[]{:S(2)}, u32[]{:S(2)}) async-start(bf16[8,48,512]{2,1,0:T(8,128)(2,1)} %bitcast.4), calls=%async_computation.2 | async-start | bytes 786432 | tf_op jit(solution)/shard_map/all_to_all | solution.py:262
  65.5 4.2 %collective-permute-start.2 = (bf16[4,2,64,640]{3,2,1,0:T(8,128)(2,1)}, bf16[4,2,64,640]{3,2,1,0:T(8,128)(2,1)S(1)}, u32[]{:S(2)}, u32[]{:S(2)}) collective-permute-start(bf16[4,2,64,640]{3,2,1,0:T(8,128)(2,1)} %copy-done), channel_id=1, source_target_pairs={{0,32},{32,0},{1,33},{33,1},{2,34},{34,2},{3,35},{35,3},{4,36},{36... | collective-permute-start | bytes 1966088 | tf_op jit(solution)/shard_map/ppermute | solution.py:264
  69.8 9.8 %collective-permute-start.3 = (bf16[2,64,640]{2,1,0:T(8,128)(2,1)S(1)}, bf16[2,64,640]{2,1,0:T(8,128)(2,1)S(1)}, u32[]{:S(2)}, u32[]{:S(2)}) collective-permute-start(bf16[2,64,640]{2,1,0:T(8,128)(2,1)S(1)} %get-tuple-element.30), channel_id=1, source_target_pairs={{0,8},{8,16},{16,24},{24,0},{1,9},{9,17},{17,25},{25,1},{2,10},{10... | collective-permute-start | bytes 491528 | tf_op jit(solution)/shard_map/ppermute | solution.py:241
  73.2 7.9 %collective-permute-start.4 = (bf16[2,64,640]{2,1,0:T(8,128)(2,1)S(1)}, bf16[2,64,640]{2,1,0:T(8,128)(2,1)S(1)}, u32[]{:S(2)}, u32[]{:S(2)}) collective-permute-start(bf16[2,64,640]{2,1,0:T(8,128)(2,1)S(1)} %get-tuple-element.31), channel_id=1, source_target_pairs={{0,24},{8,0},{16,8},{24,16},{1,25},{9,1},{17,9},{25,17},{2,26},{10... | collective-permute-start | bytes 491528 | tf_op jit(solution)/shard_map/ppermute | solution.py:241
  75.7 9.5 %collective-permute-start.5 = (bf16[2,64,640]{2,1,0:T(8,128)(2,1)S(1)}, bf16[2,64,640]{2,1,0:T(8,128)(2,1)S(1)}, u32[]{:S(2)}, u32[]{:S(2)}) collective-permute-start(bf16[2,64,640]{2,1,0:T(8,128)(2,1)S(1)} %get-tuple-element.32), channel_id=1, source_target_pairs={{0,16},{8,24},{16,0},{24,8},{1,17},{9,25},{17,1},{25,9},{2,18},{10... | collective-permute-start | bytes 491528 | tf_op jit(solution)/shard_map/ppermute | solution.py:241

commit v10 on v8

--- a/solution.py
+++ b/solution.py
@@ -64,6 +64,26 @@
         ],
         name="prep",
     )(core, queries, out_grad, outputs, lse_t, keys, values)
+
+
+def copies_kernel(x_ref, out_ref, sems):
+    copies = [pltpu.make_async_copy(x_ref, out_ref.at[b], sems.at[b]) for b in range(out_ref.shape[0])]
+    for copy in copies:
+        copy.start()
+    for copy in copies:
+        copy.wait()
+
+
+def copies_of(x, count):
+    return pl.pallas_call(
+        copies_kernel,
+        in_specs=[pl.BlockSpec(memory_space=pltpu.VMEM)],
+        out_specs=pl.BlockSpec(memory_space=pltpu.HBM),
+        out_shape=jax.ShapeDtypeStruct((count,) + x.shape, x.dtype),
+        scratch_shapes=[pltpu.SemaphoreType.DMA((count,))],
+        compiler_params=SMALL,
+        name="copies_of",
+    )(x)
 
 
 def grads_kernel(last, *refs):
@@ -132,7 +152,7 @@
         copy.wait()
         if last:
             total = held[j] + got[j]
-            keep_ref[j] = total[:, :half]
+            keep_ref[j] = total[:, :half].astype(BF)
             send_ref[j] = total[:, half:].astype(BF)
 
 
@@ -153,7 +173,7 @@
         in_specs = [small] + [whole] * 4 + [far]
         out_shape = [
             jax.ShapeDtypeStruct((2, blocks, rows, WIDTH), BF),
-            jax.ShapeDtypeStruct(halves, F32),
+            jax.ShapeDtypeStruct(halves, BF),
             jax.ShapeDtypeStruct(halves, BF),
         ]
         out_specs = [whole] * 3
@@ -208,7 +228,7 @@
     count = len(out_refs)
     for r, out_ref in enumerate(out_refs):
         at = lax.rem(y_ref[0] + r, count)
-        out_ref[...] = (keep_ref[at] + got_ref[at].astype(F32)).astype(out_ref.dtype)
+        out_ref[...] = (keep_ref[at].astype(F32) + got_ref[at].astype(F32)).astype(out_ref.dtype)
 
 
 def both_cores(y, keep, got):
@@ -257,7 +277,7 @@
     own = lax.all_gather(kv, "y")
     far, own = lax.optimization_barrier((far, own))
     other = lax.ppermute(own, "core", SWAP)
-    x_far = lax.all_to_all(jnp.broadcast_to(far, copies.shape), "zi", 0, 0)
+    x_far = lax.all_to_all(copies_of(far, copies.shape[0]), "zi", 0, 0)
 
     before = grads(x_near, own, other)
     dq, keep, send = grads(x_far, own, other, index("zq"), before)

time: 84 us -> 83.1 us (0.989)
  local copies, waits for them, and re-layouts: 1.66 us -> 0 us
  Pallas kernels: 15.2 us -> 16.1 us
  transfers between devices with their start and end apart: 9 -> 9, of which waited for: 5 -> 5; matrix products, arithmetic and copies ran while one was open for 0% -> 0% of each run, Pallas kernels for 8% -> 9%
where the time goes in v10:
time: 83.1 us; the launch traced here: 82.6 us
  starting transfers between devices  40.5 us (49%)
  Pallas kernels  16.1 us (19%)
  blocking collectives  13.8 us (17%)
  waiting for transfers between devices  11.5 us (14%)
    all_gather x1, blocking collectives, per_device(): own = lax.all_gather(kv, 'y')  13.8 us
    pallas_call x2, Pallas kernels, grads(): pl.pallas_call(lambda *refs: grads_kernel(last, *refs), in_specs=in_specs...  11.4 us
    ppermute x3, starting transfers between devices, along(): lax.ppermute(value, axis, [(i, (i + steps) % count) for i in range(count)])  10.9 us
    ppermute x1, starting transfers between devices, per_device(): far = lax.ppermute(x, 'zq', SWAP)  9.08 us
    all_to_all x1, starting transfers between devices, per_device(): x_near = lax.all_to_all(copies, 'zi', 0, 0)  5.89 us
    all_to_all x1, starting transfers between devices, per_device(): x_far = lax.all_to_all(copies_of(far, copies.shape[0]), 'zi', 0, 0)  5.38 us
    all_to_all x1, starting transfers between devices, per_device(): query_grad = query_total(core, lax.all_to_all(dq, ('zq', 'zi'), 0, 0))  5.35 us
    ppermute x3, waiting for transfers between devices, along(): lax.ppermute(value, axis, [(i, (i + steps) % count) for i in range(count)])  5.24 us
  transfers between devices with their start and end apart: 9, of which 5 were waited for; matrix products, arithmetic and copies ran while one was open for 0% of the time, Pallas kernels for 9%

profile of v10, /device:TPU:6, one launch (start us, length us, event | category | flops | bytes accessed | tf_op | source)
XLA Modules:
  0.0 82.6 jit_solution(5914385501378379844)
XLA Ops:
  0.6 2.3 %prep.1 = (bf16[400,128]{1,0:T(8,128)(2,1)}, bf16[4,400,128]{2,1,0:T(8,128)(2,1)}, bf16[2,64,640]{2,1,0:T(8,128)(2,1)}) custom-call(s32[1]{0:T(128)} %bitcast.core_ref, bf16[48,512]{1,0:T(8,128)(2,1)} %q_ref.1, bf16[48,512]{1,0:T(8,128)(2,1)} %g_ref.1, bf16[48,512]{1,0:T(8,128)(2,1)} %o_ref.1, f32[4,48]{1,0:T(4,128)} %bitcast.9, bf16[64,640]{1,0:T(8,128)(2,1)} %k_ref.1, ...), custom_call_target="tpu_custom_call" | custom-call | tf_op jit(solution)/shard_map/prep/pallas_call | solution.py:57
  2.9 5.9 %all-to-all-start.1 = ((bf16[4,400,128]{2,1,0:T(8,128)(2,1)}), bf16[4,400,128]{2,1,0:T(8,128)(2,1)S(1)}, u32[]{:S(2)}, u32[]{:S(2)}) async-start(bf16[4,400,128]{2,1,0:T(8,128)(2,1)} %get-tuple-element.23), calls=%async_computation.1 | async-start | bytes 819200 | tf_op jit(solution)/shard_map/all_to_all | solution.py:275
  8.8 9.1 %collective-permute-start = (bf16[400,128]{1,0:T(8,128)(2,1)}, bf16[400,128]{1,0:T(8,128)(2,1)S(1)}, u32[]{:S(2)}, u32[]{:S(2)}) collective-permute-start(bf16[400,128]{1,0:T(8,128)(2,1)} %get-tuple-element.19), channel_id=1, source_target_pairs={{0,4},{4,0},{1,5},{5,1},{2,6},{6,2},{3,7},{7,3},{8,12},{12,8},{9,1... | collective-permute-start | bytes 307208 | tf_op jit(solution)/shard_map/ppermute | solution.py:274
  17.9 13.8 %all-gather = bf16[8,64,640]{2,1,0:T(8,128)(2,1)S(1)} all-gather(bf16[2,64,640]{2,1,0:T(8,128)(2,1)} %get-tuple-element.20), channel_id=2, replica_groups=mesh['zh'=2,'x'=4,'core'=2,'y'=4,'zq'=2,'zi'=4] {'y'}, dimensions={0}, use_global_device_ids=true | all-gather | bytes 819200 | tf_op jit(solution)/shard_map/all_gather | solution.py:277
  31.7 0.0 collective-permute-done.x_ref
  31.7 0.8 copies_of.1
  32.5 0.0 all-to-all-done.1.refs_0_
  32.5 5.4 %all-to-all-start = ((bf16[4,400,128]{2,1,0:T(8,128)(2,1)}), bf16[4,400,128]{2,1,0:T(8,128)(2,1)S(1)}, u32[]{:S(2)}, u32[]{:S(2)}) async-start(bf16[4,400,128]{2,1,0:T(8,128)(2,1)} %copies_of.1), calls=%async_computation | async-start | bytes 819200 | tf_op jit(solution)/shard_map/all_to_all | solution.py:280
  37.9 1.9 %collective-permute-start.1 = (bf16[4,2,64,640]{3,2,1,0:T(8,128)(2,1)S(1)}, bf16[4,2,64,640]{3,2,1,0:T(8,128)(2,1)S(1)}, u32[]{:S(2)}, u32[]{:S(2)}) collective-permute-start(bf16[4,2,64,640]{3,2,1,0:T(8,128)(2,1)S(1)} %bitcast.6), channel_id=1, source_target_pairs={{0,32},{32,0},{1,33},{33,1},{2,34},{34,2},{3,35},{35,3},{4,36},{36... | collective-permute-start | bytes 1966088 | tf_op jit(solution)/shard_map/ppermute | solution.py:279
  39.8 2.1 %collective-permute-done.1.refs_2_.refs_3_ = bf16[4,2,64,640]{3,2,1,0:T(8,128)(2,1)S(1)} collective-permute-done((bf16[4,2,64,640]{3,2,1,0:T(8,128)(2,1)S(1)}, bf16[4,2,64,640]{3,2,1,0:T(8,128)(2,1)S(1)}, u32[]{:S(2)}, u32[]{:S(2)}) %collective-permute-start.1) | collective-permute-done | bytes 655392 | tf_op jit(solution)/shard_map/ppermute | solution.py:279
  41.9 5.4 %grads.2 = (bf16[4,48,512]{2,1,0:T(8,128)(2,1)S(1)}, f32[40,2,128,640]{3,2,1,0:T(8,128)}) custom-call(bf16[4,400,128]{2,1,0:T(8,128)(2,1)S(1)} %all-to-all-done.1.refs_0_, bf16[4,2,64,640]{3,2,1,0:T(8,128)(2,1)S(1)} %bitcast.7, bf16[4,2,64,640]{3,2,1,0:T(8,128)(2,1)S(1)} %collective-permute-done.1.refs_2_.refs_3_), custom_call_target="tpu_custom_call" | custom-call | flops 2516582400 | bytes 4194304 | tf_op jit(solution)/shard_map/grads/pallas_call | solution.py:188
  47.4 0.0 all-to-all-done.refs_1_
  47.4 5.9 %grads.3 = (bf16[2,4,48,512]{3,2,1,0:T(8,128)(2,1)}, bf16[4,2,64,640]{3,2,1,0:T(8,128)(2,1)S(1)}, bf16[4,2,64,640]{3,2,1,0:T(8,128)(2,1)S(1)}) custom-call(s32[1]{0:T(128)} %bitcast.1.refs_0_, bf16[4,400,128]{2,1,0:T(8,128)(2,1)S(1)} %all-to-all-done.refs_1_, bf16[4,2,64,640]{3,2,1,0:T(8,128)(2,1)S(1)} %bitcast.8, ...), custom_call_target="tpu_custom_call" | custom-call | flops 2516582400 | bytes 4194304 | tf_op jit(solution)/shard_map/grads/pallas_call | solution.py:188
  53.3 5.4 %all-to-all-start.2 = ((bf16[8,48,512]{2,1,0:T(8,128)(2,1)}), bf16[8,48,512]{2,1,0:T(8,128)(2,1)S(1)}, u32[]{:S(2)}, u32[]{:S(2)}) async-start(bf16[8,48,512]{2,1,0:T(8,128)(2,1)} %bitcast.4), calls=%async_computation.2 | async-start | bytes 786432 | tf_op jit(solution)/shard_map/all_to_all | solution.py:285
  58.7 1.9 %collective-permute-start.2 = (bf16[4,2,64,640]{3,2,1,0:T(8,128)(2,1)S(1)}, bf16[4,2,64,640]{3,2,1,0:T(8,128)(2,1)S(1)}, u32[]{:S(2)}, u32[]{:S(2)}) collective-permute-start(bf16[4,2,64,640]{3,2,1,0:T(8,128)(2,1)S(1)} %get-tuple-element.28), channel_id=1, source_target_pairs={{0,32},{32,0},{1,33},{33,1},{2,34},{34,2},{3,35},{35,3},{4,36},{36... | collective-permute-start | bytes 1966088 | tf_op jit(solution)/shard_map/ppermute | solution.py:287
  60.6 2.1 %collective-permute-done.2.got_ref = bf16[4,2,64,640]{3,2,1,0:T(8,128)(2,1)S(1)} collective-permute-done((bf16[4,2,64,640]{3,2,1,0:T(8,128)(2,1)S(1)}, bf16[4,2,64,640]{3,2,1,0:T(8,128)(2,1)S(1)}, u32[]{:S(2)}, u32[]{:S(2)}) %collective-permute-start.2) | collective-permute-done | bytes 655392 | tf_op jit(solution)/shard_map/ppermute | solution.py:287
  62.7 0.2 both_cores.1
  62.8 3.5 %collective-permute-start.3 = (bf16[2,64,640]{2,1,0:T(8,128)(2,1)S(1)}, bf16[2,64,640]{2,1,0:T(8,128)(2,1)S(1)}, u32[]{:S(2)}, u32[]{:S(2)}) collective-permute-start(bf16[2,64,640]{2,1,0:T(8,128)(2,1)S(1)} %get-tuple-element.30), channel_id=1, source_target_pairs={{0,8},{8,16},{16,24},{24,0},{1,9},{9,17},{17,25},{25,1},{2,10},{10... | collective-permute-start | bytes 491528 | tf_op jit(solution)/shard_map/ppermute | solution.py:263
  66.3 3.6 %collective-permute-start.4 = (bf16[2,64,640]{2,1,0:T(8,128)(2,1)S(1)}, bf16[2,64,640]{2,1,0:T(8,128)(2,1)S(1)}, u32[]{:S(2)}, u32[]{:S(2)}) collective-permute-start(bf16[2,64,640]{2,1,0:T(8,128)(2,1)S(1)} %get-tuple-element.31), channel_id=1, source_target_pairs={{0,24},{8,0},{16,8},{24,16},{1,25},{9,1},{17,9},{25,17},{2,26},{10... | collective-permute-start | bytes 491528 | tf_op jit(solution)/shard_map/ppermute | solution.py:263
  69.9 3.9 %collective-permute-start.5 = (bf16[2,64,640]{2,1,0:T(8,128)(2,1)S(1)}, bf16[2,64,640]{2,1,0:T(8,128)(2,1)S(1)}, u32[]{:S(2)}, u32[]{:S(2)}) collective-permute-start(bf16[2,64,640]{2,1,0:T(8,128)(2,1)S(1)} %get-tuple-element.32), channel_id=1, source_target_pairs={{0,16},{8,24},{16,0},{24,8},{1,17},{9,25},{17,1},{25,9},{2,18},{10... | collective-permute-start | bytes 491528 | tf_op jit(solution)/shard_map/ppermute | solution.py:263
  73.8 0.0 collective-permute-done.3.refs_1_
  73.8 0.4 collective-permute-done.4.refs_2_
  74.2 4.9 %collective-permute-done.5.refs_3_ = bf16[2,64,640]{2,1,0:T(8,128)(2,1)S(1)} collective-permute-done((bf16[2,64,640]{2,1,0:T(8,128)(2,1)S(1)}, bf16[2,64,640]{2,1,0:T(8,128)(2,1)S(1)}, u32[]{:S(2)}, u32[]{:S(2)}) %collective-permute-start.5) | collective-permute-done | bytes 163872 | tf_op jit(solution)/shard_map/ppermute | solution.py:263
  79.0 0.7 visual_total.1
  79.7 2.1 %all-to-all-done.2.parts_ref = bf16[8,48,512]{2,1,0:T(8,128)(2,1)S(1)} async-done(((bf16[8,48,512]{2,1,0:T(8,128)(2,1)}), bf16[8,48,512]{2,1,0:T(8,128)(2,1)S(1)}, u32[]{:S(2)}, u32[]{:S(2)}) %all-to-all-start.2) | async-done | bytes 393248 | tf_op jit(solution)/shard_map/all_to_all | solution.py:285
  81.8 0.7 query_total.1
Async XLA Ops:
  2.9 29.6 %all-to-all-start.1 = ((bf16[4,400,128]{2,1,0:T(8,128)(2,1)}), bf16[4,400,128]{2,1,0:T(8,128)(2,1)S(1)}, u32[]{:S(2)}, u32[]{:S(2)}) async-start(bf16[4,400,128]{2,1,0:T(8,128)(2,1)} %get-tuple-element.23), calls=%async_computation.1 | async-start | bytes 819200 | tf_op jit(solution)/shard_map/all_to_all | solution.py:275
  8.8 22.9 %collective-permute-start = (bf16[400,128]{1,0:T(8,128)(2,1)}, bf16[400,128]{1,0:T(8,128)(2,1)S(1)}, u32[]{:S(2)}, u32[]{:S(2)}) collective-permute-start(bf16[400,128]{1,0:T(8,128)(2,1)} %get-tuple-element.19), channel_id=1, source_target_pairs={{0,4},{4,0},{1,5},{5,1},{2,6},{6,2},{3,7},{7,3},{8,12},{12,8},{9,1... | collective-permute-start | bytes 307208 | tf_op jit(solution)/shard_map/ppermute | solution.py:274
  32.5 14.8 %all-to-all-start = ((bf16[4,400,128]{2,1,0:T(8,128)(2,1)}), bf16[4,400,128]{2,1,0:T(8,128)(2,1)S(1)}, u32[]{:S(2)}, u32[]{:S(2)}) async-start(bf16[4,400,128]{2,1,0:T(8,128)(2,1)} %copies_of.1), calls=%async_computation | async-start | bytes 819200 | tf_op jit(solution)/shard_map/all_to_all | solution.py:280
  37.9 4.0 %collective-permute-start.1 = (bf16[4,2,64,640]{3,2,1,0:T(8,128)(2,1)S(1)}, bf16[4,2,64,640]{3,2,1,0:T(8,128)(2,1)S(1)}, u32[]{:S(2)}, u32[]{:S(2)}) collective-permute-start(bf16[4,2,64,640]{3,2,1,0:T(8,128)(2,1)S(1)} %bitcast.6), channel_id=1, source_target_pairs={{0,32},{32,0},{1,33},{33,1},{2,34},{34,2},{3,35},{35,3},{4,36},{36... | collective-permute-start | bytes 1966088 | tf_op jit(solution)/shard_map/ppermute | solution.py:279
  53.3 28.5 %all-to-all-start.2 = ((bf16[8,48,512]{2,1,0:T(8,128)(2,1)}), bf16[8,48,512]{2,1,0:T(8,128)(2,1)S(1)}, u32[]{:S(2)}, u32[]{:S(2)}) async-start(bf16[8,48,512]{2,1,0:T(8,128)(2,1)} %bitcast.4), calls=%async_computation.2 | async-start | bytes 786432 | tf_op jit(solution)/shard_map/all_to_all | solution.py:285
  58.7 4.0 %collective-permute-start.2 = (bf16[4,2,64,640]{3,2,1,0:T(8,128)(2,1)S(1)}, bf16[4,2,64,640]{3,2,1,0:T(8,128)(2,1)S(1)}, u32[]{:S(2)}, u32[]{:S(2)}) collective-permute-start(bf16[4,2,64,640]{3,2,1,0:T(8,128)(2,1)S(1)} %get-tuple-element.28), channel_id=1, source_target_pairs={{0,32},{32,0},{1,33},{33,1},{2,34},{34,2},{3,35},{35,3},{4,36},{36... | collective-permute-start | bytes 1966088 | tf_op jit(solution)/shard_map/ppermute | solution.py:287
  62.8 11.0 %collective-permute-start.3 = (bf16[2,64,640]{2,1,0:T(8,128)(2,1)S(1)}, bf16[2,64,640]{2,1,0:T(8,128)(2,1)S(1)}, u32[]{:S(2)}, u32[]{:S(2)}) collective-permute-start(bf16[2,64,640]{2,1,0:T(8,128)(2,1)S(1)} %get-tuple-element.30), channel_id=1, source_target_pairs={{0,8},{8,16},{16,24},{24,0},{1,9},{9,17},{17,25},{25,1},{2,10},{10... | collective-permute-start | bytes 491528 | tf_op jit(solution)/shard_map/ppermute | solution.py:263
  66.3 7.9 %collective-permute-start.4 = (bf16[2,64,640]{2,1,0:T(8,128)(2,1)S(1)}, bf16[2,64,640]{2,1,0:T(8,128)(2,1)S(1)}, u32[]{:S(2)}, u32[]{:S(2)}) collective-permute-start(bf16[2,64,640]{2,1,0:T(8,128)(2,1)S(1)} %get-tuple-element.31), channel_id=1, source_target_pairs={{0,24},{8,0},{16,8},{24,16},{1,25},{9,1},{17,9},{25,17},{2,26},{10... | collective-permute-start | bytes 491528 | tf_op jit(solution)/shard_map/ppermute | solution.py:263
  69.9 9.1 %collective-permute-start.5 = (bf16[2,64,640]{2,1,0:T(8,128)(2,1)S(1)}, bf16[2,64,640]{2,1,0:T(8,128)(2,1)S(1)}, u32[]{:S(2)}, u32[]{:S(2)}) collective-permute-start(bf16[2,64,640]{2,1,0:T(8,128)(2,1)S(1)} %get-tuple-element.32), channel_id=1, source_target_pairs={{0,16},{8,24},{16,0},{24,8},{1,17},{9,25},{17,1},{25,9},{2,18},{10... | collective-permute-start | bytes 491528 | tf_op jit(solution)/shard_map/ppermute | solution.py:263

commit v11 on v10

--- a/solution.py
+++ b/solution.py
@@ -285,7 +285,7 @@
     query_grad = query_total(core, lax.all_to_all(dq, ("zq", "zi"), 0, 0))
 
     both = both_cores(index("y"), keep, lax.ppermute(send, "core", SWAP))
-    parts = [both[0]] + [along("y", both[r], r) for r in (1, 3, 2)]
+    parts = [both[0]] + [along("y", both[r], r) for r in (2, 1, 3)]
     key_grad, value_grad = visual_total(parts)
     return query_grad, key_grad, value_grad
 

time: 83.1 us -> 83.1 us (level)
  starting transfers between devices: 40.5 us -> 41.7 us
  waiting for transfers between devices: 11.5 us -> 10.3 us
    ppermute x3, waiting for transfers between devices: 5.24 us -> 3.17 us  [along(): lax.ppermute(value, axis, [(i, (i + steps) % count) for i in range(count)])]
    ppermute x3, starting transfers between devices: 10.9 us -> 12.2 us  [along(): lax.ppermute(value, axis, [(i, (i + steps) % count) for i in range(count)])]
    all_to_all x1, waiting for transfers between devices: 2.1 us -> 2.96 us  [per_device(): query_grad = query_total(core, lax.all_to_all(dq, ('zq', 'zi'), 0, 0))]
where the time goes in v11:
time: 83.1 us; the launch traced here: 82.6 us
  starting transfers between devices  41.7 us (50%)
  Pallas kernels  16.1 us (19%)
  blocking collectives  13.8 us (17%)
  waiting for transfers between devices  10.3 us (12%)
    all_gather x1, blocking collectives, per_device(): own = lax.all_gather(kv, 'y')  13.8 us
    ppermute x3, starting transfers between devices, along(): lax.ppermute(value, axis, [(i, (i + steps) % count) for i in range(count)])  12.2 us
    pallas_call x2, Pallas kernels, grads(): pl.pallas_call(lambda *refs: grads_kernel(last, *refs), in_specs=in_specs...  11.4 us
    ppermute x1, starting transfers between devices, per_device(): far = lax.ppermute(x, 'zq', SWAP)  9.08 us
    all_to_all x1, starting transfers between devices, per_device(): x_near = lax.all_to_all(copies, 'zi', 0, 0)  5.89 us
    all_to_all x1, starting transfers between devices, per_device(): x_far = lax.all_to_all(copies_of(far, copies.shape[0]), 'zi', 0, 0)  5.38 us
    all_to_all x1, starting transfers between devices, per_device(): query_grad = query_total(core, lax.all_to_all(dq, ('zq', 'zi'), 0, 0))  5.35 us
    ppermute x3, waiting for transfers between devices, along(): lax.ppermute(value, axis, [(i, (i + steps) % count) for i in range(count)])  3.17 us
  transfers between devices with their start and end apart: 9, of which 5 were waited for; matrix products, arithmetic and copies ran while one was open for 0% of the time, Pallas kernels for 9%

profile of v11, /device:TPU:6, one launch (start us, length us, event | category | flops | bytes accessed | tf_op | source)
XLA Modules:
  0.0 82.6 jit_solution(17924955545744974498)
XLA Ops:
  0.6 2.3 %prep.1 = (bf16[400,128]{1,0:T(8,128)(2,1)}, bf16[4,400,128]{2,1,0:T(8,128)(2,1)}, bf16[2,64,640]{2,1,0:T(8,128)(2,1)}) custom-call(s32[1]{0:T(128)} %bitcast.core_ref, bf16[48,512]{1,0:T(8,128)(2,1)} %q_ref.1, bf16[48,512]{1,0:T(8,128)(2,1)} %g_ref.1, bf16[48,512]{1,0:T(8,128)(2,1)} %o_ref.1, f32[4,48]{1,0:T(4,128)} %bitcast.9, bf16[64,640]{1,0:T(8,128)(2,1)} %k_ref.1, ...), custom_call_target="tpu_custom_call" | custom-call | tf_op jit(solution)/shard_map/prep/pallas_call | solution.py:57
  2.9 5.9 %all-to-all-start.1 = ((bf16[4,400,128]{2,1,0:T(8,128)(2,1)}), bf16[4,400,128]{2,1,0:T(8,128)(2,1)S(1)}, u32[]{:S(2)}, u32[]{:S(2)}) async-start(bf16[4,400,128]{2,1,0:T(8,128)(2,1)} %get-tuple-element.23), calls=%async_computation.1 | async-start | bytes 819200 | tf_op jit(solution)/shard_map/all_to_all | solution.py:275
  8.8 9.1 %collective-permute-start = (bf16[400,128]{1,0:T(8,128)(2,1)}, bf16[400,128]{1,0:T(8,128)(2,1)S(1)}, u32[]{:S(2)}, u32[]{:S(2)}) collective-permute-start(bf16[400,128]{1,0:T(8,128)(2,1)} %get-tuple-element.19), channel_id=1, source_target_pairs={{0,4},{4,0},{1,5},{5,1},{2,6},{6,2},{3,7},{7,3},{8,12},{12,8},{9,1... | collective-permute-start | bytes 307208 | tf_op jit(solution)/shard_map/ppermute | solution.py:274
  17.9 13.8 %all-gather = bf16[8,64,640]{2,1,0:T(8,128)(2,1)S(1)} all-gather(bf16[2,64,640]{2,1,0:T(8,128)(2,1)} %get-tuple-element.20), channel_id=2, replica_groups=mesh['zh'=2,'x'=4,'core'=2,'y'=4,'zq'=2,'zi'=4] {'y'}, dimensions={0}, use_global_device_ids=true | all-gather | bytes 819200 | tf_op jit(solution)/shard_map/all_gather | solution.py:277
  31.7 0.0 collective-permute-done.x_ref
  31.7 0.8 copies_of.1
  32.5 0.0 all-to-all-done.1.refs_0_
  32.5 5.4 %all-to-all-start = ((bf16[4,400,128]{2,1,0:T(8,128)(2,1)}), bf16[4,400,128]{2,1,0:T(8,128)(2,1)S(1)}, u32[]{:S(2)}, u32[]{:S(2)}) async-start(bf16[4,400,128]{2,1,0:T(8,128)(2,1)} %copies_of.1), calls=%async_computation | async-start | bytes 819200 | tf_op jit(solution)/shard_map/all_to_all | solution.py:280
  37.9 1.9 %collective-permute-start.1 = (bf16[4,2,64,640]{3,2,1,0:T(8,128)(2,1)S(1)}, bf16[4,2,64,640]{3,2,1,0:T(8,128)(2,1)S(1)}, u32[]{:S(2)}, u32[]{:S(2)}) collective-permute-start(bf16[4,2,64,640]{3,2,1,0:T(8,128)(2,1)S(1)} %bitcast.6), channel_id=1, source_target_pairs={{0,32},{32,0},{1,33},{33,1},{2,34},{34,2},{3,35},{35,3},{4,36},{36... | collective-permute-start | bytes 1966088 | tf_op jit(solution)/shard_map/ppermute | solution.py:279
  39.8 2.1 %collective-permute-done.1.refs_2_.refs_3_ = bf16[4,2,64,640]{3,2,1,0:T(8,128)(2,1)S(1)} collective-permute-done((bf16[4,2,64,640]{3,2,1,0:T(8,128)(2,1)S(1)}, bf16[4,2,64,640]{3,2,1,0:T(8,128)(2,1)S(1)}, u32[]{:S(2)}, u32[]{:S(2)}) %collective-permute-start.1) | collective-permute-done | bytes 655392 | tf_op jit(solution)/shard_map/ppermute | solution.py:279
  41.9 5.4 %grads.2 = (bf16[4,48,512]{2,1,0:T(8,128)(2,1)S(1)}, f32[40,2,128,640]{3,2,1,0:T(8,128)}) custom-call(bf16[4,400,128]{2,1,0:T(8,128)(2,1)S(1)} %all-to-all-done.1.refs_0_, bf16[4,2,64,640]{3,2,1,0:T(8,128)(2,1)S(1)} %bitcast.7, bf16[4,2,64,640]{3,2,1,0:T(8,128)(2,1)S(1)} %collective-permute-done.1.refs_2_.refs_3_), custom_call_target="tpu_custom_call" | custom-call | flops 2516582400 | bytes 4194304 | tf_op jit(solution)/shard_map/grads/pallas_call | solution.py:188
  47.4 0.0 all-to-all-done.refs_1_
  47.4 5.9 %grads.3 = (bf16[2,4,48,512]{3,2,1,0:T(8,128)(2,1)}, bf16[4,2,64,640]{3,2,1,0:T(8,128)(2,1)S(1)}, bf16[4,2,64,640]{3,2,1,0:T(8,128)(2,1)S(1)}) custom-call(s32[1]{0:T(128)} %bitcast.1.refs_0_, bf16[4,400,128]{2,1,0:T(8,128)(2,1)S(1)} %all-to-all-done.refs_1_, bf16[4,2,64,640]{3,2,1,0:T(8,128)(2,1)S(1)} %bitcast.8, ...), custom_call_target="tpu_custom_call" | custom-call | flops 2516582400 | bytes 4194304 | tf_op jit(solution)/shard_map/grads/pallas_call | solution.py:188
  53.3 5.4 %all-to-all-start.2 = ((bf16[8,48,512]{2,1,0:T(8,128)(2,1)}), bf16[8,48,512]{2,1,0:T(8,128)(2,1)S(1)}, u32[]{:S(2)}, u32[]{:S(2)}) async-start(bf16[8,48,512]{2,1,0:T(8,128)(2,1)} %bitcast.4), calls=%async_computation.2 | async-start | bytes 786432 | tf_op jit(solution)/shard_map/all_to_all | solution.py:285
  58.7 1.9 %collective-permute-start.2 = (bf16[4,2,64,640]{3,2,1,0:T(8,128)(2,1)S(1)}, bf16[4,2,64,640]{3,2,1,0:T(8,128)(2,1)S(1)}, u32[]{:S(2)}, u32[]{:S(2)}) collective-permute-start(bf16[4,2,64,640]{3,2,1,0:T(8,128)(2,1)S(1)} %get-tuple-element.28), channel_id=1, source_target_pairs={{0,32},{32,0},{1,33},{33,1},{2,34},{34,2},{3,35},{35,3},{4,36},{36... | collective-permute-start | bytes 1966088 | tf_op jit(solution)/shard_map/ppermute | solution.py:287
  60.6 2.1 %collective-permute-done.2.got_ref = bf16[4,2,64,640]{3,2,1,0:T(8,128)(2,1)S(1)} collective-permute-done((bf16[4,2,64,640]{3,2,1,0:T(8,128)(2,1)S(1)}, bf16[4,2,64,640]{3,2,1,0:T(8,128)(2,1)S(1)}, u32[]{:S(2)}, u32[]{:S(2)}) %collective-permute-start.2) | collective-permute-done | bytes 655392 | tf_op jit(solution)/shard_map/ppermute | solution.py:287
  62.7 0.2 both_cores.1
  62.8 5.1 %collective-permute-start.3 = (bf16[2,64,640]{2,1,0:T(8,128)(2,1)S(1)}, bf16[2,64,640]{2,1,0:T(8,128)(2,1)S(1)}, u32[]{:S(2)}, u32[]{:S(2)}) collective-permute-start(bf16[2,64,640]{2,1,0:T(8,128)(2,1)S(1)} %get-tuple-element.30), channel_id=1, source_target_pairs={{0,16},{8,24},{16,0},{24,8},{1,17},{9,25},{17,1},{25,9},{2,18},{10... | collective-permute-start | bytes 491528 | tf_op jit(solution)/shard_map/ppermute | solution.py:263
  67.9 2.6 %collective-permute-start.4 = (bf16[2,64,640]{2,1,0:T(8,128)(2,1)S(1)}, bf16[2,64,640]{2,1,0:T(8,128)(2,1)S(1)}, u32[]{:S(2)}, u32[]{:S(2)}) collective-permute-start(bf16[2,64,640]{2,1,0:T(8,128)(2,1)S(1)} %get-tuple-element.31), channel_id=1, source_target_pairs={{0,8},{8,16},{16,24},{24,0},{1,9},{9,17},{17,25},{25,1},{2,10},{10... | collective-permute-start | bytes 491528 | tf_op jit(solution)/shard_map/ppermute | solution.py:263
  70.5 4.5 %collective-permute-start.5 = (bf16[2,64,640]{2,1,0:T(8,128)(2,1)S(1)}, bf16[2,64,640]{2,1,0:T(8,128)(2,1)S(1)}, u32[]{:S(2)}, u32[]{:S(2)}) collective-permute-start(bf16[2,64,640]{2,1,0:T(8,128)(2,1)S(1)} %get-tuple-element.32), channel_id=1, source_target_pairs={{0,24},{8,0},{16,8},{24,16},{1,25},{9,1},{17,9},{25,17},{2,26},{10... | collective-permute-start | bytes 491528 | tf_op jit(solution)/shard_map/ppermute | solution.py:263
  75.0 0.0 collective-permute-done.3.refs_1_
  75.0 2.0 %collective-permute-done.4.refs_2_ = bf16[2,64,640]{2,1,0:T(8,128)(2,1)S(1)} collective-permute-done((bf16[2,64,640]{2,1,0:T(8,128)(2,1)S(1)}, bf16[2,64,640]{2,1,0:T(8,128)(2,1)S(1)}, u32[]{:S(2)}, u32[]{:S(2)}) %collective-permute-start.4) | collective-permute-done | bytes 163872 | tf_op jit(solution)/shard_map/ppermute | solution.py:263
  77.0 1.2 %collective-permute-done.5.refs_3_ = bf16[2,64,640]{2,1,0:T(8,128)(2,1)S(1)} collective-permute-done((bf16[2,64,640]{2,1,0:T(8,128)(2,1)S(1)}, bf16[2,64,640]{2,1,0:T(8,128)(2,1)S(1)}, u32[]{:S(2)}, u32[]{:S(2)}) %collective-permute-start.5) | collective-permute-done | bytes 163872 | tf_op jit(solution)/shard_map/ppermute | solution.py:263
  78.2 0.7 visual_total.1
  78.9 3.0 %all-to-all-done.2.parts_ref = bf16[8,48,512]{2,1,0:T(8,128)(2,1)S(1)} async-done(((bf16[8,48,512]{2,1,0:T(8,128)(2,1)}), bf16[8,48,512]{2,1,0:T(8,128)(2,1)S(1)}, u32[]{:S(2)}, u32[]{:S(2)}) %all-to-all-start.2) | async-done | bytes 393248 | tf_op jit(solution)/shard_map/all_to_all | solution.py:285
  81.8 0.7 query_total.1
Async XLA Ops:
  2.9 29.6 %all-to-all-start.1 = ((bf16[4,400,128]{2,1,0:T(8,128)(2,1)}), bf16[4,400,128]{2,1,0:T(8,128)(2,1)S(1)}, u32[]{:S(2)}, u32[]{:S(2)}) async-start(bf16[4,400,128]{2,1,0:T(8,128)(2,1)} %get-tuple-element.23), calls=%async_computation.1 | async-start | bytes 819200 | tf_op jit(solution)/shard_map/all_to_all | solution.py:275
  8.8 22.9 %collective-permute-start = (bf16[400,128]{1,0:T(8,128)(2,1)}, bf16[400,128]{1,0:T(8,128)(2,1)S(1)}, u32[]{:S(2)}, u32[]{:S(2)}) collective-permute-start(bf16[400,128]{1,0:T(8,128)(2,1)} %get-tuple-element.19), channel_id=1, source_target_pairs={{0,4},{4,0},{1,5},{5,1},{2,6},{6,2},{3,7},{7,3},{8,12},{12,8},{9,1... | collective-permute-start | bytes 307208 | tf_op jit(solution)/shard_map/ppermute | solution.py:274
  32.5 14.8 %all-to-all-start = ((bf16[4,400,128]{2,1,0:T(8,128)(2,1)}), bf16[4,400,128]{2,1,0:T(8,128)(2,1)S(1)}, u32[]{:S(2)}, u32[]{:S(2)}) async-start(bf16[4,400,128]{2,1,0:T(8,128)(2,1)} %copies_of.1), calls=%async_computation | async-start | bytes 819200 | tf_op jit(solution)/shard_map/all_to_all | solution.py:280
  37.9 4.0 %collective-permute-start.1 = (bf16[4,2,64,640]{3,2,1,0:T(8,128)(2,1)S(1)}, bf16[4,2,64,640]{3,2,1,0:T(8,128)(2,1)S(1)}, u32[]{:S(2)}, u32[]{:S(2)}) collective-permute-start(bf16[4,2,64,640]{3,2,1,0:T(8,128)(2,1)S(1)} %bitcast.6), channel_id=1, source_target_pairs={{0,32},{32,0},{1,33},{33,1},{2,34},{34,2},{3,35},{35,3},{4,36},{36... | collective-permute-start | bytes 1966088 | tf_op jit(solution)/shard_map/ppermute | solution.py:279
  53.3 28.5 %all-to-all-start.2 = ((bf16[8,48,512]{2,1,0:T(8,128)(2,1)}), bf16[8,48,512]{2,1,0:T(8,128)(2,1)S(1)}, u32[]{:S(2)}, u32[]{:S(2)}) async-start(bf16[8,48,512]{2,1,0:T(8,128)(2,1)} %bitcast.4), calls=%async_computation.2 | async-start | bytes 786432 | tf_op jit(solution)/shard_map/all_to_all | solution.py:285
  58.7 4.0 %collective-permute-start.2 = (bf16[4,2,64,640]{3,2,1,0:T(8,128)(2,1)S(1)}, bf16[4,2,64,640]{3,2,1,0:T(8,128)(2,1)S(1)}, u32[]{:S(2)}, u32[]{:S(2)}) collective-permute-start(bf16[4,2,64,640]{3,2,1,0:T(8,128)(2,1)S(1)} %get-tuple-element.28), channel_id=1, source_target_pairs={{0,32},{32,0},{1,33},{33,1},{2,34},{34,2},{3,35},{35,3},{4,36},{36... | collective-permute-start | bytes 1966088 | tf_op jit(solution)/shard_map/ppermute | solution.py:287
  62.8 12.2 %collective-permute-start.3 = (bf16[2,64,640]{2,1,0:T(8,128)(2,1)S(1)}, bf16[2,64,640]{2,1,0:T(8,128)(2,1)S(1)}, u32[]{:S(2)}, u32[]{:S(2)}) collective-permute-start(bf16[2,64,640]{2,1,0:T(8,128)(2,1)S(1)} %get-tuple-element.30), channel_id=1, source_target_pairs={{0,16},{8,24},{16,0},{24,8},{1,17},{9,25},{17,1},{25,9},{2,18},{10... | collective-permute-start | bytes 491528 | tf_op jit(solution)/shard_map/ppermute | solution.py:263
  67.9 9.1 %collective-permute-start.4 = (bf16[2,64,640]{2,1,0:T(8,128)(2,1)S(1)}, bf16[2,64,640]{2,1,0:T(8,128)(2,1)S(1)}, u32[]{:S(2)}, u32[]{:S(2)}) collective-permute-start(bf16[2,64,640]{2,1,0:T(8,128)(2,1)S(1)} %get-tuple-element.31), channel_id=1, source_target_pairs={{0,8},{8,16},{16,24},{24,0},{1,9},{9,17},{17,25},{25,1},{2,10},{10... | collective-permute-start | bytes 491528 | tf_op jit(solution)/shard_map/ppermute | solution.py:263
  70.5 7.7 %collective-permute-start.5 = (bf16[2,64,640]{2,1,0:T(8,128)(2,1)S(1)}, bf16[2,64,640]{2,1,0:T(8,128)(2,1)S(1)}, u32[]{:S(2)}, u32[]{:S(2)}) collective-permute-start(bf16[2,64,640]{2,1,0:T(8,128)(2,1)S(1)} %get-tuple-element.32), channel_id=1, source_target_pairs={{0,24},{8,0},{16,8},{24,16},{1,25},{9,1},{17,9},{25,17},{2,26},{10... | collective-permute-start | bytes 491528 | tf_op jit(solution)/shard_map/ppermute | solution.py:263
